TPU v7x, 128 devices: a whole 4x4x4 slice. The times are simulated.
128 devices in a mesh: sector: 8 (over z, core), table: 16 (over y, x).
Axes of the slice: x: 4, y: 4, z: 4, core: 2. Of those that a mesh axis runs over, the one named last changes fastest.
Arguments:
- wave_blocks: bfloat16 [64, 256, 256], P('sector', 'table'), may hold values from -6 to 6
- recoupling: bfloat16 [256, 256, 256], P('table'), may hold values from -0.375 to 0.375
- right_blocks: bfloat16 [64, 256, 256], P('sector'), may hold values from -0.02734375 to 0.02734375
- sector_sizes: int32 [64], P('sector'), may hold values from 128 to 256
- channel_env: int32 [64, 2], P('sector'), may hold values from 0 to 7
- fetch_list: int32 [8, 8, 3], P('sector'), may hold values from 0 to 7
- term_pick: int32 [24576], P(('sector', 'table')), may hold values from 0 to 23
- term_table: int32 [24576], P(('sector', 'table')), may hold values from 0 to 15
- term_slot: int32 [24576], P(('sector', 'table')), may hold values from 0 to 15
- term_live: int32 [24576], P(('sector', 'table')), may hold values from 0 to 1, as said below
Outputs:
- sigma_blocks: float32 [64, 256, 256], P('sector', 'table')
Inputs may be any that keep to these rules, and one draw needn't show every extreme that they name: `term_live`: in each aligned block of 192 terms (one device's) the live terms come first; some block is all live.
All inputs are finite; a program needn't handle non-finite values.
Results may differ from a plain program's by a relative error of at most 0.0003.
Values may be sent and summed in bfloat16 or wider, within the bound.
No kernel may reach another device: no remote copies, remote signals or barrier semaphores. Data moves between devices by JAX's collectives and lax.ppermute only.
A program may use at most 128 MiB of HBM per device.

v0:
```python
import jax
import jax.numpy as jnp
from jax import lax
from jax.sharding import PartitionSpec as P


def local(
    wave_blocks,
    recoupling,
    right_blocks,
    sector_sizes,
    channel_env,
    fetch_list,
    term_pick,
    term_table,
    term_slot,
    term_live,
):
    sec_local, row_count, width = wave_blocks.shape
    groups = lax.axis_size("sector")
    listed = fetch_list.shape[2]
    channels = channel_env.shape[1]
    slots_local = sec_local * channels
    local_all = lax.all_gather(wave_blocks, "sector", axis=0, tiled=True)
    pool = lax.all_gather(local_all, "table", axis=1, tiled=True)
    flat_list = fetch_list[0].reshape(-1)
    pick_ids = jnp.arange(groups * listed, dtype=jnp.int32)
    chosen = jnp.sum(
        jnp.where(term_pick[:, None] == pick_ids[None, :], flat_list[None, :], 0), axis=1
    )
    sources = term_pick // listed * sec_local + chosen

    def accumulate(number, totals):
        start = number * 32
        src_ids = lax.dynamic_slice_in_dim(sources, start, 32)
        tab_ids = lax.dynamic_slice_in_dim(term_table, start, 32)
        out_ids = lax.dynamic_slice_in_dim(term_slot, start, 32)
        live_ids = lax.dynamic_slice_in_dim(term_live, start, 32)
        product = jnp.einsum(
            "tij,tjk->tik", recoupling[tab_ids], pool[src_ids], preferred_element_type=jnp.float32
        )
        weighted = product * live_ids.astype(jnp.float32)[:, None, None]
        return totals.at[out_ids].add(weighted)

    channel = lax.fori_loop(
        0, term_pick.shape[0] // 32, accumulate, jnp.zeros((slots_local, width, width), jnp.float32)
    )
    env_blocks = right_blocks[channel_env].astype(jnp.float32)
    joined = jnp.einsum(
        "opij,opjk->oik",
        channel.reshape(sec_local, channels, width, width),
        env_blocks,
        precision=lax.Precision.HIGHEST,
    )
    result = lax.psum_scatter(joined, "table", scatter_dimension=1, tiled=True)
    row_ids = lax.axis_index("table") * row_count + jnp.arange(row_count, dtype=jnp.int32)
    column_ids = jnp.arange(width, dtype=jnp.int32)
    limits = sector_sizes[:, None, None]
    keep = (row_ids[None, :, None] < limits) & (column_ids[None, None, :] < limits)
    return jnp.where(keep, result, jnp.float32(0.0))


def solution(mesh):
    placed = (
        P("sector", "table", None),
        P("table", None, None),
        P("sector", None, None),
        P("sector"),
        P("sector", None),
        P("sector", None, None),
        P(("sector", "table")),
        P(("sector", "table")),
        P(("sector", "table")),
        P(("sector", "table")),
    )
    return jax.shard_map(
        local, mesh=mesh, in_specs=placed, out_specs=P("sector", "table", None), check_vma=False
    )
```

profile of v0, /device:TPU:0, one launch (start us, length us, event | category | flops | bytes accessed | tf_op | source)
XLA Modules:
  0.0 405.9 jit_solution(15083389853588667448)
XLA Ops:
  6.5 15.8 %all_gather.6 = bf16[64,16,256]{2,1,0:T(8,128)(2,1)} all-gather(bf16[8,16,256]{2,1,0:T(8,128)(2,1)} %param.12), channel_id=1, replica_groups=mesh['sector'=8,'table'=16] {'sector'}, dimensions={0}, use_global_device_ids=true | all-gather | bytes 589824 | tf_op jit(solution)/shard_map/all_gather | solution.py:24
  22.4 0.8 copy.17
  23.2 0.1 broadcast_in_dim.54
  23.3 0.7 compare_select_fusion.3
  23.9 0.1 copy.18
  24.0 0.1 reshape.82
  24.2 2.0 gather_fusion.2
  26.2 0.1 select_reduce_fusion
  26.3 75.7 %all-gather.2.cloned.1.call-done = bf16[64,256,256]{2,1,0:T(8,128)(2,1)} async-done(((bf16[64,16,256]{2,1,0:T(8,128)(2,1)}), bf16[64,256,256]{2,1,0:T(8,128)(2,1)}) %all-gather.2.cloned.1.call-update) | async-done | bytes 8388624 | tf_op jit(solution)/shard_map/all_gather | solution.py:25
  101.9 2.4 broadcast_in_dim.53
  104.4 212.2 %while.13 = (s32[]{:T(128)}, f32[16,256,256]{2,1,0:T(8,128)}, s32[192]{0:T(256)S(1)}, s32[192]{0:T(256)S(1)}, bf16[16,256,256]{2,1,0:T(8,128)(2,1)S(1)}, /*index...) while((s32[]{:T(128)}, f32[16,256,256]{2,1,0:T(8,128)}, ...), condition=%wide.region_3.4_spmd, body=%wide.region_1.3_spmd.sunk | while | flops 1077938560 | bytes 58730416 | solution.py:45
  104.4 0.1 compare_select_fusion.6
  104.5 0.1 compare_select_fusion.7
  104.5 2.8 gather_fusion
  107.3 6.2 %gather_fusion.1 = bf16[32,256,256]{2,1,0:T(8,128)(2,1)} fusion(bf16[64,256,256]{2,1,0:T(8,128)(2,1)} %get-tuple-element.252, s32[1024]{0:T(1024)S(1)} %pad_clamp_fusion.6), kind=kCustom, calls=%fused_computation.1.clone.1 | custom fusion | bytes 8388736 | tf_op jit(solution)/shard_map/while/body/eval_jaxpr/gather | solution.py:40
  113.5 7.9 %broadcast_multiply_fusion.2 = f32[32,256,256]{2,1,0:T(8,128)} fusion(f32[32]{0:T(128)S(1)} %get-tuple-element.219, bf16[32,256,256]{2,1,0:T(8,128)(2,1)} %gather_fusion, bf16[32,256,256]{2,1,0:T(8,128)(2,1)} %gather_fusion.1), kind=kOutput, calls=%fused_computation.4.clone.1 | convolution fusion | flops 1075838976 | bytes 16777344 | tf_op jit(solution)/shard_map/while/body/eval_jaxpr/tij,tjk->tik/dot_general | solution.py:39
  121.4 18.6 %scatter_fusion = f32[16,256,256]{2,1,0:T(8,128)} fusion(f32[16,256,256]{2,1,0:T(8,128)} %get-tuple-element.235, s32[32]{0:T(128)S(1)} %get-tuple-element.218, f32[32,256,256]{2,1,0:T(8,128)} %broadcast_multiply_fusion.2), kind=kCustom, calls=%fused_computation.3.clone.1 | custom fusion | flops 2097152 | bytes 25165952 | tf_op jit(solution)/shard_map/while/body/eval_jaxpr/scatter-add | solution.py:43
  140.0 0.1 compare_select_fusion.6
  140.1 0.1 compare_select_fusion.7
  140.2 2.8 gather_fusion
  143.0 6.2 %gather_fusion.1 = bf16[32,256,256]{2,1,0:T(8,128)(2,1)} fusion(bf16[64,256,256]{2,1,0:T(8,128)(2,1)} %get-tuple-element.252, s32[1024]{0:T(1024)S(1)} %pad_clamp_fusion.6), kind=kCustom, calls=%fused_computation.1.clone.1 | custom fusion | bytes 8388736 | tf_op jit(solution)/shard_map/while/body/eval_jaxpr/gather | solution.py:40
  149.1 7.9 %broadcast_multiply_fusion.2 = f32[32,256,256]{2,1,0:T(8,128)} fusion(f32[32]{0:T(128)S(1)} %get-tuple-element.219, bf16[32,256,256]{2,1,0:T(8,128)(2,1)} %gather_fusion, bf16[32,256,256]{2,1,0:T(8,128)(2,1)} %gather_fusion.1), kind=kOutput, calls=%fused_computation.4.clone.1 | convolution fusion | flops 1075838976 | bytes 16777344 | tf_op jit(solution)/shard_map/while/body/eval_jaxpr/tij,tjk->tik/dot_general | solution.py:39
  157.1 18.3 %scatter_fusion = f32[16,256,256]{2,1,0:T(8,128)} fusion(f32[16,256,256]{2,1,0:T(8,128)} %get-tuple-element.235, s32[32]{0:T(128)S(1)} %get-tuple-element.218, f32[32,256,256]{2,1,0:T(8,128)} %broadcast_multiply_fusion.2), kind=kCustom, calls=%fused_computation.3.clone.1 | custom fusion | flops 2097152 | bytes 25165952 | tf_op jit(solution)/shard_map/while/body/eval_jaxpr/scatter-add | solution.py:43
  175.4 0.1 compare_select_fusion.6
  175.4 0.1 compare_select_fusion.7
  175.5 2.8 gather_fusion
  178.3 6.2 %gather_fusion.1 = bf16[32,256,256]{2,1,0:T(8,128)(2,1)} fusion(bf16[64,256,256]{2,1,0:T(8,128)(2,1)} %get-tuple-element.252, s32[1024]{0:T(1024)S(1)} %pad_clamp_fusion.6), kind=kCustom, calls=%fused_computation.1.clone.1 | custom fusion | bytes 8388736 | tf_op jit(solution)/shard_map/while/body/eval_jaxpr/gather | solution.py:40
  184.5 7.9 %broadcast_multiply_fusion.2 = f32[32,256,256]{2,1,0:T(8,128)} fusion(f32[32]{0:T(128)S(1)} %get-tuple-element.219, bf16[32,256,256]{2,1,0:T(8,128)(2,1)} %gather_fusion, bf16[32,256,256]{2,1,0:T(8,128)(2,1)} %gather_fusion.1), kind=kOutput, calls=%fused_computation.4.clone.1 | convolution fusion | flops 1075838976 | bytes 16777344 | tf_op jit(solution)/shard_map/while/body/eval_jaxpr/tij,tjk->tik/dot_general | solution.py:39
  192.4 18.1 %scatter_fusion = f32[16,256,256]{2,1,0:T(8,128)} fusion(f32[16,256,256]{2,1,0:T(8,128)} %get-tuple-element.235, s32[32]{0:T(128)S(1)} %get-tuple-element.218, f32[32,256,256]{2,1,0:T(8,128)} %broadcast_multiply_fusion.2), kind=kCustom, calls=%fused_computation.3.clone.1 | custom fusion | flops 2097152 | bytes 25165952 | tf_op jit(solution)/shard_map/while/body/eval_jaxpr/scatter-add | solution.py:43
  210.5 0.1 compare_select_fusion.6
  210.6 0.1 compare_select_fusion.7
  210.7 2.8 gather_fusion
  213.4 6.2 %gather_fusion.1 = bf16[32,256,256]{2,1,0:T(8,128)(2,1)} fusion(bf16[64,256,256]{2,1,0:T(8,128)(2,1)} %get-tuple-element.252, s32[1024]{0:T(1024)S(1)} %pad_clamp_fusion.6), kind=kCustom, calls=%fused_computation.1.clone.1 | custom fusion | bytes 8388736 | tf_op jit(solution)/shard_map/while/body/eval_jaxpr/gather | solution.py:40
  219.6 7.9 %broadcast_multiply_fusion.2 = f32[32,256,256]{2,1,0:T(8,128)} fusion(f32[32]{0:T(128)S(1)} %get-tuple-element.219, bf16[32,256,256]{2,1,0:T(8,128)(2,1)} %gather_fusion, bf16[32,256,256]{2,1,0:T(8,128)(2,1)} %gather_fusion.1), kind=kOutput, calls=%fused_computation.4.clone.1 | convolution fusion | flops 1075838976 | bytes 16777344 | tf_op jit(solution)/shard_map/while/body/eval_jaxpr/tij,tjk->tik/dot_general | solution.py:39
  227.6 18.1 %scatter_fusion = f32[16,256,256]{2,1,0:T(8,128)} fusion(f32[16,256,256]{2,1,0:T(8,128)} %get-tuple-element.235, s32[32]{0:T(128)S(1)} %get-tuple-element.218, f32[32,256,256]{2,1,0:T(8,128)} %broadcast_multiply_fusion.2), kind=kCustom, calls=%fused_computation.3.clone.1 | custom fusion | flops 2097152 | bytes 25165952 | tf_op jit(solution)/shard_map/while/body/eval_jaxpr/scatter-add | solution.py:43
  245.7 0.1 compare_select_fusion.7
  245.8 2.8 gather_fusion
  248.6 6.2 %gather_fusion.1 = bf16[32,256,256]{2,1,0:T(8,128)(2,1)} fusion(bf16[64,256,256]{2,1,0:T(8,128)(2,1)} %get-tuple-element.252, s32[1024]{0:T(1024)S(1)} %pad_clamp_fusion.6), kind=kCustom, calls=%fused_computation.1.clone.1 | custom fusion | bytes 8388736 | tf_op jit(solution)/shard_map/while/body/eval_jaxpr/gather | solution.py:40
  254.8 7.9 %broadcast_multiply_fusion.2 = f32[32,256,256]{2,1,0:T(8,128)} fusion(f32[32]{0:T(128)S(1)} %get-tuple-element.219, bf16[32,256,256]{2,1,0:T(8,128)(2,1)} %gather_fusion, bf16[32,256,256]{2,1,0:T(8,128)(2,1)} %gather_fusion.1), kind=kOutput, calls=%fused_computation.4.clone.1 | convolution fusion | flops 1075838976 | bytes 16777344 | tf_op jit(solution)/shard_map/while/body/eval_jaxpr/tij,tjk->tik/dot_general | solution.py:39
  262.7 18.3 %scatter_fusion = f32[16,256,256]{2,1,0:T(8,128)} fusion(f32[16,256,256]{2,1,0:T(8,128)} %get-tuple-element.235, s32[32]{0:T(128)S(1)} %get-tuple-element.218, f32[32,256,256]{2,1,0:T(8,128)} %broadcast_multiply_fusion.2), kind=kCustom, calls=%fused_computation.3.clone.1 | custom fusion | flops 2097152 | bytes 25165952 | tf_op jit(solution)/shard_map/while/body/eval_jaxpr/scatter-add | solution.py:43
  281.1 0.1 compare_select_fusion.7
  281.2 2.8 gather_fusion
  284.0 6.2 %gather_fusion.1 = bf16[32,256,256]{2,1,0:T(8,128)(2,1)} fusion(bf16[64,256,256]{2,1,0:T(8,128)(2,1)} %get-tuple-element.252, s32[1024]{0:T(1024)S(1)} %pad_clamp_fusion.6), kind=kCustom, calls=%fused_computation.1.clone.1 | custom fusion | bytes 8388736 | tf_op jit(solution)/shard_map/while/body/eval_jaxpr/gather | solution.py:40
  290.2 7.9 %broadcast_multiply_fusion.2 = f32[32,256,256]{2,1,0:T(8,128)} fusion(f32[32]{0:T(128)S(1)} %get-tuple-element.219, bf16[32,256,256]{2,1,0:T(8,128)(2,1)} %gather_fusion, bf16[32,256,256]{2,1,0:T(8,128)(2,1)} %gather_fusion.1), kind=kOutput, calls=%fused_computation.4.clone.1 | convolution fusion | flops 1075838976 | bytes 16777344 | tf_op jit(solution)/shard_map/while/body/eval_jaxpr/tij,tjk->tik/dot_general | solution.py:39
  298.1 18.4 %scatter_fusion = f32[16,256,256]{2,1,0:T(8,128)} fusion(f32[16,256,256]{2,1,0:T(8,128)} %get-tuple-element.235, s32[32]{0:T(128)S(1)} %get-tuple-element.218, f32[32,256,256]{2,1,0:T(8,128)} %broadcast_multiply_fusion.2), kind=kCustom, calls=%fused_computation.3.clone.1 | custom fusion | flops 2097152 | bytes 25165952 | tf_op jit(solution)/shard_map/while/body/eval_jaxpr/scatter-add | solution.py:43
  316.6 6.2 %convolution_bitcast_fusion = f32[8,256,256]{2,1,0:T(8,128)} fusion(f32[8,2,256,256]{3,2,1,0:T(8,128)} %bitcast.13, bf16[8,2,256,256]{3,2,1,0:T(8,128)(2,1)} %bitcast.14), kind=kOutput, calls=%fused_computation.11 | convolution fusion | flops 3221225472 | bytes 8388608 | tf_op jit(solution)/shard_map/opij,opjk->oik/dot_general | solution.py:49
  323.0 74.4 %reduce-scatter.2.cloned.1.call-done = f32[8,16,256]{2,1,0:T(8,128)} async-done(((f32[8,256,256]{2,1,0:T(8,128)}), f32[8,16,256]{2,1,0:T(8,128)}) %reduce-scatter.2.cloned.1.call-update) | async-done | bytes 131088 | tf_op jit(solution)/shard_map/reduce_scatter | solution.py:55
  397.4 1.6 and_select_fusion
  (37 shorter events, 0.5 us)
Async XLA Ops:
  6.5 17.6 %copy-start = (bf16[8,256,256]{2,1,0:T(8,128)(2,1)S(1)}, bf16[8,256,256]{2,1,0:T(8,128)(2,1)}, u32[]{:S(2)}) copy-start(bf16[8,256,256]{2,1,0:T(8,128)(2,1)} %param.14) | copy-start | bytes 3145732
  6.5 19.6 %copy-start.5 = (s32[192]{0:T(256)S(1)}, s32[192]{0:T(256)}, u32[]{:S(2)}) copy-start(s32[192]{0:T(256)} %param.18) | copy-start | bytes 2308
  6.5 95.4 %all-gather.2.cloned.1.call-start = ((), (), s32[]{:S(2)}) async-start(), calls=%async_computation.1 | async-start | bytes 8912896 | tf_op jit(solution)/shard_map/all_gather | solution.py:25
  22.4 375.0 %reduce-scatter.2.cloned.1.call-start = ((), (), s32[]{:S(2)}) async-start(), calls=%async_computation.2 | async-start | bytes 2228224 | tf_op jit(solution)/shard_map/reduce_scatter | solution.py:55
  24.1 80.2 %copy-start.1 = (bf16[16,256,256]{2,1,0:T(8,128)(2,1)S(1)}, bf16[16,256,256]{2,1,0:T(8,128)(2,1)}, u32[]{:S(2)}) copy-start(bf16[16,256,256]{2,1,0:T(8,128)(2,1)} %param.13) | copy-start | bytes 6291460
  24.1 80.2 %copy-start.2 = (s32[192]{0:T(256)S(1)}, s32[192]{0:T(256)}, u32[]{:S(2)}) copy-start(s32[192]{0:T(256)} %param.20) | copy-start | bytes 2308
  24.1 80.2 %copy-start.3 = (s32[192]{0:T(256)S(1)}, s32[192]{0:T(256)}, u32[]{:S(2)}) copy-start(s32[192]{0:T(256)} %param.19) | copy-start | bytes 2308
  24.2 80.2 %copy-start.4 = (s32[192]{0:T(256)S(1)}, s32[192]{0:T(256)}, u32[]{:S(2)}) copy-start(s32[192]{0:T(256)} %param.21) | copy-start | bytes 2308
  316.5 6.3 %copy-start.6 = (s32[8]{0:T(128)S(1)}, s32[8]{0:T(128)}, u32[]{:S(2)}) copy-start(s32[8]{0:T(128)} %param.15) | copy-start | bytes 100
Sparse Core Ops, SparseCore 0:
  22.5 79.4 all-gather.1
  322.9 74.4 reduce-scatter.1
where the time goes:
time: 407 us; the launch traced here: 406 us
  waiting for transfers between devices  150 us (37%)
  other arithmetic  113 us (28%)
  local copies, waits for them, and re-layouts  59.1 us (15%)
  matrix products  53.9 us (13%)
  blocking collectives  15.8 us (4%)
  between operations  13.5 us (3%)
    scatter-add x6, other arithmetic, accumulate(): return totals.at[out_ids].add(weighted)  110 us
    all_gather x1, waiting for transfers between devices, local(): pool = lax.all_gather(local_all, 'table', axis=1, tiled=True)  75.7 us
    reduce_scatter x1, waiting for transfers between devices, local(): result = lax.psum_scatter(joined, 'table', scatter_dimension=1, tiled=True)  74.4 us
    dot_general x6, matrix products, accumulate(): jnp.einsum('tij,tjk->tik', recoupling[tab_ids], pool[src_ids], preferred_...  47.7 us
    gather x6, local copies, waits for them, and re-layouts, accumulate(): pool[src_ids]  37.1 us
    gather x6, local copies, waits for them, and re-layouts, accumulate(): recoupling[tab_ids]  16.5 us
    all_gather x1, blocking collectives, local(): local_all = lax.all_gather(wave_blocks, 'sector', axis=0, tiled=True)  15.8 us
  transfers between devices with their start and end apart: 2, of which 2 were waited for; matrix products, arithmetic and copies ran while one was open for 1% of the time, Pallas kernels for 0%

commit v1 on v0

v1 whole, which is shorter than its diff:
```python
import functools

import jax
import jax.numpy as jnp
from jax import lax
from jax.experimental import pallas as pl
from jax.experimental.pallas import tpu as pltpu
from jax.sharding import PartitionSpec as P

BF = jnp.bfloat16
F32 = jnp.float32
SIDE = 4
TABS = 16
ROWS = 16
HALF = 64
WIDTH = 256
SLOTS = 16
PICKS = 24
PAIRS = SLOTS * PICKS
SHARE = ROWS * 128
SENT = SHARE + PAIRS
DEPTH = PICKS * HALF
MIB = 1 << 20


def swap_halves(value):
    return pltpu.roll(value, 64, 1)


def pack_kernel(meta, t0_ref, t1_ref, terms_ref, out_ref, rows0, rows1, count):
    low = lax.broadcasted_iota(jnp.int32, (TABS, 128), 1) < 64

    @pl.when(pl.program_id(0) == 0)
    def _():
        pair = terms_ref[0:1, :]
        tab = terms_ref[1:2, :]
        live = terms_ref[2:3, :]
        terms = terms_ref.shape[1]
        tab_hot = (lax.broadcasted_iota(jnp.int32, (TABS, terms), 0) == tab) & (live > 0)
        pair_hot = lax.broadcasted_iota(jnp.int32, (PAIRS, terms), 0) == pair
        counts = lax.dot_general(
            tab_hot.astype(F32).astype(BF),
            pair_hot.astype(F32).astype(BF),
            (((1,), (1,)), ((), ())),
            preferred_element_type=F32,
        )
        count[...] = counts.astype(BF)

    for k in range(2):
        rows0[k] = t0_ref[:, 0, :, k * 128 : k * 128 + 128].reshape(TABS * ROWS, 128).astype(F32)
        rows1[k] = t1_ref[:, 0, :, k * 128 : k * 128 + 128].reshape(TABS * ROWS, 128).astype(F32)
    for y in range(SIDE):
        out_ref[y, 0, :, SHARE:SENT] = count[...]
    for q in range(ROWS):
        lanes = slice(q * 128, q * 128 + 128)
        for k in range(2):
            a = rows0[k, pl.ds(q, TABS, stride=ROWS), :]
            b = rows1[k, pl.ds(q, TABS, stride=ROWS), :]
            out_ref[2 * k, 0, :, lanes] = jnp.where(low, a, swap_halves(b)).astype(BF)
            out_ref[2 * k + 1, 0, :, lanes] = jnp.where(low, swap_halves(a), b).astype(BF)


def pack(core, recoupling, terms):
    blocks = recoupling.reshape(TABS, SIDE, HALF, WIDTH)
    out = pl.pallas_call(
        pack_kernel,
        grid_spec=pltpu.PrefetchScalarGridSpec(
            num_scalar_prefetch=1,
            grid=(SIDE,),
            in_specs=[
                pl.BlockSpec((TABS, 1, ROWS, WIDTH), lambda x, m: (0, m[0], x, 0)),
                pl.BlockSpec((TABS, 1, ROWS, WIDTH), lambda x, m: (0, m[0] + 2, x, 0)),
                pl.BlockSpec(terms.shape, lambda x, m: (0, 0)),
            ],
            out_specs=pl.BlockSpec((SIDE, 1, TABS, SENT), lambda x, m: (0, x, 0, 0)),
            scratch_shapes=[
                pltpu.VMEM((2, TABS * ROWS, 128), F32),
                pltpu.VMEM((2, TABS * ROWS, 128), F32),
                pltpu.VMEM((TABS, PAIRS), BF),
            ],
        ),
        out_shape=jax.ShapeDtypeStruct((SIDE, SIDE, TABS, SENT), BF),
        compiler_params=pltpu.CompilerParams(vmem_limit_bytes=24 * MIB),
        name="pack",
    )(core, blocks, blocks, terms)
    return out.reshape(SIDE * SIDE, TABS, SENT)


def select_kernel(meta, w0, w1, w2, w3, out_ref):
    z = meta[0]
    core = meta[1]
    for p in range(PICKS):
        group = p // 3
        piece = meta[2 + p]
        step = lax.rem(z - group // 2 + SIDE, SIDE)
        other = jnp.where(core == group % 2, 0, 1)
        for d, ref in enumerate((w0, w1, w2, w3)):

            @pl.when(step == d)
            def _(ref=ref, p=p, other=other, piece=piece):
                out_ref[p] = ref[other * 8 + piece]


def select(meta, pieces):
    return pl.pallas_call(
        select_kernel,
        in_specs=[pl.BlockSpec(memory_space=pltpu.SMEM)] + [pl.BlockSpec(memory_space=pltpu.VMEM)] * 4,
        out_specs=pl.BlockSpec(memory_space=pltpu.VMEM),
        out_shape=jax.ShapeDtypeStruct((PICKS, ROWS, WIDTH), BF),
        compiler_params=pltpu.CompilerParams(vmem_limit_bytes=8 * MIB),
        name="select",
    )(meta, *pieces)


def weigh_kernel(c_ref, t_ref, hi_ref, lo_ref, sums):
    counts = c_ref[...]
    for n in range(ROWS // 2):
        part = lax.dot_general(
            counts, t_ref[:, n * 256 : n * 256 + 256], (((0,), (0,)), ((), ())), preferred_element_type=F32
        )
        sums[2 * n * PAIRS : (2 * n + 1) * PAIRS, :] = part[:, :128]
        sums[(2 * n + 1) * PAIRS : (2 * n + 2) * PAIRS, :] = part[:, 128:]
    low = lax.broadcasted_iota(jnp.int32, (ROWS, 128), 1) < 64

    def one(s, carry):
        for k in range(PICKS // 2):
            row = s * PICKS + 2 * k
            a = sums[pl.ds(row, ROWS, stride=PAIRS), :]
            b = sums[pl.ds(row + 1, ROWS, stride=PAIRS), :]
            for u, value in enumerate((jnp.where(low, a, swap_halves(b)), jnp.where(low, swap_halves(a), b))):
                hi = value.astype(BF)
                lo = (value - hi.astype(F32)).astype(BF)
                hi_ref[s, u, :, k * 128 : k * 128 + 128] = hi
                lo_ref[s, u, :, k * 128 : k * 128 + 128] = lo
        return carry

    lax.fori_loop(0, SLOTS, one, 0)


def weigh(counts, share):
    shape = jax.ShapeDtypeStruct((SLOTS, 2, ROWS, DEPTH), BF)
    tabs = TABS * SIDE * SIDE
    return pl.pallas_call(
        weigh_kernel,
        grid=(1,),
        in_specs=[
            pl.BlockSpec((tabs, PAIRS), lambda i: (0, 0)),
            pl.BlockSpec((tabs, SHARE), lambda i: (0, 0)),
        ],
        out_specs=[pl.BlockSpec(shape.shape, lambda i: (0, 0, 0, 0))] * 2,
        out_shape=[shape, shape],
        scratch_shapes=[pltpu.VMEM((ROWS * PAIRS, 128), F32)],
        compiler_params=pltpu.CompilerParams(vmem_limit_bytes=32 * MIB),
        name="weigh",
    )(counts, share)


def apply_kernel(meta, oh, ol, xh, xl, w0, w1, w2, w3, right, s0, s1, s2, s3, wave, lhs_hi, lhs_lo, total):
    core, x, y = meta[0], meta[1], meta[2]
    o = pl.program_id(0)

    @pl.when(o == 0)
    def _():
        for d, ref in enumerate((w0, w1, w2, w3)):
            place = pl.multiple_of(lax.rem(x - d + SIDE, SIDE) * ROWS, ROWS)
            wave[:, pl.ds(place, ROWS), :] = ref[...]

    weights = wave[...].reshape(DEPTH, WIDTH)
    mine = pl.multiple_of(core * ROWS, ROWS)
    theirs = pl.multiple_of((1 - core) * ROWS, ROWS)
    for half, hi_ref, lo_ref in ((mine, oh, ol), (theirs, xh, xl)):
        lhs_hi[:, pl.ds(half, ROWS), :] = hi_ref[...].reshape(4, ROWS, DEPTH)
        lhs_lo[:, pl.ds(half, ROWS), :] = lo_ref[...].reshape(4, ROWS, DEPTH)
    channel = jnp.dot(lhs_hi[...].reshape(128, DEPTH), weights, preferred_element_type=F32)
    channel = channel + jnp.dot(lhs_lo[...].reshape(128, DEPTH), weights, preferred_element_type=F32)
    hi = channel.astype(BF)
    lo = (channel - hi.astype(F32)).astype(BF)
    result = jnp.zeros((HALF, WIDTH), F32)
    for p in range(2):
        env = right[meta[3 + 2 * o + p]]
        rows = slice(p * HALF, (p + 1) * HALF)
        result = result + jnp.dot(hi[rows], env, preferred_element_type=F32)
        result = result + jnp.dot(lo[rows], env, preferred_element_type=F32)
    total[...] = result
    for d, ref in enumerate((s0, s1, s2, s3)):
        place = pl.multiple_of(lax.rem(y + d, SIDE) * ROWS, ROWS)
        ref[0] = total[pl.ds(place, ROWS), :]


def apply(meta, own, far, pieces, right):
    sectors = SLOTS // 2
    lhs_spec = pl.BlockSpec((2, 2, ROWS, DEPTH), lambda o, m: (o, 0, 0, 0))
    whole = lambda a: pl.BlockSpec(a.shape, lambda o, m: (0, 0, 0))
    return pl.pallas_call(
        apply_kernel,
        grid_spec=pltpu.PrefetchScalarGridSpec(
            num_scalar_prefetch=1,
            grid=(sectors,),
            in_specs=[lhs_spec] * 4 + [whole(p) for p in pieces] + [whole(right)],
            out_specs=[pl.BlockSpec((1, ROWS, WIDTH), lambda o, m: (o, 0, 0))] * 4,
            scratch_shapes=[
                pltpu.VMEM((PICKS, HALF, WIDTH), BF),
                pltpu.VMEM((4, 2 * ROWS, DEPTH), BF),
                pltpu.VMEM((4, 2 * ROWS, DEPTH), BF),
                pltpu.VMEM((HALF, WIDTH), F32),
            ],
        ),
        out_shape=[jax.ShapeDtypeStruct((sectors, ROWS, WIDTH), F32)] * 4,
        compiler_params=pltpu.CompilerParams(vmem_limit_bytes=32 * MIB),
        name="apply",
    )(meta, *own, *far, *pieces, right)


def along_table(dy, dx):
    return [
        (y * SIDE + x, (y + dy) % SIDE * SIDE + (x + dx) % SIDE) for y in range(SIDE) for x in range(SIDE)
    ]


def along_sector(dz, dc):
    return [(z * 2 + c, (z + dz) % SIDE * 2 + (c ^ dc)) for z in range(SIDE) for c in range(2)]


def local(
    wave_blocks,
    recoupling,
    right_blocks,
    sector_sizes,
    channel_env,
    fetch_list,
    term_pick,
    term_table,
    term_slot,
    term_live,
):
    sector = lax.axis_index("sector")
    place = lax.axis_index("table")
    z, core = sector // 2, sector % 2
    y, x = place // SIDE, place % SIDE

    other = lax.ppermute(wave_blocks, "sector", along_sector(0, 1))
    both = jnp.concatenate([wave_blocks, other], axis=0)
    pool = [both] + [lax.ppermute(both, "sector", along_sector(d, 0)) for d in (1, 2, 3)]

    terms = jnp.stack([term_slot * PICKS + term_pick, term_table, term_live])
    sent = pack(core.reshape(1), recoupling, terms)
    mine = lax.all_to_all(sent, "table", 0, 0).reshape(TABS * SIDE * SIDE, SENT)
    theirs = lax.ppermute(mine, "sector", along_sector(0, 1))

    chosen = select(jnp.concatenate([jnp.stack([z, core]), fetch_list.reshape(-1)]), pool)
    pieces = [chosen] + [lax.ppermute(chosen, "table", along_table(0, d)) for d in (1, 2, 3)]

    counts = mine[:, SHARE:]
    own = weigh(counts, mine)
    far = weigh(counts, theirs)
    meta = jnp.concatenate([jnp.stack([core, x, y]), channel_env.reshape(-1)])
    parts = apply(meta, own, far, pieces, right_blocks)
    result = parts[0]
    for d in (1, 2, 3):
        result = result + lax.ppermute(parts[d], "table", along_table(d, 0))

    rows = place * ROWS + jnp.arange(ROWS, dtype=jnp.int32)
    columns = jnp.arange(WIDTH, dtype=jnp.int32)
    limits = sector_sizes[:, None, None]
    keep = (rows[None, :, None] < limits) & (columns[None, None, :] < limits)
    return jnp.where(keep, result, jnp.float32(0.0))


def solution(mesh):
    placed = (
        P("sector", "table", None),
        P("table", None, None),
        P("sector", None, None),
        P("sector"),
        P("sector", None),
        P("sector", None, None),
        P(("sector", "table")),
        P(("sector", "table")),
        P(("sector", "table")),
        P(("sector", "table")),
    )
    return jax.shard_map(
        local, mesh=mesh, in_specs=placed, out_specs=P("sector", "table", None), check_vma=False
    )
```

time: 407 us -> 76 us (0.19)
  waiting for transfers between devices: 150 us -> 14.7 us
  other arithmetic: 113 us -> 2.45 us
  local copies, waits for them, and re-layouts: 59.1 us -> 1.97 us
  matrix products: 53.9 us -> 0 us
  Pallas kernels: 0 us -> 15.8 us
  starting transfers between devices: 0.04 us -> 13.7 us
  between operations: 13.5 us -> 0.11 us
  blocking collectives: 15.8 us -> 26.3 us
    scatter-add x6 -> x0, other arithmetic: 110 us -> none  [accumulate(): return totals.at[out_ids].add(weighted)]
    all_gather x1 -> x0, waiting for transfers between devices: 75.7 us -> none  [local(): pool = lax.all_gather(local_all, 'table', axis=1, tiled=True)]
    reduce_scatter x1 -> x0, waiting for transfers between devices: 74.4 us -> none  [local(): result = lax.psum_scatter(joined, 'table', scatter_dimension=1, tiled=True)]
    gather x13 -> x0, local copies, waits for them, and re-layouts: 55.6 us -> none  [the longest x6 37.1 us: accumulate(): pool[src_ids]]
    dot_general x7 -> x0, matrix products: 53.9 us -> none  [the longest x6 47.7 us: accumulate(): jnp.einsum('tij,tjk->tik', recoupling[tab_ids], pool[src_ids], preferred_...]
    all_to_all x0 -> x1, blocking collectives: none -> 26.3 us  [local(): mine = lax.all_to_all(sent, 'table', 0, 0).reshape(TABS * SIDE * SIDE, SENT)]
    all_gather x1 -> x0, blocking collectives: 15.8 us -> none  [local(): local_all = lax.all_gather(wave_blocks, 'sector', axis=0, tiled=True)]
    pallas_call x0 -> x5, Pallas kernels: none -> 15.8 us  [the longest x2 7.13 us: weigh(): pl.pallas_call(weigh_kernel, grid=(1,), in_specs=[pl.BlockSpec((tabs, PAI...]
  transfers between devices with their start and end apart: 2 -> 11, of which waited for: 2 -> 7; matrix products, arithmetic and copies ran while one was open for 1% -> 1% of each run, Pallas kernels for 0% -> 11%
where the time goes in v1:
time: 76 us; the launch traced here: 75.1 us
  blocking collectives  26.3 us (35%)
  Pallas kernels  15.8 us (21%)
  waiting for transfers between devices  14.7 us (19%)
  starting transfers between devices  13.7 us (18%)
  other arithmetic  2.45 us (3%)
  local copies, waits for them, and re-layouts  1.97 us (3%)
    all_to_all x1, blocking collectives, local(): mine = lax.all_to_all(sent, 'table', 0, 0).reshape(TABS * SIDE * SIDE, SENT)  26.3 us
    pallas_call x2, Pallas kernels, weigh(): pl.pallas_call(weigh_kernel, grid=(1,), in_specs=[pl.BlockSpec((tabs, PAI...  7.13 us
    ppermute x3, starting transfers between devices, local(): lax.ppermute(both, 'sector', along_sector(d, 0))  6.51 us
    ppermute x3, waiting for transfers between devices, local(): result = result + lax.ppermute(parts[d], 'table', along_table(d, 0))  6.16 us
    pallas_call x1, Pallas kernels, apply(): pl.pallas_call(apply_kernel, grid_spec=pltpu.PrefetchScalarGridSpec(num_s...  6.08 us
    ppermute x3, waiting for transfers between devices, local(): lax.ppermute(both, 'sector', along_sector(d, 0))  4.99 us
    ppermute x3, starting transfers between devices, local(): lax.ppermute(chosen, 'table', along_table(0, d))  3.77 us
    ppermute x3, starting transfers between devices, local(): result = result + lax.ppermute(parts[d], 'table', along_table(d, 0))  2.94 us
  transfers between devices with their start and end apart: 11, of which 7 were waited for; matrix products, arithmetic and copies ran while one was open for 1% of the time, Pallas kernels for 11%

profile of v1, /device:TPU:0, one launch (start us, length us, event | category | flops | bytes accessed | tf_op | source)
XLA Modules:
  0.0 75.1 jit_solution(5072676943294610134)
XLA Ops:
  0.0 0.7 multiply_add_fusion
  0.7 0.7 pad_add_fusion.terms_ref
  1.4 1.6 %copy-done = bf16[16,256,256]{2,1,0:T(8,128)(2,1)S(1)} copy-done((bf16[16,256,256]{2,1,0:T(8,128)(2,1)S(1)}, bf16[16,256,256]{2,1,0:T(8,128)(2,1)}, u32[]{:S(2)}) %copy-start) | copy-done | bytes 2097176
  3.0 1.6 %pack.1 = bf16[4,4,16,2432]{3,2,1,0:T(8,128)(2,1)S(1)} custom-call(s32[1]{0:T(128)} %bitcast.meta, bf16[16,4,64,256]{3,2,1,0:T(8,128)(2,1)S(1)} %bitcast.10, bf16[16,4,64,256]{3,2,1,0:T(8,128)(2,1)S(1)} %bitcast.11, s32[3,192]{1,0:T(4,128)S(1)} %pad_add_fusion.terms_ref), custom_call_target="tpu_custom_call" | custom-call | tf_op jit(solution)/shard_map/pack/pallas_call | solution.py:65
  4.6 0.0 copy-start.2
  4.7 0.0 copy-start.4
  4.7 0.0 copy-start.5
  4.7 0.0 copy-start.3
  4.7 26.3 %all_to_all.5 = bf16[16,16,2432]{2,1,0:T(8,128)(2,1)S(1)} all-to-all(bf16[16,16,2432]{2,1,0:T(8,128)(2,1)S(1)} %bitcast.15), channel_id=1, replica_groups=mesh['sector'=8,'table'=16] {'table'}, dimensions={0} | all-to-all | bytes 2490368 | tf_op jit(solution)/shard_map/all_to_all | solution.py:247
  31.0 0.0 collective-permute-start
  31.0 0.0 copy-done.2
  31.0 0.5 collective-permute-start.1
  31.5 0.0 copy-done.4
  31.5 0.1 copy.14
  31.6 0.1 reshape.77
  31.7 2.3 %collective-permute-done.1 = bf16[8,16,256]{2,1,0:T(8,128)(2,1)S(1)} collective-permute-done((bf16[8,16,256]{2,1,0:T(8,128)(2,1)S(1)}, bf16[8,16,256]{2,1,0:T(8,128)(2,1)S(1)}, u32[]{:S(2)}, u32[]{:S(2)}) %collective-permute-start.1) | collective-permute-done | bytes 65568 | tf_op jit(solution)/shard_map/ppermute | solution.py:241
  34.0 1.9 %collective-permute-start.2 = (bf16[16,16,256]{2,1,0:T(8,128)(2,1)S(1)}, bf16[16,16,256]{2,1,0:T(8,128)(2,1)S(1)}, u32[]{:S(2)}, u32[]{:S(2)}) collective-permute-start(bf16[16,16,256]{2,1,0:T(8,128)(2,1)S(1)} %constant_dynamic-update-slice_fusion.w0), channel_id=1, source_target_pairs={{0,32},{16,48},{32,64},{48,80},{64,96},{80,112},{96,0},{112,16},{1... | collective-permute-start | bytes 393224 | tf_op jit(solution)/shard_map/ppermute | solution.py:243
  36.0 3.6 %collective-permute-start.3 = (bf16[16,16,256]{2,1,0:T(8,128)(2,1)S(1)}, bf16[16,16,256]{2,1,0:T(8,128)(2,1)S(1)}, u32[]{:S(2)}, u32[]{:S(2)}) collective-permute-start(bf16[16,16,256]{2,1,0:T(8,128)(2,1)S(1)} %constant_dynamic-update-slice_fusion.w0), channel_id=1, source_target_pairs={{0,64},{16,80},{32,96},{48,112},{64,0},{80,16},{96,32},{112,48},{1... | collective-permute-start | bytes 393224 | tf_op jit(solution)/shard_map/ppermute | solution.py:243
  39.5 1.0 %collective-permute-start.4 = (bf16[16,16,256]{2,1,0:T(8,128)(2,1)S(1)}, bf16[16,16,256]{2,1,0:T(8,128)(2,1)S(1)}, u32[]{:S(2)}, u32[]{:S(2)}) collective-permute-start(bf16[16,16,256]{2,1,0:T(8,128)(2,1)S(1)} %constant_dynamic-update-slice_fusion.w0), channel_id=1, source_target_pairs={{0,96},{16,112},{32,0},{48,16},{64,32},{80,48},{96,64},{112,80},{1... | collective-permute-start | bytes 393224 | tf_op jit(solution)/shard_map/ppermute | solution.py:243
  40.5 0.1 pad_add_fusion.2.meta
  40.6 0.0 copy-done.5
  40.6 0.1 copy.13
  40.7 0.1 reshape.73
  40.8 0.1 pad_add_fusion.1.meta
  40.9 1.0 %collective-permute-done.2.w1 = bf16[16,16,256]{2,1,0:T(8,128)(2,1)S(1)} collective-permute-done((bf16[16,16,256]{2,1,0:T(8,128)(2,1)S(1)}, bf16[16,16,256]{2,1,0:T(8,128)(2,1)S(1)}, u32[]{:S(2)}, u32[]{:S(2)}) %collective-permute-start.2) | collective-permute-done | bytes 131104 | tf_op jit(solution)/shard_map/ppermute | solution.py:243
  41.9 4.0 %collective-permute-done.3.w2 = bf16[16,16,256]{2,1,0:T(8,128)(2,1)S(1)} collective-permute-done((bf16[16,16,256]{2,1,0:T(8,128)(2,1)S(1)}, bf16[16,16,256]{2,1,0:T(8,128)(2,1)S(1)}, u32[]{:S(2)}, u32[]{:S(2)}) %collective-permute-start.3) | collective-permute-done | bytes 131104 | tf_op jit(solution)/shard_map/ppermute | solution.py:243
  45.9 0.0 collective-permute-done.4.w3
  45.9 0.9 %select.13.w0 = bf16[24,16,256]{2,1,0:T(8,128)(2,1)S(1)} custom-call(s32[26]{0:T(128)S(1)} %pad_add_fusion.2.meta, bf16[16,16,256]{2,1,0:T(8,128)(2,1)S(1)} %constant_dynamic-update-slice_fusion.w0, bf16[16,16,256]{2,1,0:T(8,128)(2,1)S(1)} %collective-permute-done.2.w1, bf16[16,16,256]{2,1,0:T(8,128)(2,1)S(1)} %collective-permute-done.3.w2, ...), custom_call_target="tpu_custom_call" | custom-call | tf_op jit(solution)/shard_map/select/pallas_call | solution.py:105
  46.8 0.6 collective-permute-start.5
  47.5 1.8 %collective-permute-start.6 = (bf16[24,16,256]{2,1,0:T(8,128)(2,1)S(1)}, bf16[24,16,256]{2,1,0:T(8,128)(2,1)S(1)}, u32[]{:S(2)}, u32[]{:S(2)}) collective-permute-start(bf16[24,16,256]{2,1,0:T(8,128)(2,1)S(1)} %select.13.w0), channel_id=1, source_target_pairs={{0,2},{1,3},{2,0},{3,1},{4,6},{5,7},{6,4},{7,5},{8,10},{9,11},{10,... | collective-permute-start | bytes 589832 | tf_op jit(solution)/shard_map/ppermute | solution.py:251
  49.2 1.4 %collective-permute-start.7 = (bf16[24,16,256]{2,1,0:T(8,128)(2,1)S(1)}, bf16[24,16,256]{2,1,0:T(8,128)(2,1)S(1)}, u32[]{:S(2)}, u32[]{:S(2)}) collective-permute-start(bf16[24,16,256]{2,1,0:T(8,128)(2,1)S(1)} %select.13.w0), channel_id=1, source_target_pairs={{0,3},{1,0},{2,1},{3,2},{4,7},{5,4},{6,5},{7,6},{8,11},{9,8},{10,9... | collective-permute-start | bytes 589832 | tf_op jit(solution)/shard_map/ppermute | solution.py:251
  50.6 0.0 copy-done.3
  50.6 0.1 iota_compare_fusion
  50.7 3.6 %weigh.2 = (bf16[16,2,16,1536]{3,2,1,0:T(8,128)(2,1)S(1)}, bf16[16,2,16,1536]{3,2,1,0:T(8,128)(2,1)S(1)}) custom-call(bf16[256,384]{1,0:T(8,128)(2,1)S(1)} %slice.4.c_ref, bf16[256,2432]{1,0:T(8,128)(2,1)S(1)} %bitcast.14), custom_call_target="tpu_custom_call" | custom-call | tf_op jit(solution)/shard_map/weigh/pallas_call | solution.py:143
  54.3 0.0 collective-permute-done.t_ref
  54.3 3.6 %weigh.3 = (bf16[16,2,16,1536]{3,2,1,0:T(8,128)(2,1)S(1)}, bf16[16,2,16,1536]{3,2,1,0:T(8,128)(2,1)S(1)}) custom-call(bf16[256,384]{1,0:T(8,128)(2,1)S(1)} %slice.4.c_ref, bf16[256,2432]{1,0:T(8,128)(2,1)S(1)} %collective-permute-done.t_ref), custom_call_target="tpu_custom_call" | custom-call | tf_op jit(solution)/shard_map/weigh/pallas_call | solution.py:143
  57.8 0.6 collective-permute-done.5.w1
  58.4 0.0 collective-permute-done.6.w2
  58.4 0.6 collective-permute-done.7.w3
  59.1 6.1 %apply.1 = (f32[8,16,256]{2,1,0:T(8,128)S(1)}, f32[8,16,256]{2,1,0:T(8,128)S(1)}, f32[8,16,256]{2,1,0:T(8,128)S(1)}, f32[8,16,256]{2,1,0:T(8,128)S(1)}) custom-call(s32[19]{0:T(128)S(1)} %pad_add_fusion.1.meta, bf16[16,2,16,1536]{3,2,1,0:T(8,128)(2,1)S(1)} %get-tuple-element.13.oh, bf16[16,2,16,1536]{3,2,1,0:T(8,128)(2,1)S(1)} %get-tuple-element.14.ol, ...), custom_call_target="tpu_custom_call" | custom-call | tf_op jit(solution)/shard_map/apply/pallas_call | solution.py:194
  65.1 0.9 %collective-permute-start.10 = (f32[8,16,256]{2,1,0:T(8,128)S(1)}, f32[8,16,256]{2,1,0:T(8,128)S(1)}, u32[]{:S(2)}, u32[]{:S(2)}) collective-permute-start(f32[8,16,256]{2,1,0:T(8,128)S(1)} %get-tuple-element.20), channel_id=1, source_target_pairs={{0,12},{1,13},{2,14},{3,15},{4,0},{5,1},{6,2},{7,3},{8,4},{9,5},{1... | collective-permute-start | bytes 393224 | tf_op jit(solution)/shard_map/ppermute | solution.py:260
  66.1 1.2 %collective-permute-start.8 = (f32[8,16,256]{2,1,0:T(8,128)S(1)}, f32[8,16,256]{2,1,0:T(8,128)S(1)}, u32[]{:S(2)}, u32[]{:S(2)}) collective-permute-start(f32[8,16,256]{2,1,0:T(8,128)S(1)} %get-tuple-element.18), channel_id=1, source_target_pairs={{0,4},{1,5},{2,6},{3,7},{4,8},{5,9},{6,10},{7,11},{8,12},{9,13},{1... | collective-permute-start | bytes 393224 | tf_op jit(solution)/shard_map/ppermute | solution.py:260
  67.2 0.8 %collective-permute-start.9 = (f32[8,16,256]{2,1,0:T(8,128)S(1)}, f32[8,16,256]{2,1,0:T(8,128)S(1)}, u32[]{:S(2)}, u32[]{:S(2)}) collective-permute-start(f32[8,16,256]{2,1,0:T(8,128)S(1)} %get-tuple-element.19), channel_id=1, source_target_pairs={{0,8},{1,9},{2,10},{3,11},{4,12},{5,13},{6,14},{7,15},{8,0},{9,1},... | collective-permute-start | bytes 393224 | tf_op jit(solution)/shard_map/ppermute | solution.py:260
  68.1 0.1 broadcast_compare_fusion
  68.2 3.1 %collective-permute-done.10 = f32[8,16,256]{2,1,0:T(8,128)S(1)} collective-permute-done((f32[8,16,256]{2,1,0:T(8,128)S(1)}, f32[8,16,256]{2,1,0:T(8,128)S(1)}, u32[]{:S(2)}, u32[]{:S(2)}) %collective-permute-start.10) | collective-permute-done | bytes 131104 | tf_op jit(solution)/shard_map/ppermute | solution.py:260
  71.2 3.1 %collective-permute-done.8 = f32[8,16,256]{2,1,0:T(8,128)S(1)} collective-permute-done((f32[8,16,256]{2,1,0:T(8,128)S(1)}, f32[8,16,256]{2,1,0:T(8,128)S(1)}, u32[]{:S(2)}, u32[]{:S(2)}) %collective-permute-start.8) | collective-permute-done | bytes 131104 | tf_op jit(solution)/shard_map/ppermute | solution.py:260
  74.3 0.0 collective-permute-done.9
  74.3 0.7 add_select_fusion
  (7 shorter events, 0.0 us)
Async XLA Ops:
  1.4 1.6 %copy-start = (bf16[16,256,256]{2,1,0:T(8,128)(2,1)S(1)}, bf16[16,256,256]{2,1,0:T(8,128)(2,1)}, u32[]{:S(2)}) copy-start(bf16[16,256,256]{2,1,0:T(8,128)(2,1)} %param.11) | copy-start | bytes 6291460
  4.6 26.4 %copy-start.2 = (bf16[8,16,256]{2,1,0:T(8,128)(2,1)S(1)}, bf16[8,16,256]{2,1,0:T(8,128)(2,1)}, u32[]{:S(2)}) copy-start(bf16[8,16,256]{2,1,0:T(8,128)(2,1)} %param.10) | copy-start | bytes 196612
  4.7 26.9 %copy-start.4 = (s32[1,8,3]{1,0,2:T(1,128)S(1)}, s32[1,8,3]{1,0,2:T(1,128)}, u32[]{:S(2)}) copy-start(s32[1,8,3]{1,0,2:T(1,128)} %param.15) | copy-start | bytes 292
  4.7 36.0 %copy-start.5 = (s32[8,2]{0,1:T(2,128)S(1)}, s32[8,2]{0,1:T(2,128)}, u32[]{:S(2)}) copy-start(s32[8,2]{0,1:T(2,128)} %param.14) | copy-start | bytes 196
  4.7 45.9 %copy-start.3 = (s32[8]{0:T(128)S(1)}, s32[8]{0:T(128)}, u32[]{:S(2)}) copy-start(s32[8]{0:T(128)} %param.13) | copy-start | bytes 100
  31.0 23.3 %collective-permute-start = (bf16[256,2432]{1,0:T(8,128)(2,1)S(1)}, bf16[256,2432]{1,0:T(8,128)(2,1)S(1)}, u32[]{:S(2)}, u32[]{:S(2)}) collective-permute-start(bf16[256,2432]{1,0:T(8,128)(2,1)S(1)} %bitcast.12), channel_id=1, source_target_pairs={{0,16},{16,0},{32,48},{48,32},{64,80},{80,64},{96,112},{112,96},{1... | collective-permute-start | bytes 3735560 | tf_op jit(solution)/shard_map/ppermute | solution.py:248
  31.0 3.0 %collective-permute-start.1 = (bf16[8,16,256]{2,1,0:T(8,128)(2,1)S(1)}, bf16[8,16,256]{2,1,0:T(8,128)(2,1)S(1)}, u32[]{:S(2)}, u32[]{:S(2)}) collective-permute-start(bf16[8,16,256]{2,1,0:T(8,128)(2,1)S(1)} %copy-done.2), channel_id=1, source_target_pairs={{0,16},{16,0},{32,48},{48,32},{64,80},{80,64},{96,112},{112,96},{1... | collective-permute-start | bytes 196616 | tf_op jit(solution)/shard_map/ppermute | solution.py:241
  34.0 7.8 %collective-permute-start.2 = (bf16[16,16,256]{2,1,0:T(8,128)(2,1)S(1)}, bf16[16,16,256]{2,1,0:T(8,128)(2,1)S(1)}, u32[]{:S(2)}, u32[]{:S(2)}) collective-permute-start(bf16[16,16,256]{2,1,0:T(8,128)(2,1)S(1)} %constant_dynamic-update-slice_fusion.w0), channel_id=1, source_target_pairs={{0,32},{16,48},{32,64},{48,80},{64,96},{80,112},{96,0},{112,16},{1... | collective-permute-start | bytes 393224 | tf_op jit(solution)/shard_map/ppermute | solution.py:243
  36.0 9.9 %collective-permute-start.3 = (bf16[16,16,256]{2,1,0:T(8,128)(2,1)S(1)}, bf16[16,16,256]{2,1,0:T(8,128)(2,1)S(1)}, u32[]{:S(2)}, u32[]{:S(2)}) collective-permute-start(bf16[16,16,256]{2,1,0:T(8,128)(2,1)S(1)} %constant_dynamic-update-slice_fusion.w0), channel_id=1, source_target_pairs={{0,64},{16,80},{32,96},{48,112},{64,0},{80,16},{96,32},{112,48},{1... | collective-permute-start | bytes 393224 | tf_op jit(solution)/shard_map/ppermute | solution.py:243
  39.5 6.3 %collective-permute-start.4 = (bf16[16,16,256]{2,1,0:T(8,128)(2,1)S(1)}, bf16[16,16,256]{2,1,0:T(8,128)(2,1)S(1)}, u32[]{:S(2)}, u32[]{:S(2)}) collective-permute-start(bf16[16,16,256]{2,1,0:T(8,128)(2,1)S(1)} %constant_dynamic-update-slice_fusion.w0), channel_id=1, source_target_pairs={{0,96},{16,112},{32,0},{48,16},{64,32},{80,48},{96,64},{112,80},{1... | collective-permute-start | bytes 393224 | tf_op jit(solution)/shard_map/ppermute | solution.py:243
  46.8 11.6 %collective-permute-start.5 = (bf16[24,16,256]{2,1,0:T(8,128)(2,1)S(1)}, bf16[24,16,256]{2,1,0:T(8,128)(2,1)S(1)}, u32[]{:S(2)}, u32[]{:S(2)}) collective-permute-start(bf16[24,16,256]{2,1,0:T(8,128)(2,1)S(1)} %select.13.w0), channel_id=1, source_target_pairs={{0,1},{1,2},{2,3},{3,0},{4,5},{5,6},{6,7},{7,4},{8,9},{9,10},{10,1... | collective-permute-start | bytes 589832 | tf_op jit(solution)/shard_map/ppermute | solution.py:251
  47.5 11.0 %collective-permute-start.6 = (bf16[24,16,256]{2,1,0:T(8,128)(2,1)S(1)}, bf16[24,16,256]{2,1,0:T(8,128)(2,1)S(1)}, u32[]{:S(2)}, u32[]{:S(2)}) collective-permute-start(bf16[24,16,256]{2,1,0:T(8,128)(2,1)S(1)} %select.13.w0), channel_id=1, source_target_pairs={{0,2},{1,3},{2,0},{3,1},{4,6},{5,7},{6,4},{7,5},{8,10},{9,11},{10,... | collective-permute-start | bytes 589832 | tf_op jit(solution)/shard_map/ppermute | solution.py:251
  49.2 9.8 %collective-permute-start.7 = (bf16[24,16,256]{2,1,0:T(8,128)(2,1)S(1)}, bf16[24,16,256]{2,1,0:T(8,128)(2,1)S(1)}, u32[]{:S(2)}, u32[]{:S(2)}) collective-permute-start(bf16[24,16,256]{2,1,0:T(8,128)(2,1)S(1)} %select.13.w0), channel_id=1, source_target_pairs={{0,3},{1,0},{2,1},{3,2},{4,7},{5,4},{6,5},{7,6},{8,11},{9,8},{10,9... | collective-permute-start | bytes 589832 | tf_op jit(solution)/shard_map/ppermute | solution.py:251
  50.7 8.4 %copy-start.1 = (bf16[8,256,256]{2,1,0:T(8,128)(2,1)S(1)}, bf16[8,256,256]{2,1,0:T(8,128)(2,1)}, u32[]{:S(2)}) copy-start(bf16[8,256,256]{2,1,0:T(8,128)(2,1)} %right.1) | copy-start | bytes 3145732
  65.1 6.1 %collective-permute-start.10 = (f32[8,16,256]{2,1,0:T(8,128)S(1)}, f32[8,16,256]{2,1,0:T(8,128)S(1)}, u32[]{:S(2)}, u32[]{:S(2)}) collective-permute-start(f32[8,16,256]{2,1,0:T(8,128)S(1)} %get-tuple-element.20), channel_id=1, source_target_pairs={{0,12},{1,13},{2,14},{3,15},{4,0},{5,1},{6,2},{7,3},{8,4},{9,5},{1... | collective-permute-start | bytes 393224 | tf_op jit(solution)/shard_map/ppermute | solution.py:260
  66.1 8.3 %collective-permute-start.8 = (f32[8,16,256]{2,1,0:T(8,128)S(1)}, f32[8,16,256]{2,1,0:T(8,128)S(1)}, u32[]{:S(2)}, u32[]{:S(2)}) collective-permute-start(f32[8,16,256]{2,1,0:T(8,128)S(1)} %get-tuple-element.18), channel_id=1, source_target_pairs={{0,4},{1,5},{2,6},{3,7},{4,8},{5,9},{6,10},{7,11},{8,12},{9,13},{1... | collective-permute-start | bytes 393224 | tf_op jit(solution)/shard_map/ppermute | solution.py:260
  67.2 7.1 %collective-permute-start.9 = (f32[8,16,256]{2,1,0:T(8,128)S(1)}, f32[8,16,256]{2,1,0:T(8,128)S(1)}, u32[]{:S(2)}, u32[]{:S(2)}) collective-permute-start(f32[8,16,256]{2,1,0:T(8,128)S(1)} %get-tuple-element.19), channel_id=1, source_target_pairs={{0,8},{1,9},{2,10},{3,11},{4,12},{5,13},{6,14},{7,15},{8,0},{9,1},... | collective-permute-start | bytes 393224 | tf_op jit(solution)/shard_map/ppermute | solution.py:260

commit v2 on v1

--- a/solution.py
+++ b/solution.py
@@ -20,7 +20,9 @@
 SHARE = ROWS * 128
 SENT = SHARE + PAIRS
 DEPTH = PICKS * HALF
+PITCH = PAIRS + 8
 MIB = 1 << 20
+WEIGH_COST = 100_000_000_000
 
 
 def swap_halves(value):
@@ -113,100 +115,88 @@
 
 
 def weigh_kernel(c_ref, t_ref, hi_ref, lo_ref, sums):
-    counts = c_ref[...]
+    counts = c_ref[:, SHARE:SENT]
     for n in range(ROWS // 2):
         part = lax.dot_general(
             counts, t_ref[:, n * 256 : n * 256 + 256], (((0,), (0,)), ((), ())), preferred_element_type=F32
         )
-        sums[2 * n * PAIRS : (2 * n + 1) * PAIRS, :] = part[:, :128]
-        sums[(2 * n + 1) * PAIRS : (2 * n + 2) * PAIRS, :] = part[:, 128:]
+        for k in range(2):
+            start = (2 * n + k) * PITCH
+            sums[start : start + PAIRS, :] = part[:, k * 128 : k * 128 + 128]
     low = lax.broadcasted_iota(jnp.int32, (ROWS, 128), 1) < 64
 
     def one(s, carry):
         for k in range(PICKS // 2):
             row = s * PICKS + 2 * k
-            a = sums[pl.ds(row, ROWS, stride=PAIRS), :]
-            b = sums[pl.ds(row + 1, ROWS, stride=PAIRS), :]
+            a = sums[pl.ds(row, ROWS, stride=PITCH), :]
+            b = sums[pl.ds(row + 1, ROWS, stride=PITCH), :]
             for u, value in enumerate((jnp.where(low, a, swap_halves(b)), jnp.where(low, swap_halves(a), b))):
                 hi = value.astype(BF)
                 lo = (value - hi.astype(F32)).astype(BF)
-                hi_ref[s, u, :, k * 128 : k * 128 + 128] = hi
-                lo_ref[s, u, :, k * 128 : k * 128 + 128] = lo
+                place = pl.ds(pl.multiple_of((2 * s + u) * ROWS, ROWS), ROWS)
+                hi_ref[place, k * 128 : k * 128 + 128] = hi
+                lo_ref[place, k * 128 : k * 128 + 128] = lo
         return carry
 
-    lax.fori_loop(0, SLOTS, one, 0)
+    lax.fori_loop(0, SLOTS, one, 0, unroll=4)
 
 
 def weigh(counts, share):
-    shape = jax.ShapeDtypeStruct((SLOTS, 2, ROWS, DEPTH), BF)
-    tabs = TABS * SIDE * SIDE
+    shape = jax.ShapeDtypeStruct((SLOTS * 2 * ROWS, DEPTH), BF)
+    here = pl.BlockSpec(memory_space=pltpu.VMEM)
     return pl.pallas_call(
         weigh_kernel,
-        grid=(1,),
-        in_specs=[
-            pl.BlockSpec((tabs, PAIRS), lambda i: (0, 0)),
-            pl.BlockSpec((tabs, SHARE), lambda i: (0, 0)),
-        ],
-        out_specs=[pl.BlockSpec(shape.shape, lambda i: (0, 0, 0, 0))] * 2,
+        in_specs=[here, here],
+        out_specs=[here, here],
         out_shape=[shape, shape],
-        scratch_shapes=[pltpu.VMEM((ROWS * PAIRS, 128), F32)],
-        compiler_params=pltpu.CompilerParams(vmem_limit_bytes=32 * MIB),
+        scratch_shapes=[pltpu.VMEM((ROWS * PITCH, 128), F32)],
+        compiler_params=pltpu.CompilerParams(vmem_limit_bytes=24 * MIB),
+        cost_estimate=pl.CostEstimate(flops=WEIGH_COST, bytes_accessed=8 * MIB, transcendentals=0),
         name="weigh",
     )(counts, share)
 
 
-def apply_kernel(meta, oh, ol, xh, xl, w0, w1, w2, w3, right, s0, s1, s2, s3, wave, lhs_hi, lhs_lo, total):
+def apply_kernel(meta, oh, ol, xh, xl, w0, w1, w2, w3, right, s0, s1, s2, s3, wave, channel, total):
     core, x, y = meta[0], meta[1], meta[2]
-    o = pl.program_id(0)
-
-    @pl.when(o == 0)
-    def _():
-        for d, ref in enumerate((w0, w1, w2, w3)):
-            place = pl.multiple_of(lax.rem(x - d + SIDE, SIDE) * ROWS, ROWS)
-            wave[:, pl.ds(place, ROWS), :] = ref[...]
-
+    for d, ref in enumerate((w0, w1, w2, w3)):
+        place = pl.multiple_of(lax.rem(x - d + SIDE, SIDE) * ROWS, ROWS)
+        wave[:, pl.ds(place, ROWS), :] = ref[...]
     weights = wave[...].reshape(DEPTH, WIDTH)
-    mine = pl.multiple_of(core * ROWS, ROWS)
-    theirs = pl.multiple_of((1 - core) * ROWS, ROWS)
-    for half, hi_ref, lo_ref in ((mine, oh, ol), (theirs, xh, xl)):
-        lhs_hi[:, pl.ds(half, ROWS), :] = hi_ref[...].reshape(4, ROWS, DEPTH)
-        lhs_lo[:, pl.ds(half, ROWS), :] = lo_ref[...].reshape(4, ROWS, DEPTH)
-    channel = jnp.dot(lhs_hi[...].reshape(128, DEPTH), weights, preferred_element_type=F32)
-    channel = channel + jnp.dot(lhs_lo[...].reshape(128, DEPTH), weights, preferred_element_type=F32)
-    hi = channel.astype(BF)
-    lo = (channel - hi.astype(F32)).astype(BF)
-    result = jnp.zeros((HALF, WIDTH), F32)
-    for p in range(2):
-        env = right[meta[3 + 2 * o + p]]
-        rows = slice(p * HALF, (p + 1) * HALF)
-        result = result + jnp.dot(hi[rows], env, preferred_element_type=F32)
-        result = result + jnp.dot(lo[rows], env, preferred_element_type=F32)
-    total[...] = result
+    for half, (hi_ref, lo_ref) in enumerate(((oh, ol), (xh, xl))):
+        part = jnp.dot(hi_ref[...], weights, preferred_element_type=F32)
+        channel[half] = part + jnp.dot(lo_ref[...], weights, preferred_element_type=F32)
+    step = 2 * ROWS
+    for o in range(SLOTS // 2):
+        result = jnp.zeros((HALF, WIDTH), F32)
+        for s in (2 * o, 2 * o + 1):
+            env = right[meta[3 + s]]
+            value = jnp.concatenate([channel[half, s * step : (s + 1) * step] for half in range(2)], axis=0)
+            hi = value.astype(BF)
+            lo = (value - hi.astype(F32)).astype(BF)
+            part = jnp.dot(jnp.concatenate([hi, lo], axis=0), env, preferred_element_type=F32)
+            result = result + (part[:HALF] + part[HALF:])
+        for half in range(2):
+            for u in range(2):
+                owner = 2 * u + (core if half == 0 else 1 - core)
+                total[owner, o] = result[(2 * half + u) * ROWS : (2 * half + u + 1) * ROWS]
     for d, ref in enumerate((s0, s1, s2, s3)):
-        place = pl.multiple_of(lax.rem(y + d, SIDE) * ROWS, ROWS)
-        ref[0] = total[pl.ds(place, ROWS), :]
+        ref[...] = total[lax.rem(y + d, SIDE)]
 
 
 def apply(meta, own, far, pieces, right):
     sectors = SLOTS // 2
-    lhs_spec = pl.BlockSpec((2, 2, ROWS, DEPTH), lambda o, m: (o, 0, 0, 0))
-    whole = lambda a: pl.BlockSpec(a.shape, lambda o, m: (0, 0, 0))
+    here = pl.BlockSpec(memory_space=pltpu.VMEM)
     return pl.pallas_call(
         apply_kernel,
-        grid_spec=pltpu.PrefetchScalarGridSpec(
-            num_scalar_prefetch=1,
-            grid=(sectors,),
-            in_specs=[lhs_spec] * 4 + [whole(p) for p in pieces] + [whole(right)],
-            out_specs=[pl.BlockSpec((1, ROWS, WIDTH), lambda o, m: (o, 0, 0))] * 4,
-            scratch_shapes=[
-                pltpu.VMEM((PICKS, HALF, WIDTH), BF),
-                pltpu.VMEM((4, 2 * ROWS, DEPTH), BF),
-                pltpu.VMEM((4, 2 * ROWS, DEPTH), BF),
-                pltpu.VMEM((HALF, WIDTH), F32),
-            ],
-        ),
+        in_specs=[pl.BlockSpec(memory_space=pltpu.SMEM)] + [here] * 9,
+        out_specs=[here] * 4,
         out_shape=[jax.ShapeDtypeStruct((sectors, ROWS, WIDTH), F32)] * 4,
-        compiler_params=pltpu.CompilerParams(vmem_limit_bytes=32 * MIB),
+        scratch_shapes=[
+            pltpu.VMEM((PICKS, HALF, WIDTH), BF),
+            pltpu.VMEM((2, SLOTS * 2 * ROWS, WIDTH), F32),
+            pltpu.VMEM((SIDE, sectors, ROWS, WIDTH), F32),
+        ],
+        compiler_params=pltpu.CompilerParams(vmem_limit_bytes=24 * MIB),
         name="apply",
     )(meta, *own, *far, *pieces, right)
 
@@ -240,19 +230,18 @@
 
     other = lax.ppermute(wave_blocks, "sector", along_sector(0, 1))
     both = jnp.concatenate([wave_blocks, other], axis=0)
-    pool = [both] + [lax.ppermute(both, "sector", along_sector(d, 0)) for d in (1, 2, 3)]
-
     terms = jnp.stack([term_slot * PICKS + term_pick, term_table, term_live])
     sent = pack(core.reshape(1), recoupling, terms)
+    sent, both = lax.optimization_barrier((sent, both))
     mine = lax.all_to_all(sent, "table", 0, 0).reshape(TABS * SIDE * SIDE, SENT)
     theirs = lax.ppermute(mine, "sector", along_sector(0, 1))
 
+    pool = [both] + [lax.ppermute(both, "sector", along_sector(d, 0)) for d in (1, 2, 3)]
     chosen = select(jnp.concatenate([jnp.stack([z, core]), fetch_list.reshape(-1)]), pool)
     pieces = [chosen] + [lax.ppermute(chosen, "table", along_table(0, d)) for d in (1, 2, 3)]
 
-    counts = mine[:, SHARE:]
-    own = weigh(counts, mine)
-    far = weigh(counts, theirs)
+    own = weigh(mine, mine)
+    far = weigh(mine, theirs)
     meta = jnp.concatenate([jnp.stack([core, x, y]), channel_env.reshape(-1)])
     parts = apply(meta, own, far, pieces, right_blocks)
     result = parts[0]

time: 76 us -> 56.6 us (0.74)
  blocking collectives: 26.3 us -> 0 us
  starting transfers between devices: 13.7 us -> 24.1 us
  Pallas kernels: 15.8 us -> 11.2 us
  other arithmetic: 2.45 us -> 3.54 us
    all_to_all x1 -> x0, blocking collectives: 26.3 us -> none  [local(): mine = lax.all_to_all(sent, 'table', 0, 0).reshape(TABS * SIDE * SIDE, SENT)]
    all_to_all x0 -> x1, starting transfers between devices: none -> 7.13 us  [local(): mine = lax.all_to_all(sent, 'table', 0, 0).reshape(TABS * SIDE * SIDE, SENT)]
    pallas_call x3, Pallas kernels: 13.2 us -> 6.84 us  [the longest x2 3.45 us: weigh(): pl.pallas_call(weigh_kernel, in_specs=[here, here], out_specs=[here, here...]
    ppermute x1, waiting for transfers between devices: 2.33 us -> 0.01 us  [local(): other = lax.ppermute(wave_blocks, 'sector', along_sector(0, 1))]
    ppermute x3, starting transfers between devices: 3.77 us -> 5.77 us  [local(): lax.ppermute(chosen, 'table', along_table(0, d))]
    ppermute x3, starting transfers between devices: 2.94 us -> 4.65 us  [local(): result = result + lax.ppermute(parts[d], 'table', along_table(d, 0))]
    all_to_all x0 -> x1, waiting for transfers between devices: none -> 1.34 us  [local(): mine = lax.all_to_all(sent, 'table', 0, 0).reshape(TABS * SIDE * SIDE, SENT)]
    ppermute x1, waiting for transfers between devices: 0.01 us -> 1.19 us  [local(): theirs = lax.ppermute(mine, 'sector', along_sector(0, 1))]
  transfers between devices with their start and end apart: 11 -> 12, of which waited for: 7 -> 7; matrix products, arithmetic and copies ran while one was open for 1% -> 6% of each run, Pallas kernels for 11% -> 14%
where the time goes in v2:
time: 56.6 us; the launch traced here: 56 us
  starting transfers between devices  24.1 us (43%)
  waiting for transfers between devices  15.2 us (27%)
  Pallas kernels  11.2 us (20%)
  other arithmetic  3.54 us (6%)
  local copies, waits for them, and re-layouts  1.95 us (3%)
    all_to_all x1, starting transfers between devices, local(): mine = lax.all_to_all(sent, 'table', 0, 0).reshape(TABS * SIDE * SIDE, SENT)  7.13 us
    ppermute x3, starting transfers between devices, local(): lax.ppermute(both, 'sector', along_sector(d, 0))  6.51 us
    ppermute x3, starting transfers between devices, local(): lax.ppermute(chosen, 'table', along_table(0, d))  5.77 us
    ppermute x3, waiting for transfers between devices, local(): result = result + lax.ppermute(parts[d], 'table', along_table(d, 0))  5.17 us
    ppermute x3, waiting for transfers between devices, local(): lax.ppermute(both, 'sector', along_sector(d, 0))  5.08 us
    ppermute x3, starting transfers between devices, local(): result = result + lax.ppermute(parts[d], 'table', along_table(d, 0))  4.65 us
    pallas_call x2, Pallas kernels, weigh(): pl.pallas_call(weigh_kernel, in_specs=[here, here], out_specs=[here, here...  3.45 us
    pallas_call x1, Pallas kernels, apply(): pl.pallas_call(apply_kernel, in_specs=[pl.BlockSpec(memory_space=pltpu.SM...  3.39 us
  transfers between devices with their start and end apart: 12, of which 7 were waited for; matrix products, arithmetic and copies ran while one was open for 6% of the time, Pallas kernels for 14%

profile of v2, /device:TPU:0, one launch (start us, length us, event | category | flops | bytes accessed | tf_op | source)
XLA Modules:
  0.0 56.0 jit_solution(4583566721118913833)
XLA Ops:
  0.0 0.0 collective-permute-start
  0.0 0.7 %multiply_add_fusion = s32[192]{0:T(256)S(1)} fusion(s32[192]{0:T(256)} %param.16, s32[192]{0:T(256)} %param.18), kind=kLoop, calls=%fused_computation.5 | loop fusion | flops 384 | bytes 2304 | tf_op jit(solution)/shard_map/add | solution.py:233
  0.7 0.7 %pad_add_fusion.terms_ref = s32[3,192]{1,0:T(4,128)S(1)} fusion(s32[1,192]{1,0:T(1,128)} %bitcast.17, s32[1,192]{1,0:T(1,128)} %bitcast.18, s32[1,192]{1,0:T(1,128)S(1)} %bitcast.16), kind=kLoop, calls=%fused_computation.3 | loop fusion | flops 1152 | bytes 4608 | tf_op jit(solution)/shard_map/stack | solution.py:233
  1.4 1.6 %copy-done = bf16[16,256,256]{2,1,0:T(8,128)(2,1)S(1)} copy-done((bf16[16,256,256]{2,1,0:T(8,128)(2,1)S(1)}, bf16[16,256,256]{2,1,0:T(8,128)(2,1)}, u32[]{:S(2)}) %copy-start) | copy-done | bytes 2097176
  3.0 2.7 %pack.1 = bf16[4,4,16,2432]{3,2,1,0:T(8,128)(2,1)} custom-call(s32[1]{0:T(128)} %bitcast.meta, bf16[16,4,64,256]{3,2,1,0:T(8,128)(2,1)S(1)} %bitcast.10, bf16[16,4,64,256]{3,2,1,0:T(8,128)(2,1)S(1)} %bitcast.11, s32[3,192]{1,0:T(4,128)S(1)} %pad_add_fusion.terms_ref), custom_call_target="tpu_custom_call" | custom-call | tf_op jit(solution)/shard_map/pack/pallas_call | solution.py:67
  5.7 0.0 collective-permute-done
  5.7 0.0 copy-done.2
  5.7 7.1 %all-to-all-start = ((bf16[16,16,2432]{2,1,0:T(8,128)(2,1)}), bf16[16,16,2432]{2,1,0:T(8,128)(2,1)S(1)}, u32[]{:S(2)}, u32[]{:S(2)}) async-start(bf16[16,16,2432]{2,1,0:T(8,128)(2,1)} %bitcast.7), calls=%async_computation | async-start | bytes 2490368 | tf_op jit(solution)/shard_map/all_to_all | solution.py:236
  12.9 0.1 copy.14
  13.0 0.1 reshape.77
  13.1 0.5 iota_add_fusion
  13.6 0.0 copy-done.4
  13.6 0.6 %iota_compare_fusion = pred[8,256]{1,0:T(8,128)(4,1)} fusion(s32[8]{0:T(128)S(1)} %copy-done.4), kind=kLoop, calls=%fused_computation.2 | loop fusion | flops 2048 | bytes 2080 | tf_op jit(solution)/shard_map/lt | solution.py:254
  14.2 1.9 %collective-permute-start.2 = (bf16[16,16,256]{2,1,0:T(8,128)(2,1)S(1)}, bf16[16,16,256]{2,1,0:T(8,128)(2,1)S(1)}, u32[]{:S(2)}, u32[]{:S(2)}) collective-permute-start(bf16[16,16,256]{2,1,0:T(8,128)(2,1)S(1)} %pad_maximum_fusion.w0), channel_id=1, source_target_pairs={{0,32},{16,48},{32,64},{48,80},{64,96},{80,112},{96,0},{112,16},{1... | collective-permute-start | bytes 393224 | tf_op jit(solution)/shard_map/ppermute | solution.py:239
  16.1 3.6 %collective-permute-start.3 = (bf16[16,16,256]{2,1,0:T(8,128)(2,1)S(1)}, bf16[16,16,256]{2,1,0:T(8,128)(2,1)S(1)}, u32[]{:S(2)}, u32[]{:S(2)}) collective-permute-start(bf16[16,16,256]{2,1,0:T(8,128)(2,1)S(1)} %pad_maximum_fusion.w0), channel_id=1, source_target_pairs={{0,64},{16,80},{32,96},{48,112},{64,0},{80,16},{96,32},{112,48},{1... | collective-permute-start | bytes 393224 | tf_op jit(solution)/shard_map/ppermute | solution.py:239
  19.7 1.0 %collective-permute-start.4 = (bf16[16,16,256]{2,1,0:T(8,128)(2,1)S(1)}, bf16[16,16,256]{2,1,0:T(8,128)(2,1)S(1)}, u32[]{:S(2)}, u32[]{:S(2)}) collective-permute-start(bf16[16,16,256]{2,1,0:T(8,128)(2,1)S(1)} %pad_maximum_fusion.w0), channel_id=1, source_target_pairs={{0,96},{16,112},{32,0},{48,16},{64,32},{80,48},{96,64},{112,80},{1... | collective-permute-start | bytes 393224 | tf_op jit(solution)/shard_map/ppermute | solution.py:239
  20.7 0.1 pad_add_fusion.2.meta
  20.8 0.0 copy-done.7
  20.8 0.1 copy.13
  20.9 0.1 reshape.73
  21.0 0.1 pad_add_fusion.1.meta
  21.0 1.1 %collective-permute-done.2.w1 = bf16[16,16,256]{2,1,0:T(8,128)(2,1)S(1)} collective-permute-done((bf16[16,16,256]{2,1,0:T(8,128)(2,1)S(1)}, bf16[16,16,256]{2,1,0:T(8,128)(2,1)S(1)}, u32[]{:S(2)}, u32[]{:S(2)}) %collective-permute-start.2) | collective-permute-done | bytes 131104 | tf_op jit(solution)/shard_map/ppermute | solution.py:239
  22.1 4.0 %collective-permute-done.3.w2 = bf16[16,16,256]{2,1,0:T(8,128)(2,1)S(1)} collective-permute-done((bf16[16,16,256]{2,1,0:T(8,128)(2,1)S(1)}, bf16[16,16,256]{2,1,0:T(8,128)(2,1)S(1)}, u32[]{:S(2)}, u32[]{:S(2)}) %collective-permute-start.3) | collective-permute-done | bytes 131104 | tf_op jit(solution)/shard_map/ppermute | solution.py:239
  26.1 0.0 collective-permute-done.4.w3
  26.1 1.6 %select.13.w0 = bf16[24,16,256]{2,1,0:T(8,128)(2,1)} custom-call(s32[26]{0:T(128)S(1)} %pad_add_fusion.2.meta, bf16[16,16,256]{2,1,0:T(8,128)(2,1)S(1)} %pad_maximum_fusion.w0, bf16[16,16,256]{2,1,0:T(8,128)(2,1)S(1)} %collective-permute-done.2.w1, bf16[16,16,256]{2,1,0:T(8,128)(2,1)S(1)} %collective-permute-done.3.w2, ...), custom_call_target="tpu_custom_call" | custom-call | tf_op jit(solution)/shard_map/select/pallas_call | solution.py:107
  27.8 1.6 %collective-permute-start.5 = (bf16[24,16,256]{2,1,0:T(8,128)(2,1)}, bf16[24,16,256]{2,1,0:T(8,128)(2,1)}, u32[]{:S(2)}, u32[]{:S(2)}) collective-permute-start(bf16[24,16,256]{2,1,0:T(8,128)(2,1)} %select.13.w0), channel_id=1, source_target_pairs={{0,1},{1,2},{2,3},{3,0},{4,5},{5,6},{6,7},{7,4},{8,9},{9,10},{10,1... | collective-permute-start | bytes 589832 | tf_op jit(solution)/shard_map/ppermute | solution.py:241
  29.4 2.7 %collective-permute-start.6 = (bf16[24,16,256]{2,1,0:T(8,128)(2,1)}, bf16[24,16,256]{2,1,0:T(8,128)(2,1)}, u32[]{:S(2)}, u32[]{:S(2)}) collective-permute-start(bf16[24,16,256]{2,1,0:T(8,128)(2,1)} %select.13.w0), channel_id=1, source_target_pairs={{0,2},{1,3},{2,0},{3,1},{4,6},{5,7},{6,4},{7,5},{8,10},{9,11},{10,... | collective-permute-start | bytes 589832 | tf_op jit(solution)/shard_map/ppermute | solution.py:241
  32.1 1.5 %collective-permute-start.7 = (bf16[24,16,256]{2,1,0:T(8,128)(2,1)}, bf16[24,16,256]{2,1,0:T(8,128)(2,1)}, u32[]{:S(2)}, u32[]{:S(2)}) collective-permute-start(bf16[24,16,256]{2,1,0:T(8,128)(2,1)} %select.13.w0), channel_id=1, source_target_pairs={{0,3},{1,0},{2,1},{3,2},{4,7},{5,4},{6,5},{7,6},{8,11},{9,8},{10,9... | collective-permute-start | bytes 589832 | tf_op jit(solution)/shard_map/ppermute | solution.py:241
  33.5 1.3 %all-to-all-done = bf16[16,16,2432]{2,1,0:T(8,128)(2,1)S(1)} async-done(((bf16[16,16,2432]{2,1,0:T(8,128)(2,1)}), bf16[16,16,2432]{2,1,0:T(8,128)(2,1)S(1)}, u32[]{:S(2)}, u32[]{:S(2)}) %all-to-all-start) | async-done | bytes 1245216 | tf_op jit(solution)/shard_map/all_to_all | solution.py:236
  34.9 0.0 collective-permute-start.1
  34.9 1.7 %weigh.2 = (bf16[512,1536]{1,0:T(8,128)(2,1)S(1)}, bf16[512,1536]{1,0:T(8,128)(2,1)S(1)}) custom-call(bf16[256,2432]{1,0:T(8,128)(2,1)S(1)} %bitcast.13, bf16[256,2432]{1,0:T(8,128)(2,1)S(1)} %bitcast.14), custom_call_target="tpu_custom_call" | custom-call | flops 99999997952 | bytes 8388608 | tf_op jit(solution)/shard_map/weigh/pallas_call | solution.py:147
  36.6 0.0 copy-start.1
  36.6 1.2 %collective-permute-done.1.t_ref = bf16[256,2432]{1,0:T(8,128)(2,1)S(1)} collective-permute-done((bf16[256,2432]{1,0:T(8,128)(2,1)S(1)}, bf16[256,2432]{1,0:T(8,128)(2,1)S(1)}, u32[]{:S(2)}, u32[]{:S(2)}) %collective-permute-start.1) | collective-permute-done | bytes 1245216 | tf_op jit(solution)/shard_map/ppermute | solution.py:237
  37.8 1.7 %weigh.3 = (bf16[512,1536]{1,0:T(8,128)(2,1)S(1)}, bf16[512,1536]{1,0:T(8,128)(2,1)S(1)}) custom-call(bf16[256,2432]{1,0:T(8,128)(2,1)S(1)} %bitcast.15, bf16[256,2432]{1,0:T(8,128)(2,1)S(1)} %collective-permute-done.1.t_ref), custom_call_target="tpu_custom_call" | custom-call | flops 99999997952 | bytes 8388608 | tf_op jit(solution)/shard_map/weigh/pallas_call | solution.py:147
  39.5 0.0 collective-permute-done.5.w1
  39.6 2.4 %collective-permute-done.6.w2 = bf16[24,16,256]{2,1,0:T(8,128)(2,1)} collective-permute-done((bf16[24,16,256]{2,1,0:T(8,128)(2,1)}, bf16[24,16,256]{2,1,0:T(8,128)(2,1)}, u32[]{:S(2)}, u32[]{:S(2)}) %collective-permute-start.6) | collective-permute-done | bytes 196640 | tf_op jit(solution)/shard_map/ppermute | solution.py:241
  41.9 0.0 collective-permute-done.7.w3
  42.0 0.0 copy-start.3
  42.0 3.4 %apply.1 = (f32[8,16,256]{2,1,0:T(8,128)S(1)}, f32[8,16,256]{2,1,0:T(8,128)S(1)}, f32[8,16,256]{2,1,0:T(8,128)S(1)}, f32[8,16,256]{2,1,0:T(8,128)S(1)}) custom-call(s32[19]{0:T(128)S(1)} %pad_add_fusion.1.meta, bf16[512,1536]{1,0:T(8,128)(2,1)S(1)} %get-tuple-element.16.oh, bf16[512,1536]{1,0:T(8,128)(2,1)S(1)} %get-tuple-element.17.ol, ...), custom_call_target="tpu_custom_call" | custom-call | tf_op jit(solution)/shard_map/apply/pallas_call | solution.py:189
  45.4 1.7 %collective-permute-start.10 = (f32[8,16,256]{2,1,0:T(8,128)S(1)}, f32[8,16,256]{2,1,0:T(8,128)S(1)}, u32[]{:S(2)}, u32[]{:S(2)}) collective-permute-start(f32[8,16,256]{2,1,0:T(8,128)S(1)} %get-tuple-element.24), channel_id=1, source_target_pairs={{0,12},{1,13},{2,14},{3,15},{4,0},{5,1},{6,2},{7,3},{8,4},{9,5},{1... | collective-permute-start | bytes 393224 | tf_op jit(solution)/shard_map/ppermute | solution.py:249
  47.1 0.4 collective-permute-start.8
  47.5 2.6 %collective-permute-start.9 = (f32[8,16,256]{2,1,0:T(8,128)S(1)}, f32[8,16,256]{2,1,0:T(8,128)S(1)}, u32[]{:S(2)}, u32[]{:S(2)}) collective-permute-start(f32[8,16,256]{2,1,0:T(8,128)S(1)} %get-tuple-element.23), channel_id=1, source_target_pairs={{0,8},{1,9},{2,10},{3,11},{4,12},{5,13},{6,14},{7,15},{8,0},{9,1},... | collective-permute-start | bytes 393224 | tf_op jit(solution)/shard_map/ppermute | solution.py:249
  50.0 0.1 broadcast_compare_fusion
  50.1 0.9 %collective-permute-done.10 = f32[8,16,256]{2,1,0:T(8,128)S(1)} collective-permute-done((f32[8,16,256]{2,1,0:T(8,128)S(1)}, f32[8,16,256]{2,1,0:T(8,128)S(1)}, u32[]{:S(2)}, u32[]{:S(2)}) %collective-permute-start.10) | collective-permute-done | bytes 131104 | tf_op jit(solution)/shard_map/ppermute | solution.py:249
  51.0 4.2 %collective-permute-done.8 = f32[8,16,256]{2,1,0:T(8,128)S(1)} collective-permute-done((f32[8,16,256]{2,1,0:T(8,128)S(1)}, f32[8,16,256]{2,1,0:T(8,128)S(1)}, u32[]{:S(2)}, u32[]{:S(2)}) %collective-permute-start.8) | collective-permute-done | bytes 131104 | tf_op jit(solution)/shard_map/ppermute | solution.py:249
  55.3 0.0 collective-permute-done.9
  55.3 0.0 copy-done.3
  55.3 0.7 %add_select_fusion = f32[8,16,256]{2,1,0:T(8,128)} fusion(f32[8,16,256]{2,1,0:T(8,128)S(1)} %collective-permute-done.10, f32[8,16,256]{2,1,0:T(8,128)S(1)} %collective-permute-done.9, f32[8,16,256]{2,1,0:T(8,128)S(1)} %get-tuple-element.21, f32[8,16,256]{2,1,0:T(8,128)S(1)} %collective-permute-done.8, pred[8,256]{1,0:T(8,128)(4,1)S(1)} %copy-done.3, ...), kind=kLoop, calls=%fused_computation.1 | loop fusion | flops 163840 | bytes 657536 | tf_op jit(solution)/shard_map/jit(_where)/select_n | solution.py:255
  (12 shorter events, 0.0 us)
Async XLA Ops:
  0.0 5.7 %collective-permute-start = (bf16[8,16,256]{2,1,0:T(8,128)(2,1)}, bf16[8,16,256]{2,1,0:T(8,128)(2,1)S(1)}, u32[]{:S(2)}, u32[]{:S(2)}) collective-permute-start(bf16[8,16,256]{2,1,0:T(8,128)(2,1)} %param.10), channel_id=1, source_target_pairs={{0,16},{16,0},{32,48},{48,32},{64,80},{80,64},{96,112},{112,96},{1... | collective-permute-start | bytes 196616 | tf_op jit(solution)/shard_map/ppermute | solution.py:231
  1.4 1.6 %copy-start = (bf16[16,256,256]{2,1,0:T(8,128)(2,1)S(1)}, bf16[16,256,256]{2,1,0:T(8,128)(2,1)}, u32[]{:S(2)}) copy-start(bf16[16,256,256]{2,1,0:T(8,128)(2,1)} %param.11) | copy-start | bytes 6291460
  3.0 2.7 %copy-start.2 = (bf16[8,16,256]{2,1,0:T(8,128)(2,1)S(1)}, bf16[8,16,256]{2,1,0:T(8,128)(2,1)}, u32[]{:S(2)}) copy-start(bf16[8,16,256]{2,1,0:T(8,128)(2,1)} %param.10) | copy-start | bytes 196612
  5.7 7.2 %copy-start.6 = (s32[1,8,3]{1,0,2:T(1,128)S(1)}, s32[1,8,3]{1,0,2:T(1,128)}, u32[]{:S(2)}) copy-start(s32[1,8,3]{1,0,2:T(1,128)} %param.15) | copy-start | bytes 292
  5.7 7.9 %copy-start.4 = (s32[8]{0:T(128)S(1)}, s32[8]{0:T(128)}, u32[]{:S(2)}) copy-start(s32[8]{0:T(128)} %param.13) | copy-start | bytes 100
  5.7 15.1 %copy-start.7 = (s32[8,2]{0,1:T(2,128)S(1)}, s32[8,2]{0,1:T(2,128)}, u32[]{:S(2)}) copy-start(s32[8,2]{0,1:T(2,128)} %param.14) | copy-start | bytes 196
  5.7 29.1 %all-to-all-start = ((bf16[16,16,2432]{2,1,0:T(8,128)(2,1)}), bf16[16,16,2432]{2,1,0:T(8,128)(2,1)S(1)}, u32[]{:S(2)}, u32[]{:S(2)}) async-start(bf16[16,16,2432]{2,1,0:T(8,128)(2,1)} %bitcast.7), calls=%async_computation | async-start | bytes 2490368 | tf_op jit(solution)/shard_map/all_to_all | solution.py:236
  14.2 7.9 %collective-permute-start.2 = (bf16[16,16,256]{2,1,0:T(8,128)(2,1)S(1)}, bf16[16,16,256]{2,1,0:T(8,128)(2,1)S(1)}, u32[]{:S(2)}, u32[]{:S(2)}) collective-permute-start(bf16[16,16,256]{2,1,0:T(8,128)(2,1)S(1)} %pad_maximum_fusion.w0), channel_id=1, source_target_pairs={{0,32},{16,48},{32,64},{48,80},{64,96},{80,112},{96,0},{112,16},{1... | collective-permute-start | bytes 393224 | tf_op jit(solution)/shard_map/ppermute | solution.py:239
  16.1 10.0 %collective-permute-start.3 = (bf16[16,16,256]{2,1,0:T(8,128)(2,1)S(1)}, bf16[16,16,256]{2,1,0:T(8,128)(2,1)S(1)}, u32[]{:S(2)}, u32[]{:S(2)}) collective-permute-start(bf16[16,16,256]{2,1,0:T(8,128)(2,1)S(1)} %pad_maximum_fusion.w0), channel_id=1, source_target_pairs={{0,64},{16,80},{32,96},{48,112},{64,0},{80,16},{96,32},{112,48},{1... | collective-permute-start | bytes 393224 | tf_op jit(solution)/shard_map/ppermute | solution.py:239
  19.7 6.4 %collective-permute-start.4 = (bf16[16,16,256]{2,1,0:T(8,128)(2,1)S(1)}, bf16[16,16,256]{2,1,0:T(8,128)(2,1)S(1)}, u32[]{:S(2)}, u32[]{:S(2)}) collective-permute-start(bf16[16,16,256]{2,1,0:T(8,128)(2,1)S(1)} %pad_maximum_fusion.w0), channel_id=1, source_target_pairs={{0,96},{16,112},{32,0},{48,16},{64,32},{80,48},{96,64},{112,80},{1... | collective-permute-start | bytes 393224 | tf_op jit(solution)/shard_map/ppermute | solution.py:239
  27.8 11.8 %collective-permute-start.5 = (bf16[24,16,256]{2,1,0:T(8,128)(2,1)}, bf16[24,16,256]{2,1,0:T(8,128)(2,1)}, u32[]{:S(2)}, u32[]{:S(2)}) collective-permute-start(bf16[24,16,256]{2,1,0:T(8,128)(2,1)} %select.13.w0), channel_id=1, source_target_pairs={{0,1},{1,2},{2,3},{3,0},{4,5},{5,6},{6,7},{7,4},{8,9},{9,10},{10,1... | collective-permute-start | bytes 589832 | tf_op jit(solution)/shard_map/ppermute | solution.py:241
  29.4 12.5 %collective-permute-start.6 = (bf16[24,16,256]{2,1,0:T(8,128)(2,1)}, bf16[24,16,256]{2,1,0:T(8,128)(2,1)}, u32[]{:S(2)}, u32[]{:S(2)}) collective-permute-start(bf16[24,16,256]{2,1,0:T(8,128)(2,1)} %select.13.w0), channel_id=1, source_target_pairs={{0,2},{1,3},{2,0},{3,1},{4,6},{5,7},{6,4},{7,5},{8,10},{9,11},{10,... | collective-permute-start | bytes 589832 | tf_op jit(solution)/shard_map/ppermute | solution.py:241
  32.1 9.9 %collective-permute-start.7 = (bf16[24,16,256]{2,1,0:T(8,128)(2,1)}, bf16[24,16,256]{2,1,0:T(8,128)(2,1)}, u32[]{:S(2)}, u32[]{:S(2)}) collective-permute-start(bf16[24,16,256]{2,1,0:T(8,128)(2,1)} %select.13.w0), channel_id=1, source_target_pairs={{0,3},{1,0},{2,1},{3,2},{4,7},{5,4},{6,5},{7,6},{8,11},{9,8},{10,9... | collective-permute-start | bytes 589832 | tf_op jit(solution)/shard_map/ppermute | solution.py:241
  34.9 2.9 %collective-permute-start.1 = (bf16[256,2432]{1,0:T(8,128)(2,1)S(1)}, bf16[256,2432]{1,0:T(8,128)(2,1)S(1)}, u32[]{:S(2)}, u32[]{:S(2)}) collective-permute-start(bf16[256,2432]{1,0:T(8,128)(2,1)S(1)} %bitcast.12), channel_id=1, source_target_pairs={{0,16},{16,0},{32,48},{48,32},{64,80},{80,64},{96,112},{112,96},{1... | collective-permute-start | bytes 3735560 | tf_op jit(solution)/shard_map/ppermute | solution.py:237
  36.6 5.3 %copy-start.1 = (bf16[8,256,256]{2,1,0:T(8,128)(2,1)S(1)}, bf16[8,256,256]{2,1,0:T(8,128)(2,1)}, u32[]{:S(2)}) copy-start(bf16[8,256,256]{2,1,0:T(8,128)(2,1)} %right.1) | copy-start | bytes 3145732
  41.9 8.1 %copy-start.5 = (s32[8]{0:T(128)S(1)}, s32[8]{0:T(128)}, u32[]{:S(2)}) copy-start(s32[8]{0:T(128)} %param.13) | copy-start | bytes 100
  41.9 8.1 %copy-start.8 = (s32[16]{0:T(128)S(1)}, s32[16]{0:T(128)}, u32[]{:S(2)}) copy-start(s32[16]{0:T(128)} %iota_add_fusion) | copy-start | bytes 196
  42.0 13.3 %copy-start.3 = (pred[8,256]{1,0:T(8,128)(4,1)S(1)}, pred[8,256]{1,0:T(8,128)(4,1)}, u32[]{:S(2)}) copy-start(pred[8,256]{1,0:T(8,128)(4,1)} %iota_compare_fusion) | copy-start | bytes 6148
  45.4 5.7 %collective-permute-start.10 = (f32[8,16,256]{2,1,0:T(8,128)S(1)}, f32[8,16,256]{2,1,0:T(8,128)S(1)}, u32[]{:S(2)}, u32[]{:S(2)}) collective-permute-start(f32[8,16,256]{2,1,0:T(8,128)S(1)} %get-tuple-element.24), channel_id=1, source_target_pairs={{0,12},{1,13},{2,14},{3,15},{4,0},{5,1},{6,2},{7,3},{8,4},{9,5},{1... | collective-permute-start | bytes 393224 | tf_op jit(solution)/shard_map/ppermute | solution.py:249
  47.1 8.2 %collective-permute-start.8 = (f32[8,16,256]{2,1,0:T(8,128)S(1)}, f32[8,16,256]{2,1,0:T(8,128)S(1)}, u32[]{:S(2)}, u32[]{:S(2)}) collective-permute-start(f32[8,16,256]{2,1,0:T(8,128)S(1)} %get-tuple-element.22), channel_id=1, source_target_pairs={{0,4},{1,5},{2,6},{3,7},{4,8},{5,9},{6,10},{7,11},{8,12},{9,13},{1... | collective-permute-start | bytes 393224 | tf_op jit(solution)/shard_map/ppermute | solution.py:249
  47.5 7.8 %collective-permute-start.9 = (f32[8,16,256]{2,1,0:T(8,128)S(1)}, f32[8,16,256]{2,1,0:T(8,128)S(1)}, u32[]{:S(2)}, u32[]{:S(2)}) collective-permute-start(f32[8,16,256]{2,1,0:T(8,128)S(1)} %get-tuple-element.23), channel_id=1, source_target_pairs={{0,8},{1,9},{2,10},{3,11},{4,12},{5,13},{6,14},{7,15},{8,0},{9,1},... | collective-permute-start | bytes 393224 | tf_op jit(solution)/shard_map/ppermute | solution.py:249

commit v3 on v0

v3 whole, which is shorter than its diff:
```python
import functools

import jax
import jax.numpy as jnp
from jax import lax
from jax.experimental import pallas as pl
from jax.experimental.pallas import tpu as pltpu
from jax.sharding import PartitionSpec as P

BF = jnp.bfloat16
F32 = jnp.float32
SIDE = 4
TABS = 16
ROWS = 16
HALF = 64
WIDTH = 256
SLOTS = 16
PICKS = 24
PAIRS = SLOTS * PICKS
SHARE = ROWS * 128
SENT = SHARE + PAIRS
DEPTH = PICKS * HALF
PITCH = PAIRS + 8
ROW_PITCH = ROWS + 8
PACK_MIB = 16
MIB = 1 << 20
ENV = 4
SIZE = ENV + SLOTS
FETCH = SIZE + SLOTS // 2
LISTED = 3
STEP = SLOTS * ROWS
X_ORDER = (2, 1, 3)
Z_ORDER = (2, 1, 3)
PLANES = (0, 2, 1, 3)
CHOOSE_COST = 1_000_000_000
OWN_COST = 100_000_000_000
FAR_COST = 4_000_000_000
WEIGH_COST = 100_000_000_000


def in_hbm(value):
    return pltpu.with_memory_space_constraint(value, pltpu.HBM)


def swap_halves(value):
    return pltpu.roll(value, 64, 1)


def pack_kernel(meta, blocks, pick_in, tab_in, slot_in, live_in, out_ref, held, lists, rows, ready, sems, list_sems, out_sems):
    core = meta[0]

    def fetch(x, u):
        source = blocks.at[:, core + 2 * u, pl.ds(x * ROWS, ROWS), :]
        return pltpu.make_async_copy(source, held.at[x, u], sems.at[x, u])

    def hand(x):
        return pltpu.make_async_copy(ready.at[x], out_ref.at[:, x], out_sems.at[x])

    copies = []
    for n, ref in enumerate((pick_in, tab_in, slot_in, live_in)):
        copies.append(pltpu.make_async_copy(ref, lists.at[n], list_sems.at[n]))
        copies[n].start()
    for x in range(SIDE):
        for u in range(2):
            fetch(x, u).start()
    for copy in copies:
        copy.wait()

    terms = pick_in.shape[1]
    tab_hot = (lax.broadcasted_iota(jnp.int32, (TABS, terms), 0) == lists[1]) & (lists[3] > 0)
    pair = lists[2] * PICKS + lists[0]
    pair_hot = lax.broadcasted_iota(jnp.int32, (PAIRS, terms), 0) == pair
    counts = lax.dot_general(
        tab_hot.astype(F32).astype(BF),
        pair_hot.astype(F32).astype(BF),
        (((1,), (1,)), ((), ())),
        preferred_element_type=F32,
    ).astype(BF)
    for y in range(SIDE):
        for x in range(SIDE):
            ready[x, y, :, SHARE:SENT] = counts

    low = lax.broadcasted_iota(jnp.int32, (TABS, 128), 1) < 64
    for x in range(SIDE):
        for u in range(2):
            fetch(x, u).wait()
            for t in range(TABS):
                block = held[x, u, t].astype(F32)
                for k in range(2):
                    rows[k, u, t * ROW_PITCH : t * ROW_PITCH + ROWS, :] = block[:, k * 128 : k * 128 + 128]
        for q in range(ROWS):
            lanes = slice(q * 128, q * 128 + 128)
            for k in range(2):
                a = rows[k, 0, pl.ds(q, TABS, stride=ROW_PITCH), :]
                b = rows[k, 1, pl.ds(q, TABS, stride=ROW_PITCH), :]
                mixed = swap_halves(jnp.where(low, b, a))
                ready[x, 2 * k, :, lanes] = jnp.where(low, a, mixed).astype(BF)
                ready[x, 2 * k + 1, :, lanes] = jnp.where(low, mixed, b).astype(BF)
        hand(x).start()
    for x in range(SIDE):
        hand(x).wait()


def pack(meta, recoupling, pick, tab, slot, live):
    there = pl.BlockSpec(memory_space=pltpu.HBM)
    out = pl.pallas_call(
        pack_kernel,
        in_specs=[pl.BlockSpec(memory_space=pltpu.SMEM)] + [there] * 5,
        out_specs=there,
        out_shape=pltpu.HBM((SIDE, SIDE, TABS, SENT), BF),
        scratch_shapes=[
            pltpu.VMEM((SIDE, 2, TABS, ROWS, WIDTH), BF),
            pltpu.VMEM((4, 1, pick.shape[0]), jnp.int32),
            pltpu.VMEM((2, 2, TABS * ROW_PITCH, 128), F32),
            pltpu.VMEM((SIDE, SIDE, TABS, SENT), BF),
            pltpu.SemaphoreType.DMA((SIDE, 2)),
            pltpu.SemaphoreType.DMA((4,)),
            pltpu.SemaphoreType.DMA((SIDE,)),
        ],
        compiler_params=pltpu.CompilerParams(vmem_limit_bytes=PACK_MIB * MIB),
        name="pack",
    )(
        meta,
        in_hbm(recoupling.reshape(TABS, SIDE, HALF, WIDTH)),
        *(in_hbm(v.reshape(1, -1)) for v in (pick, tab, slot, live)),
    )
    return out.reshape(SIDE * SIDE, TABS, SENT)


def spread(counts_ref, share_ref, sums, hi_ref, lo_ref):
    counts = counts_ref[:, SHARE:SENT]
    for n in range(ROWS // 2):
        part = lax.dot_general(
            counts, share_ref[:, n * 256 : n * 256 + 256], (((0,), (0,)), ((), ())), preferred_element_type=F32
        )
        for k in range(2):
            start = (2 * n + k) * PITCH
            sums[start : start + PAIRS, :] = part[:, k * 128 : k * 128 + 128]
    low = lax.broadcasted_iota(jnp.int32, (ROWS, 128), 1) < 64

    def one(s, carry):
        for k in range(PICKS // 2):
            row = s * PICKS + 2 * k
            a = sums[pl.ds(row, ROWS, stride=PITCH), :]
            b = sums[pl.ds(row + 1, ROWS, stride=PITCH), :]
            mixed = swap_halves(jnp.where(low, b, a))
            for u, value in enumerate((jnp.where(low, a, mixed), jnp.where(low, mixed, b))):
                hi = value.astype(BF)
                place = pl.ds(pl.multiple_of(u * STEP + s * ROWS, ROWS), ROWS)
                hi_ref[place, k * 128 : k * 128 + 128] = hi
                lo_ref[place, k * 128 : k * 128 + 128] = (value - hi.astype(F32)).astype(BF)
        return carry

    lax.fori_loop(0, SLOTS, one, 0, unroll=4)


def product(hi_ref, lo_ref, wave):
    part = jnp.dot(hi_ref[...], wave[...], preferred_element_type=F32)
    return part + jnp.dot(lo_ref[...], wave[...], preferred_element_type=F32)


def multiply(hi_ref, lo_ref, weights):
    part = jnp.dot(hi_ref[...], weights, preferred_element_type=F32)
    return part + jnp.dot(lo_ref[...], weights, preferred_element_type=F32)


def own_kernel(mine, hi_ref, lo_ref, sums):
    spread(mine, mine, sums, hi_ref, lo_ref)


def own_half(mine):
    here = pl.BlockSpec(memory_space=pltpu.VMEM)
    return pl.pallas_call(
        own_kernel,
        in_specs=[here],
        out_specs=[here] * 2,
        out_shape=[pltpu.VMEM((2 * STEP, DEPTH), BF)] * 2,
        scratch_shapes=[pltpu.VMEM((ROWS * PITCH, 128), F32)],
        compiler_params=pltpu.CompilerParams(vmem_limit_bytes=16 * MIB),
        cost_estimate=pl.CostEstimate(flops=OWN_COST, bytes_accessed=MIB, transcendentals=0),
        name="own_half",
    )(mine)


def choose_kernel(meta, hi_ref, lo_ref, *refs):
    planes, (out_ref, wave) = refs[:8], refs[8:]
    core, x, z = meta[0], meta[1], meta[3]
    for c in range(2):
        for place, e in enumerate(PLANES):
            group = 2 * lax.rem(z - e + SIDE, SIDE) + (core if c == 0 else 1 - core)
            for n in range(LISTED):
                pick = LISTED * group + n
                piece = meta[FETCH + pick]
                for d in range(SIDE):
                    rows = pl.ds(pl.multiple_of(lax.rem(x - d + SIDE, SIDE) * ROWS, ROWS), ROWS)
                    wave[pick, rows, :] = planes[c * SIDE + place][d, piece]
    out_ref[...] = multiply(hi_ref, lo_ref, wave[...].reshape(DEPTH, WIDTH))


def choose(meta, own, planes):
    here = pl.BlockSpec(memory_space=pltpu.VMEM)
    return pl.pallas_call(
        choose_kernel,
        in_specs=[pl.BlockSpec(memory_space=pltpu.SMEM)] + [here] * 10,
        out_specs=[here] * 2,
        out_shape=[pltpu.VMEM((2 * STEP, WIDTH), F32), pltpu.VMEM((PICKS, HALF, WIDTH), BF)],
        compiler_params=pltpu.CompilerParams(vmem_limit_bytes=16 * MIB),
        cost_estimate=pl.CostEstimate(flops=CHOOSE_COST, bytes_accessed=MIB, transcendentals=0),
        name="choose",
    )(meta, *own, *planes)


def far_kernel(meta, mine, theirs, own, wave, right, s0, s1, s2, s3, sums, hi_ref, lo_ref, channel):
    core, x, y = meta[0], meta[1], meta[2]
    spread(mine, theirs, sums, hi_ref, lo_ref)
    weights = wave[...].reshape(DEPTH, WIDTH)
    for u in range(2):
        rows = slice(u * STEP, (u + 1) * STEP)
        channel[lax.rem(2 * u + core - y + SIDE, SIDE)] = own[rows, :]
        part = jnp.dot(hi_ref[rows, :], weights, preferred_element_type=F32)
        part = part + jnp.dot(lo_ref[rows, :], weights, preferred_element_type=F32)
        channel[lax.rem(2 * u + 1 - core - y + SIDE, SIDE)] = part
    columns = lax.broadcasted_iota(jnp.int32, (ROWS, WIDTH), 1)
    lines = lax.broadcasted_iota(jnp.int32, (ROWS, WIDTH), 0)
    reach = [jnp.maximum(lines + (lax.rem(y + d, SIDE) * SIDE + x) * ROWS, columns) for d in range(SIDE)]
    for o in range(SLOTS // 2):
        result = None
        for s in (2 * o, 2 * o + 1):
            env = right[meta[ENV + s]]
            value = channel[:, s * ROWS : (s + 1) * ROWS, :].reshape(HALF, WIDTH)
            hi = value.astype(BF)
            lo = (value - hi.astype(F32)).astype(BF)
            part = jnp.dot(jnp.concatenate([hi, lo], axis=0), env, preferred_element_type=F32)
            part = part[:HALF] + part[HALF:]
            result = part if result is None else result + part
        size = meta[SIZE + o]
        for d, ref in enumerate((s0, s1, s2, s3)):
            ref[o] = jnp.where(reach[d] < size, result[d * ROWS : (d + 1) * ROWS], 0.0)


def far_half(meta, mine, theirs, own, wave, right):
    sectors = SLOTS // 2
    here = pl.BlockSpec(memory_space=pltpu.VMEM)
    return pl.pallas_call(
        far_kernel,
        in_specs=[pl.BlockSpec(memory_space=pltpu.SMEM)] + [here] * 5,
        out_specs=[here] * 4,
        out_shape=[pltpu.VMEM((sectors, ROWS, WIDTH), F32)] * 4,
        scratch_shapes=[
            pltpu.VMEM((ROWS * PITCH, 128), F32),
            pltpu.VMEM((2 * STEP, DEPTH), BF),
            pltpu.VMEM((2 * STEP, DEPTH), BF),
            pltpu.VMEM((SIDE, STEP, WIDTH), F32),
        ],
        compiler_params=pltpu.CompilerParams(vmem_limit_bytes=24 * MIB),
        cost_estimate=pl.CostEstimate(flops=FAR_COST, bytes_accessed=MIB, transcendentals=0),
        name="far_half",
    )(meta, mine, theirs, own, wave, right)


def along_table(dy, dx):
    return [
        (y * SIDE + x, (y + dy) % SIDE * SIDE + (x + dx) % SIDE) for y in range(SIDE) for x in range(SIDE)
    ]


def along_sector(dz, dc):
    return [(z * 2 + c, (z + dz) % SIDE * 2 + (c ^ dc)) for z in range(SIDE) for c in range(2)]


def local(
    wave_blocks,
    recoupling,
    right_blocks,
    sector_sizes,
    channel_env,
    fetch_list,
    term_pick,
    term_table,
    term_slot,
    term_live,
):
    sector = lax.axis_index("sector")
    place = lax.axis_index("table")
    z, core = sector // 2, sector % 2
    y, x = place // SIDE, place % SIDE

    meta = jnp.concatenate(
        [jnp.stack([core, x, y, z]), channel_env.reshape(-1), sector_sizes, fetch_list.reshape(-1)]
    )

    lines = {0: wave_blocks}
    for d in X_ORDER:
        lines[d] = lax.ppermute(wave_blocks, "table", along_table(0, d))
    lines = [lines[d] for d in range(SIDE)]
    sent = pack(core.reshape(1), recoupling, term_pick, term_table, term_slot, term_live)
    sent, lines = lax.optimization_barrier((sent, lines))
    mine = lax.all_to_all(sent, "table", 0, 0).reshape(TABS * SIDE * SIDE, SENT)
    theirs = lax.ppermute(mine, "sector", along_sector(0, 1))

    planes = {0: jnp.stack(lines)}
    for e in Z_ORDER:
        planes[e] = lax.ppermute(planes[0], "sector", along_sector(e, 0))
    planes = [planes[e] for e in PLANES]
    planes = planes + [lax.ppermute(p, "sector", along_sector(0, 1)) for p in planes]
    own, wave = choose(meta, own_half(mine), planes)
    parts = far_half(meta, mine, theirs, own, wave, right_blocks)
    result = parts[0]
    for d in (2, 1, 3):
        result = result + lax.ppermute(parts[d], "table", along_table(d, 0))
    return result


def solution(mesh):
    placed = (
        P("sector", "table", None),
        P("table", None, None),
        P("sector", None, None),
        P("sector"),
        P("sector", None),
        P("sector", None, None),
        P(("sector", "table")),
        P(("sector", "table")),
        P(("sector", "table")),
        P(("sector", "table")),
    )
    return jax.shard_map(
        local, mesh=mesh, in_specs=placed, out_specs=P("sector", "table", None), check_vma=False
    )
```

time: 407 us -> 53 us (0.13)
  the two profiles are of different devices: /device:TPU:0 before, /device:TPU:1 now
where the time goes in v3:
time: 53 us; the launch traced here: 52.7 us
  starting transfers between devices  28.9 us (55%)
  waiting for transfers between devices  12.6 us (24%)
  Pallas kernels  9.84 us (19%)
  other arithmetic  0.73 us (1%)
    ppermute x4, starting transfers between devices, local(): lax.ppermute(p, 'sector', along_sector(0, 1))  7.36 us
    ppermute x3, waiting for transfers between devices, local(): planes[e] = lax.ppermute(planes[0], 'sector', along_sector(e, 0))  7.08 us
    all_to_all x1, starting transfers between devices, local(): mine = lax.all_to_all(sent, 'table', 0, 0).reshape(TABS * SIDE * SIDE, SENT)  5.79 us
    ppermute x3, starting transfers between devices, local(): lines[d] = lax.ppermute(wave_blocks, 'table', along_table(0, d))  5.64 us
    ppermute x3, waiting for transfers between devices, local(): result = result + lax.ppermute(parts[d], 'table', along_table(d, 0))  5.49 us
    ppermute x3, starting transfers between devices, local(): planes[e] = lax.ppermute(planes[0], 'sector', along_sector(e, 0))  4.53 us
    ppermute x3, starting transfers between devices, local(): result = result + lax.ppermute(parts[d], 'table', along_table(d, 0))  4.32 us
    pallas_call x1, Pallas kernels, far_half(): pl.pallas_call(far_kernel, in_specs=[pl.BlockSpec(memory_space=pltpu.SMEM...  3.61 us
  transfers between devices with their start and end apart: 15, of which 4 were waited for; matrix products, arithmetic and copies ran while one was open for 1% of the time, Pallas kernels for 12%

profile of v3, /device:TPU:1, one launch (start us, length us, event | category | flops | bytes accessed | tf_op | source)
XLA Modules:
  0.0 52.7 jit_solution(1037256126145441389)
XLA Ops:
  0.0 2.0 %collective-permute-start = (bf16[8,16,256]{2,1,0:T(8,128)(2,1)}, bf16[8,16,256]{2,1,0:T(8,128)(2,1)S(1)}, u32[]{:S(2)}, u32[]{:S(2)}) collective-permute-start(bf16[8,16,256]{2,1,0:T(8,128)(2,1)} %param.10), channel_id=1, source_target_pairs={{0,1},{1,2},{2,3},{3,0},{4,5},{5,6},{6,7},{7,4},{8,9},{9,10},{10,1... | collective-permute-start | bytes 196616 | tf_op jit(solution)/shard_map/ppermute | solution.py:294
  2.0 2.5 %collective-permute-start.1 = (bf16[8,16,256]{2,1,0:T(8,128)(2,1)}, bf16[8,16,256]{2,1,0:T(8,128)(2,1)S(1)}, u32[]{:S(2)}, u32[]{:S(2)}) collective-permute-start(bf16[8,16,256]{2,1,0:T(8,128)(2,1)} %param.10), channel_id=1, source_target_pairs={{0,2},{1,3},{2,0},{3,1},{4,6},{5,7},{6,4},{7,5},{8,10},{9,11},{10,... | collective-permute-start | bytes 196616 | tf_op jit(solution)/shard_map/ppermute | solution.py:294
  4.5 1.2 %collective-permute-start.2 = (bf16[8,16,256]{2,1,0:T(8,128)(2,1)}, bf16[8,16,256]{2,1,0:T(8,128)(2,1)S(1)}, u32[]{:S(2)}, u32[]{:S(2)}) collective-permute-start(bf16[8,16,256]{2,1,0:T(8,128)(2,1)} %param.10), channel_id=1, source_target_pairs={{0,3},{1,0},{2,1},{3,2},{4,7},{5,4},{6,5},{7,6},{8,11},{9,8},{10,9... | collective-permute-start | bytes 196616 | tf_op jit(solution)/shard_map/ppermute | solution.py:294
  5.6 2.9 %pack.1 = bf16[4,4,16,2432]{3,2,1,0:T(8,128)(2,1)} custom-call(s32[1]{0:T(128)} %bitcast.meta, bf16[16,4,64,256]{3,2,1,0:T(8,128)(2,1)} %bitcast.19, s32[1,192]{1,0:T(1,128)} %bitcast.24, s32[1,192]{1,0:T(1,128)} %bitcast.25, s32[1,192]{1,0:T(1,128)} %bitcast.26, s32[1,192]{1,0:T(1,128)} %bitcast.27), custom_call_target="tpu_custom_call" | custom-call | tf_op jit(solution)/shard_map/pack/pallas_call | solution.py:106
  8.6 0.0 copy-start.1
  8.6 0.0 copy-start.3
  8.6 0.0 copy-start.2
  8.6 0.0 copy-start.4
  8.6 0.0 collective-permute-done
  8.7 0.0 collective-permute-done.1
  8.7 0.0 collective-permute-done.2
  8.7 5.8 %all-to-all-start = ((bf16[16,16,2432]{2,1,0:T(8,128)(2,1)}), bf16[16,16,2432]{2,1,0:T(8,128)(2,1)S(1)}, u32[]{:S(2)}, u32[]{:S(2)}) async-start(bf16[16,16,2432]{2,1,0:T(8,128)(2,1)} %bitcast.18), calls=%async_computation | async-start | bytes 2490368 | tf_op jit(solution)/shard_map/all_to_all | solution.py:298
  14.5 0.0 copy-done.1
  14.5 3.8 %collective-permute-start.6 = (bf16[4,8,16,256]{3,2,1,0:T(8,128)(2,1)S(1)}, bf16[4,8,16,256]{3,2,1,0:T(8,128)(2,1)S(1)}, u32[]{:S(2)}, u32[]{:S(2)}) collective-permute-start(bf16[4,8,16,256]{3,2,1,0:T(8,128)(2,1)S(1)} %pad_maximum_fusion.refs_0_), channel_id=1, source_target_pairs={{0,96},{16,112},{32,0},{48,16},{64,32},{80,48},{96,64},{112,80},{1... | collective-permute-start | bytes 786440 | tf_op jit(solution)/shard_map/ppermute | solution.py:303
  18.4 0.0 collective-permute-start.4
  18.4 0.7 %collective-permute-start.5 = (bf16[4,8,16,256]{3,2,1,0:T(8,128)(2,1)S(1)}, bf16[4,8,16,256]{3,2,1,0:T(8,128)(2,1)S(1)}, u32[]{:S(2)}, u32[]{:S(2)}) collective-permute-start(bf16[4,8,16,256]{3,2,1,0:T(8,128)(2,1)S(1)} %pad_maximum_fusion.refs_0_), channel_id=1, source_target_pairs={{0,32},{16,48},{32,64},{48,80},{64,96},{80,112},{96,0},{112,16},{1... | collective-permute-start | bytes 786440 | tf_op jit(solution)/shard_map/ppermute | solution.py:303
  19.1 0.0 copy-done.3
  19.1 0.1 copy.13
  19.1 0.1 reshape.28
  19.2 0.1 copy.14
  19.3 0.1 reshape.29
  19.4 0.0 copy-done.4
  19.4 0.1 concatenate.3.meta
  19.5 3.3 %collective-permute-start.7 = (bf16[4,8,16,256]{3,2,1,0:T(8,128)(2,1)S(1)}, bf16[4,8,16,256]{3,2,1,0:T(8,128)(2,1)S(1)}, u32[]{:S(2)}, u32[]{:S(2)}) collective-permute-start(bf16[4,8,16,256]{3,2,1,0:T(8,128)(2,1)S(1)} %pad_maximum_fusion.refs_0_), channel_id=1, source_target_pairs={{0,16},{16,0},{32,48},{48,32},{64,80},{80,64},{96,112},{112,96},{1... | collective-permute-start | bytes 786440 | tf_op jit(solution)/shard_map/ppermute | solution.py:305
  22.7 5.5 %collective-permute-done.6.refs_3_ = bf16[4,8,16,256]{3,2,1,0:T(8,128)(2,1)S(1)} collective-permute-done((bf16[4,8,16,256]{3,2,1,0:T(8,128)(2,1)S(1)}, bf16[4,8,16,256]{3,2,1,0:T(8,128)(2,1)S(1)}, u32[]{:S(2)}, u32[]{:S(2)}) %collective-permute-start.6) | collective-permute-done | bytes 262176 | tf_op jit(solution)/shard_map/ppermute | solution.py:303
  28.2 2.3 %collective-permute-start.10 = (bf16[4,8,16,256]{3,2,1,0:T(8,128)(2,1)S(1)}, bf16[4,8,16,256]{3,2,1,0:T(8,128)(2,1)S(1)}, u32[]{:S(2)}, u32[]{:S(2)}) collective-permute-start(bf16[4,8,16,256]{3,2,1,0:T(8,128)(2,1)S(1)} %collective-permute-done.6.refs_3_), channel_id=1, source_target_pairs={{0,16},{16,0},{32,48},{48,32},{64,80},{80,64},{96,112},{112,96},{1... | collective-permute-start | bytes 786440 | tf_op jit(solution)/shard_map/ppermute | solution.py:305
  30.5 0.0 collective-permute-done.4.refs_1_
  30.5 1.0 %collective-permute-start.8 = (bf16[4,8,16,256]{3,2,1,0:T(8,128)(2,1)S(1)}, bf16[4,8,16,256]{3,2,1,0:T(8,128)(2,1)S(1)}, u32[]{:S(2)}, u32[]{:S(2)}) collective-permute-start(bf16[4,8,16,256]{3,2,1,0:T(8,128)(2,1)S(1)} %collective-permute-done.4.refs_1_), channel_id=1, source_target_pairs={{0,16},{16,0},{32,48},{48,32},{64,80},{80,64},{96,112},{112,96},{1... | collective-permute-start | bytes 786440 | tf_op jit(solution)/shard_map/ppermute | solution.py:305
  31.5 1.6 %collective-permute-done.5.refs_2_ = bf16[4,8,16,256]{3,2,1,0:T(8,128)(2,1)S(1)} collective-permute-done((bf16[4,8,16,256]{3,2,1,0:T(8,128)(2,1)S(1)}, bf16[4,8,16,256]{3,2,1,0:T(8,128)(2,1)S(1)}, u32[]{:S(2)}, u32[]{:S(2)}) %collective-permute-start.5) | collective-permute-done | bytes 262176 | tf_op jit(solution)/shard_map/ppermute | solution.py:303
  33.1 0.8 %collective-permute-start.9 = (bf16[4,8,16,256]{3,2,1,0:T(8,128)(2,1)S(1)}, bf16[4,8,16,256]{3,2,1,0:T(8,128)(2,1)S(1)}, u32[]{:S(2)}, u32[]{:S(2)}) collective-permute-start(bf16[4,8,16,256]{3,2,1,0:T(8,128)(2,1)S(1)} %collective-permute-done.5.refs_2_), channel_id=1, source_target_pairs={{0,16},{16,0},{32,48},{48,32},{64,80},{80,64},{96,112},{112,96},{1... | collective-permute-start | bytes 786440 | tf_op jit(solution)/shard_map/ppermute | solution.py:305
  33.9 0.0 all-to-all-done
  33.9 1.3 %collective-permute-start.3 = (bf16[256,2432]{1,0:T(8,128)(2,1)S(1)}, bf16[256,2432]{1,0:T(8,128)(2,1)S(1)}, u32[]{:S(2)}, u32[]{:S(2)}) collective-permute-start(bf16[256,2432]{1,0:T(8,128)(2,1)S(1)} %bitcast.15), channel_id=1, source_target_pairs={{0,16},{16,0},{32,48},{48,32},{64,80},{80,64},{96,112},{112,96},{1... | collective-permute-start | bytes 3735560 | tf_op jit(solution)/shard_map/ppermute | solution.py:299
  35.2 1.7 %own_half.1 = (bf16[512,1536]{1,0:T(8,128)(2,1)S(1)}, bf16[512,1536]{1,0:T(8,128)(2,1)S(1)}) custom-call(bf16[256,2432]{1,0:T(8,128)(2,1)S(1)} %bitcast.16), custom_call_target="tpu_custom_call" | custom-call | flops 99999997952 | bytes 1048576 | tf_op jit(solution)/shard_map/own_half/pallas_call | solution.py:173
  36.9 0.0 collective-permute-done.7.refs_4_
  36.9 0.0 collective-permute-done.10.refs_7_
  36.9 0.0 collective-permute-done.8.refs_5_
  36.9 0.0 collective-permute-done.9.refs_6_
  36.9 0.0 copy-start
  37.0 1.6 %choose.1 = (f32[512,256]{1,0:T(8,128)S(1)}, bf16[24,64,256]{2,1,0:T(8,128)(2,1)S(1)}) custom-call(s32[52]{0:T(128)S(1)} %concatenate.3.meta, bf16[512,1536]{1,0:T(8,128)(2,1)S(1)} %get-tuple-element.19.hi_ref, bf16[512,1536]{1,0:T(8,128)(2,1)S(1)} %get-tuple-element.20.lo_ref, bf16[4,8,16,256]{3,2,1,0:T(8,128)(2,1)S(1)} %pad_maximum_fusion.refs_0_, ...), custom_call_target="tpu_custom_call" | custom-call | flops 1000000000 | bytes 1048576 | tf_op jit(solution)/shard_map/choose/pallas_call | solution.py:202
  38.6 0.0 collective-permute-done.3.theirs
  38.6 3.6 %far_half.1 = (f32[8,16,256]{2,1,0:T(8,128)S(1)}, f32[8,16,256]{2,1,0:T(8,128)S(1)}, f32[8,16,256]{2,1,0:T(8,128)S(1)}, f32[8,16,256]{2,1,0:T(8,128)S(1)}) custom-call(s32[52]{0:T(128)S(1)} %concatenate.3.meta, bf16[256,2432]{1,0:T(8,128)(2,1)S(1)} %bitcast.17, bf16[256,2432]{1,0:T(8,128)(2,1)S(1)} %collective-permute-done.3.theirs, ...), custom_call_target="tpu_custom_call" | custom-call | flops 4000000000 | bytes 1048576 | tf_op jit(solution)/shard_map/far_half/pallas_call | solution.py:244
  42.2 1.6 %collective-permute-start.11 = (f32[8,16,256]{2,1,0:T(8,128)S(1)}, f32[8,16,256]{2,1,0:T(8,128)S(1)}, u32[]{:S(2)}, u32[]{:S(2)}) collective-permute-start(f32[8,16,256]{2,1,0:T(8,128)S(1)} %get-tuple-element.28), channel_id=1, source_target_pairs={{0,8},{1,9},{2,10},{3,11},{4,12},{5,13},{6,14},{7,15},{8,0},{9,1},... | collective-permute-start | bytes 393224 | tf_op jit(solution)/shard_map/ppermute | solution.py:310
  43.9 0.3 collective-permute-start.12
  44.1 2.4 %collective-permute-start.13 = (f32[8,16,256]{2,1,0:T(8,128)S(1)}, f32[8,16,256]{2,1,0:T(8,128)S(1)}, u32[]{:S(2)}, u32[]{:S(2)}) collective-permute-start(f32[8,16,256]{2,1,0:T(8,128)S(1)} %get-tuple-element.30), channel_id=1, source_target_pairs={{0,12},{1,13},{2,14},{3,15},{4,0},{5,1},{6,2},{7,3},{8,4},{9,5},{1... | collective-permute-start | bytes 393224 | tf_op jit(solution)/shard_map/ppermute | solution.py:310
  46.5 2.4 %collective-permute-done.11 = f32[8,16,256]{2,1,0:T(8,128)S(1)} collective-permute-done((f32[8,16,256]{2,1,0:T(8,128)S(1)}, f32[8,16,256]{2,1,0:T(8,128)S(1)}, u32[]{:S(2)}, u32[]{:S(2)}) %collective-permute-start.11) | collective-permute-done | bytes 131104 | tf_op jit(solution)/shard_map/ppermute | solution.py:310
  48.9 3.1 %collective-permute-done.12 = f32[8,16,256]{2,1,0:T(8,128)S(1)} collective-permute-done((f32[8,16,256]{2,1,0:T(8,128)S(1)}, f32[8,16,256]{2,1,0:T(8,128)S(1)}, u32[]{:S(2)}, u32[]{:S(2)}) %collective-permute-start.12) | collective-permute-done | bytes 131104 | tf_op jit(solution)/shard_map/ppermute | solution.py:310
  52.0 0.0 collective-permute-done.13
  52.0 0.7 %add_add_fusion = f32[8,16,256]{2,1,0:T(8,128)} fusion(f32[8,16,256]{2,1,0:T(8,128)S(1)} %collective-permute-done.13, f32[8,16,256]{2,1,0:T(8,128)S(1)} %collective-permute-done.12, f32[8,16,256]{2,1,0:T(8,128)S(1)} %get-tuple-element.27, f32[8,16,256]{2,1,0:T(8,128)S(1)} %collective-permute-done.11), kind=kLoop, calls=%fused_computation.1 | loop fusion | flops 98304 | bytes 655360 | tf_op jit(solution)/shard_map/add | solution.py:310
  (3 shorter events, 0.0 us)
Async XLA Ops:
  0.0 8.6 %collective-permute-start = (bf16[8,16,256]{2,1,0:T(8,128)(2,1)}, bf16[8,16,256]{2,1,0:T(8,128)(2,1)S(1)}, u32[]{:S(2)}, u32[]{:S(2)}) collective-permute-start(bf16[8,16,256]{2,1,0:T(8,128)(2,1)} %param.10), channel_id=1, source_target_pairs={{0,1},{1,2},{2,3},{3,0},{4,5},{5,6},{6,7},{7,4},{8,9},{9,10},{10,1... | collective-permute-start | bytes 196616 | tf_op jit(solution)/shard_map/ppermute | solution.py:294
  2.0 6.6 %collective-permute-start.1 = (bf16[8,16,256]{2,1,0:T(8,128)(2,1)}, bf16[8,16,256]{2,1,0:T(8,128)(2,1)S(1)}, u32[]{:S(2)}, u32[]{:S(2)}) collective-permute-start(bf16[8,16,256]{2,1,0:T(8,128)(2,1)} %param.10), channel_id=1, source_target_pairs={{0,2},{1,3},{2,0},{3,1},{4,6},{5,7},{6,4},{7,5},{8,10},{9,11},{10,... | collective-permute-start | bytes 196616 | tf_op jit(solution)/shard_map/ppermute | solution.py:294
  4.5 4.2 %collective-permute-start.2 = (bf16[8,16,256]{2,1,0:T(8,128)(2,1)}, bf16[8,16,256]{2,1,0:T(8,128)(2,1)S(1)}, u32[]{:S(2)}, u32[]{:S(2)}) collective-permute-start(bf16[8,16,256]{2,1,0:T(8,128)(2,1)} %param.10), channel_id=1, source_target_pairs={{0,3},{1,0},{2,1},{3,2},{4,7},{5,4},{6,5},{7,6},{8,11},{9,8},{10,9... | collective-permute-start | bytes 196616 | tf_op jit(solution)/shard_map/ppermute | solution.py:294
  8.6 5.9 %copy-start.1 = (bf16[8,16,256]{2,1,0:T(8,128)(2,1)S(1)}, bf16[8,16,256]{2,1,0:T(8,128)(2,1)}, u32[]{:S(2)}) copy-start(bf16[8,16,256]{2,1,0:T(8,128)(2,1)} %param.10) | copy-start | bytes 196612
  8.6 10.5 %copy-start.3 = (s32[8,2]{0,1:T(2,128)S(1)}, s32[8,2]{0,1:T(2,128)}, u32[]{:S(2)}) copy-start(s32[8,2]{0,1:T(2,128)} %param.14) | copy-start | bytes 196
  8.6 10.6 %copy-start.2 = (s32[1,8,3]{1,0,2:T(1,128)S(1)}, s32[1,8,3]{1,0,2:T(1,128)}, u32[]{:S(2)}) copy-start(s32[1,8,3]{1,0,2:T(1,128)} %param.15) | copy-start | bytes 292
  8.6 10.8 %copy-start.4 = (s32[8]{0:T(128)S(1)}, s32[8]{0:T(128)}, u32[]{:S(2)}) copy-start(s32[8]{0:T(128)} %param.13) | copy-start | bytes 100
  8.7 25.2 %all-to-all-start = ((bf16[16,16,2432]{2,1,0:T(8,128)(2,1)}), bf16[16,16,2432]{2,1,0:T(8,128)(2,1)S(1)}, u32[]{:S(2)}, u32[]{:S(2)}) async-start(bf16[16,16,2432]{2,1,0:T(8,128)(2,1)} %bitcast.18), calls=%async_computation | async-start | bytes 2490368 | tf_op jit(solution)/shard_map/all_to_all | solution.py:298
  14.5 13.7 %collective-permute-start.6 = (bf16[4,8,16,256]{3,2,1,0:T(8,128)(2,1)S(1)}, bf16[4,8,16,256]{3,2,1,0:T(8,128)(2,1)S(1)}, u32[]{:S(2)}, u32[]{:S(2)}) collective-permute-start(bf16[4,8,16,256]{3,2,1,0:T(8,128)(2,1)S(1)} %pad_maximum_fusion.refs_0_), channel_id=1, source_target_pairs={{0,96},{16,112},{32,0},{48,16},{64,32},{80,48},{96,64},{112,80},{1... | collective-permute-start | bytes 786440 | tf_op jit(solution)/shard_map/ppermute | solution.py:303
  18.4 12.1 %collective-permute-start.4 = (bf16[4,8,16,256]{3,2,1,0:T(8,128)(2,1)S(1)}, bf16[4,8,16,256]{3,2,1,0:T(8,128)(2,1)S(1)}, u32[]{:S(2)}, u32[]{:S(2)}) collective-permute-start(bf16[4,8,16,256]{3,2,1,0:T(8,128)(2,1)S(1)} %pad_maximum_fusion.refs_0_), channel_id=1, source_target_pairs={{0,64},{16,80},{32,96},{48,112},{64,0},{80,16},{96,32},{112,48},{1... | collective-permute-start | bytes 786440 | tf_op jit(solution)/shard_map/ppermute | solution.py:303
  18.4 14.7 %collective-permute-start.5 = (bf16[4,8,16,256]{3,2,1,0:T(8,128)(2,1)S(1)}, bf16[4,8,16,256]{3,2,1,0:T(8,128)(2,1)S(1)}, u32[]{:S(2)}, u32[]{:S(2)}) collective-permute-start(bf16[4,8,16,256]{3,2,1,0:T(8,128)(2,1)S(1)} %pad_maximum_fusion.refs_0_), channel_id=1, source_target_pairs={{0,32},{16,48},{32,64},{48,80},{64,96},{80,112},{96,0},{112,16},{1... | collective-permute-start | bytes 786440 | tf_op jit(solution)/shard_map/ppermute | solution.py:303
  19.5 17.4 %collective-permute-start.7 = (bf16[4,8,16,256]{3,2,1,0:T(8,128)(2,1)S(1)}, bf16[4,8,16,256]{3,2,1,0:T(8,128)(2,1)S(1)}, u32[]{:S(2)}, u32[]{:S(2)}) collective-permute-start(bf16[4,8,16,256]{3,2,1,0:T(8,128)(2,1)S(1)} %pad_maximum_fusion.refs_0_), channel_id=1, source_target_pairs={{0,16},{16,0},{32,48},{48,32},{64,80},{80,64},{96,112},{112,96},{1... | collective-permute-start | bytes 786440 | tf_op jit(solution)/shard_map/ppermute | solution.py:305
  28.2 8.7 %collective-permute-start.10 = (bf16[4,8,16,256]{3,2,1,0:T(8,128)(2,1)S(1)}, bf16[4,8,16,256]{3,2,1,0:T(8,128)(2,1)S(1)}, u32[]{:S(2)}, u32[]{:S(2)}) collective-permute-start(bf16[4,8,16,256]{3,2,1,0:T(8,128)(2,1)S(1)} %collective-permute-done.6.refs_3_), channel_id=1, source_target_pairs={{0,16},{16,0},{32,48},{48,32},{64,80},{80,64},{96,112},{112,96},{1... | collective-permute-start | bytes 786440 | tf_op jit(solution)/shard_map/ppermute | solution.py:305
  30.5 6.4 %collective-permute-start.8 = (bf16[4,8,16,256]{3,2,1,0:T(8,128)(2,1)S(1)}, bf16[4,8,16,256]{3,2,1,0:T(8,128)(2,1)S(1)}, u32[]{:S(2)}, u32[]{:S(2)}) collective-permute-start(bf16[4,8,16,256]{3,2,1,0:T(8,128)(2,1)S(1)} %collective-permute-done.4.refs_1_), channel_id=1, source_target_pairs={{0,16},{16,0},{32,48},{48,32},{64,80},{80,64},{96,112},{112,96},{1... | collective-permute-start | bytes 786440 | tf_op jit(solution)/shard_map/ppermute | solution.py:305
  33.1 3.9 %collective-permute-start.9 = (bf16[4,8,16,256]{3,2,1,0:T(8,128)(2,1)S(1)}, bf16[4,8,16,256]{3,2,1,0:T(8,128)(2,1)S(1)}, u32[]{:S(2)}, u32[]{:S(2)}) collective-permute-start(bf16[4,8,16,256]{3,2,1,0:T(8,128)(2,1)S(1)} %collective-permute-done.5.refs_2_), channel_id=1, source_target_pairs={{0,16},{16,0},{32,48},{48,32},{64,80},{80,64},{96,112},{112,96},{1... | collective-permute-start | bytes 786440 | tf_op jit(solution)/shard_map/ppermute | solution.py:305
  33.9 4.7 %collective-permute-start.3 = (bf16[256,2432]{1,0:T(8,128)(2,1)S(1)}, bf16[256,2432]{1,0:T(8,128)(2,1)S(1)}, u32[]{:S(2)}, u32[]{:S(2)}) collective-permute-start(bf16[256,2432]{1,0:T(8,128)(2,1)S(1)} %bitcast.15), channel_id=1, source_target_pairs={{0,16},{16,0},{32,48},{48,32},{64,80},{80,64},{96,112},{112,96},{1... | collective-permute-start | bytes 3735560 | tf_op jit(solution)/shard_map/ppermute | solution.py:299
  36.9 1.6 %copy-start = (bf16[8,256,256]{2,1,0:T(8,128)(2,1)S(1)}, bf16[8,256,256]{2,1,0:T(8,128)(2,1)}, u32[]{:S(2)}) copy-start(bf16[8,256,256]{2,1,0:T(8,128)(2,1)} %right.1) | copy-start | bytes 3145732
  42.2 6.7 %collective-permute-start.11 = (f32[8,16,256]{2,1,0:T(8,128)S(1)}, f32[8,16,256]{2,1,0:T(8,128)S(1)}, u32[]{:S(2)}, u32[]{:S(2)}) collective-permute-start(f32[8,16,256]{2,1,0:T(8,128)S(1)} %get-tuple-element.28), channel_id=1, source_target_pairs={{0,8},{1,9},{2,10},{3,11},{4,12},{5,13},{6,14},{7,15},{8,0},{9,1},... | collective-permute-start | bytes 393224 | tf_op jit(solution)/shard_map/ppermute | solution.py:310
  43.9 8.2 %collective-permute-start.12 = (f32[8,16,256]{2,1,0:T(8,128)S(1)}, f32[8,16,256]{2,1,0:T(8,128)S(1)}, u32[]{:S(2)}, u32[]{:S(2)}) collective-permute-start(f32[8,16,256]{2,1,0:T(8,128)S(1)} %get-tuple-element.29), channel_id=1, source_target_pairs={{0,4},{1,5},{2,6},{3,7},{4,8},{5,9},{6,10},{7,11},{8,12},{9,13},{1... | collective-permute-start | bytes 393224 | tf_op jit(solution)/shard_map/ppermute | solution.py:310
  44.1 7.9 %collective-permute-start.13 = (f32[8,16,256]{2,1,0:T(8,128)S(1)}, f32[8,16,256]{2,1,0:T(8,128)S(1)}, u32[]{:S(2)}, u32[]{:S(2)}) collective-permute-start(f32[8,16,256]{2,1,0:T(8,128)S(1)} %get-tuple-element.30), channel_id=1, source_target_pairs={{0,12},{1,13},{2,14},{3,15},{4,0},{5,1},{6,2},{7,3},{8,4},{9,5},{1... | collective-permute-start | bytes 393224 | tf_op jit(solution)/shard_map/ppermute | solution.py:310

commit v4 on v3

--- a/solution.py
+++ b/solution.py
@@ -28,6 +28,7 @@
 SIZE = ENV + SLOTS
 FETCH = SIZE + SLOTS // 2
 LISTED = 3
+LIMIT = 32700.0
 STEP = SLOTS * ROWS
 X_ORDER = (2, 1, 3)
 Z_ORDER = (2, 1, 3)
@@ -210,8 +211,9 @@
     )(meta, *own, *planes)
 
 
-def far_kernel(meta, mine, theirs, own, wave, right, s0, s1, s2, s3, sums, hi_ref, lo_ref, channel):
+def far_kernel(meta, mine, theirs, own, wave, right, s0, s1, s2, s3, sums, hi_ref, lo_ref, channel, codes):
     core, x, y = meta[0], meta[1], meta[2]
+    codes[...] = jnp.zeros_like(codes)
     spread(mine, theirs, sums, hi_ref, lo_ref)
     weights = wave[...].reshape(DEPTH, WIDTH)
     for u in range(2):
@@ -235,7 +237,17 @@
             result = part if result is None else result + part
         size = meta[SIZE + o]
         for d, ref in enumerate((s0, s1, s2, s3)):
-            ref[o] = jnp.where(reach[d] < size, result[d * ROWS : (d + 1) * ROWS], 0.0)
+            part = jnp.where(reach[d] < size, result[d * ROWS : (d + 1) * ROWS], 0.0)
+            if d == 0:
+                ref[o] = part
+                continue
+            peak = jnp.max(jnp.abs(part), axis=0, keepdims=True)
+            code = jnp.ceil(jnp.log2(jnp.maximum(peak, 1e-30)) * 8.0 + 0.01)
+            scaled = part * (jnp.exp2(code * -0.125) * LIMIT)
+            ref[o] = jnp.round(scaled).astype(jnp.int32).astype(jnp.int16)
+            codes[d - 1, o : o + 1, :] = code
+    for d, ref in enumerate((s1, s2, s3)):
+        ref[SLOTS // 2] = codes[d].astype(jnp.int32).astype(jnp.int16)
 
 
 def far_half(meta, mine, theirs, own, wave, right):
@@ -245,17 +257,40 @@
         far_kernel,
         in_specs=[pl.BlockSpec(memory_space=pltpu.SMEM)] + [here] * 5,
         out_specs=[here] * 4,
-        out_shape=[pltpu.VMEM((sectors, ROWS, WIDTH), F32)] * 4,
+        out_shape=[pltpu.VMEM((sectors, ROWS, WIDTH), F32)] + [pltpu.VMEM((sectors + 1, ROWS, WIDTH), jnp.int16)] * 3,
         scratch_shapes=[
             pltpu.VMEM((ROWS * PITCH, 128), F32),
             pltpu.VMEM((2 * STEP, DEPTH), BF),
             pltpu.VMEM((2 * STEP, DEPTH), BF),
             pltpu.VMEM((SIDE, STEP, WIDTH), F32),
+            pltpu.VMEM((3, ROWS, WIDTH), F32),
         ],
         compiler_params=pltpu.CompilerParams(vmem_limit_bytes=24 * MIB),
         cost_estimate=pl.CostEstimate(flops=FAR_COST, bytes_accessed=MIB, transcendentals=0),
         name="far_half",
     )(meta, mine, theirs, own, wave, right)
+
+
+def finish_kernel(own, *refs):
+    parts, out_ref = refs[:-1], refs[-1]
+    scales = [jnp.exp2(ref[SLOTS // 2].astype(jnp.int32).astype(F32) * 0.125) * (1.0 / LIMIT) for ref in parts]
+    for o in range(SLOTS // 2):
+        total = own[o]
+        for ref, scale in zip(parts, scales):
+            total = total + ref[o].astype(jnp.int32).astype(F32) * scale[o : o + 1]
+        out_ref[o] = total
+
+
+def finish(own, parts):
+    here = pl.BlockSpec(memory_space=pltpu.VMEM)
+    return pl.pallas_call(
+        finish_kernel,
+        in_specs=[here] * 4,
+        out_specs=here,
+        out_shape=jax.ShapeDtypeStruct(own.shape, F32),
+        compiler_params=pltpu.CompilerParams(vmem_limit_bytes=4 * MIB),
+        name="finish",
+    )(own, *parts)
 
 
 def along_table(dy, dx):
@@ -305,10 +340,7 @@
     planes = planes + [lax.ppermute(p, "sector", along_sector(0, 1)) for p in planes]
     own, wave = choose(meta, own_half(mine), planes)
     parts = far_half(meta, mine, theirs, own, wave, right_blocks)
-    result = parts[0]
-    for d in (2, 1, 3):
-        result = result + lax.ppermute(parts[d], "table", along_table(d, 0))
-    return result
+    return finish(parts[0], [lax.ppermute(parts[d], "table", along_table(d, 0)) for d in (2, 1, 3)])
 
 
 def solution(mesh):

time: 53 us -> 50 us (0.943)
  the two profiles are of different devices: /device:TPU:1 before, /device:TPU:0 now
where the time goes in v4:
time: 50 us; the launch traced here: 49.6 us
  starting transfers between devices  23.5 us (47%)
  waiting for transfers between devices  14.8 us (30%)
  Pallas kernels  10.7 us (21%)
    ppermute x3, waiting for transfers between devices, local(): planes[e] = lax.ppermute(planes[0], 'sector', along_sector(e, 0))  11.2 us
    all_to_all x1, starting transfers between devices, local(): mine = lax.all_to_all(sent, 'table', 0, 0).reshape(TABS * SIDE * SIDE, SENT)  6.66 us
    ppermute x3, starting transfers between devices, local(): lines[d] = lax.ppermute(wave_blocks, 'table', along_table(0, d))  5.74 us
    ppermute x3, starting transfers between devices, local(): lax.ppermute(parts[d], 'table', along_table(d, 0))  5.66 us
    ppermute x3, starting transfers between devices, local(): planes[e] = lax.ppermute(planes[0], 'sector', along_sector(e, 0))  5.37 us
    pallas_call x1, Pallas kernels, far_half(): pl.pallas_call(far_kernel, in_specs=[pl.BlockSpec(memory_space=pltpu.SMEM...  3.72 us
    pallas_call x1, Pallas kernels, pack(): pl.pallas_call(pack_kernel, in_specs=[pl.BlockSpec(memory_space=pltpu.SME...  2.94 us
    ppermute x3, waiting for transfers between devices, local(): lax.ppermute(parts[d], 'table', along_table(d, 0))  2.33 us
  transfers between devices with their start and end apart: 15, of which 6 were waited for; matrix products, arithmetic and copies ran while one was open for 1% of the time, Pallas kernels for 13%

profile of v4, /device:TPU:0, one launch (start us, length us, event | category | flops | bytes accessed | tf_op | source)
XLA Modules:
  0.0 49.6 jit_solution(17253011139954734952)
XLA Ops:
  0.0 1.6 %collective-permute-start = (bf16[8,16,256]{2,1,0:T(8,128)(2,1)}, bf16[8,16,256]{2,1,0:T(8,128)(2,1)S(1)}, u32[]{:S(2)}, u32[]{:S(2)}) collective-permute-start(bf16[8,16,256]{2,1,0:T(8,128)(2,1)} %param.10), channel_id=1, source_target_pairs={{0,1},{1,2},{2,3},{3,0},{4,5},{5,6},{6,7},{7,4},{8,9},{9,10},{10,1... | collective-permute-start | bytes 196616 | tf_op jit(solution)/shard_map/ppermute | solution.py:329
  1.6 2.7 %collective-permute-start.1 = (bf16[8,16,256]{2,1,0:T(8,128)(2,1)}, bf16[8,16,256]{2,1,0:T(8,128)(2,1)S(1)}, u32[]{:S(2)}, u32[]{:S(2)}) collective-permute-start(bf16[8,16,256]{2,1,0:T(8,128)(2,1)} %param.10), channel_id=1, source_target_pairs={{0,2},{1,3},{2,0},{3,1},{4,6},{5,7},{6,4},{7,5},{8,10},{9,11},{10,... | collective-permute-start | bytes 196616 | tf_op jit(solution)/shard_map/ppermute | solution.py:329
  4.3 1.4 %collective-permute-start.2 = (bf16[8,16,256]{2,1,0:T(8,128)(2,1)}, bf16[8,16,256]{2,1,0:T(8,128)(2,1)S(1)}, u32[]{:S(2)}, u32[]{:S(2)}) collective-permute-start(bf16[8,16,256]{2,1,0:T(8,128)(2,1)} %param.10), channel_id=1, source_target_pairs={{0,3},{1,0},{2,1},{3,2},{4,7},{5,4},{6,5},{7,6},{8,11},{9,8},{10,9... | collective-permute-start | bytes 196616 | tf_op jit(solution)/shard_map/ppermute | solution.py:329
  5.7 2.9 %pack.1 = bf16[4,4,16,2432]{3,2,1,0:T(8,128)(2,1)} custom-call(s32[1]{0:T(128)} %bitcast.meta, bf16[16,4,64,256]{3,2,1,0:T(8,128)(2,1)} %bitcast.19, s32[1,192]{1,0:T(1,128)} %bitcast.24, s32[1,192]{1,0:T(1,128)} %bitcast.25, s32[1,192]{1,0:T(1,128)} %bitcast.26, s32[1,192]{1,0:T(1,128)} %bitcast.27), custom_call_target="tpu_custom_call" | custom-call | tf_op jit(solution)/shard_map/pack/pallas_call | solution.py:107
  8.7 0.0 copy-start.1
  8.7 0.0 copy-start.3
  8.7 0.0 copy-start.2
  8.7 0.0 copy-start.4
  8.7 0.0 collective-permute-done
  8.7 0.0 collective-permute-done.1
  8.8 0.0 collective-permute-done.2
  8.8 6.7 %all-to-all-start = ((bf16[16,16,2432]{2,1,0:T(8,128)(2,1)}), bf16[16,16,2432]{2,1,0:T(8,128)(2,1)S(1)}, u32[]{:S(2)}, u32[]{:S(2)}) async-start(bf16[16,16,2432]{2,1,0:T(8,128)(2,1)} %bitcast.18), calls=%async_computation | async-start | bytes 2490368 | tf_op jit(solution)/shard_map/all_to_all | solution.py:333
  15.4 0.0 copy-done.1
  15.5 4.1 %collective-permute-start.6 = (bf16[4,8,16,256]{3,2,1,0:T(8,128)(2,1)S(1)}, bf16[4,8,16,256]{3,2,1,0:T(8,128)(2,1)S(1)}, u32[]{:S(2)}, u32[]{:S(2)}) collective-permute-start(bf16[4,8,16,256]{3,2,1,0:T(8,128)(2,1)S(1)} %pad_maximum_fusion.refs_0_), channel_id=1, source_target_pairs={{0,96},{16,112},{32,0},{48,16},{64,32},{80,48},{96,64},{112,80},{1... | collective-permute-start | bytes 786440 | tf_op jit(solution)/shard_map/ppermute | solution.py:338
  19.6 0.0 collective-permute-start.4
  19.6 1.3 %collective-permute-start.5 = (bf16[4,8,16,256]{3,2,1,0:T(8,128)(2,1)S(1)}, bf16[4,8,16,256]{3,2,1,0:T(8,128)(2,1)S(1)}, u32[]{:S(2)}, u32[]{:S(2)}) collective-permute-start(bf16[4,8,16,256]{3,2,1,0:T(8,128)(2,1)S(1)} %pad_maximum_fusion.refs_0_), channel_id=1, source_target_pairs={{0,32},{16,48},{32,64},{48,80},{64,96},{80,112},{96,0},{112,16},{1... | collective-permute-start | bytes 786440 | tf_op jit(solution)/shard_map/ppermute | solution.py:338
  20.9 0.0 copy-done.3
  20.9 0.1 copy.13
  21.0 0.1 reshape.28
  21.0 0.0 copy-done.2
  21.0 0.1 copy.14
  21.1 0.1 reshape.29
  21.2 0.1 concatenate.3.meta
  21.3 0.0 collective-permute-start.7
  21.3 7.7 %collective-permute-done.6.refs_3_ = bf16[4,8,16,256]{3,2,1,0:T(8,128)(2,1)S(1)} collective-permute-done((bf16[4,8,16,256]{3,2,1,0:T(8,128)(2,1)S(1)}, bf16[4,8,16,256]{3,2,1,0:T(8,128)(2,1)S(1)}, u32[]{:S(2)}, u32[]{:S(2)}) %collective-permute-start.6) | collective-permute-done | bytes 262176 | tf_op jit(solution)/shard_map/ppermute | solution.py:338
  29.1 0.0 collective-permute-start.10
  29.1 1.0 %collective-permute-done.4.refs_1_ = bf16[4,8,16,256]{3,2,1,0:T(8,128)(2,1)S(1)} collective-permute-done((bf16[4,8,16,256]{3,2,1,0:T(8,128)(2,1)S(1)}, bf16[4,8,16,256]{3,2,1,0:T(8,128)(2,1)S(1)}, u32[]{:S(2)}, u32[]{:S(2)}) %collective-permute-start.4) | collective-permute-done | bytes 262176 | tf_op jit(solution)/shard_map/ppermute | solution.py:338
  30.1 0.0 collective-permute-start.8
  30.1 2.4 %collective-permute-done.5.refs_2_ = bf16[4,8,16,256]{3,2,1,0:T(8,128)(2,1)S(1)} collective-permute-done((bf16[4,8,16,256]{3,2,1,0:T(8,128)(2,1)S(1)}, bf16[4,8,16,256]{3,2,1,0:T(8,128)(2,1)S(1)}, u32[]{:S(2)}, u32[]{:S(2)}) %collective-permute-start.5) | collective-permute-done | bytes 262176 | tf_op jit(solution)/shard_map/ppermute | solution.py:338
  32.5 0.0 collective-permute-start.9
  32.5 1.3 %all-to-all-done = bf16[16,16,2432]{2,1,0:T(8,128)(2,1)S(1)} async-done(((bf16[16,16,2432]{2,1,0:T(8,128)(2,1)}), bf16[16,16,2432]{2,1,0:T(8,128)(2,1)S(1)}, u32[]{:S(2)}, u32[]{:S(2)}) %all-to-all-start) | async-done | bytes 1245216 | tf_op jit(solution)/shard_map/all_to_all | solution.py:333
  33.8 0.0 collective-permute-start.3
  33.8 1.7 %own_half.1 = (bf16[512,1536]{1,0:T(8,128)(2,1)S(1)}, bf16[512,1536]{1,0:T(8,128)(2,1)S(1)}) custom-call(bf16[256,2432]{1,0:T(8,128)(2,1)S(1)} %bitcast.16), custom_call_target="tpu_custom_call" | custom-call | flops 99999997952 | bytes 1048576 | tf_op jit(solution)/shard_map/own_half/pallas_call | solution.py:174
  35.5 0.0 collective-permute-done.7.refs_4_
  35.5 0.0 collective-permute-done.10.refs_7_
  35.5 0.0 collective-permute-done.8.refs_5_
  35.5 0.0 collective-permute-done.9.refs_6_
  35.5 0.0 copy-start
  35.5 1.6 %choose.1 = (f32[512,256]{1,0:T(8,128)S(1)}, bf16[24,64,256]{2,1,0:T(8,128)(2,1)S(1)}) custom-call(s32[52]{0:T(128)S(1)} %concatenate.3.meta, bf16[512,1536]{1,0:T(8,128)(2,1)S(1)} %get-tuple-element.19.hi_ref, bf16[512,1536]{1,0:T(8,128)(2,1)S(1)} %get-tuple-element.20.lo_ref, bf16[4,8,16,256]{3,2,1,0:T(8,128)(2,1)S(1)} %pad_maximum_fusion.refs_0_, ...), custom_call_target="tpu_custom_call" | custom-call | flops 1000000000 | bytes 1048576 | tf_op jit(solution)/shard_map/choose/pallas_call | solution.py:203
  37.2 0.0 collective-permute-done.3.theirs
  37.2 3.7 %far_half.1 = (f32[8,16,256]{2,1,0:T(8,128)S(1)}, s16[9,16,256]{2,1,0:T(8,128)(2,1)S(1)}, s16[9,16,256]{2,1,0:T(8,128)(2,1)S(1)}, s16[9,16,256]{2,1,0:T(8,128)(2,1)S(1)}) custom-call(s32[52]{0:T(128)S(1)} %concatenate.3.meta, bf16[256,2432]{1,0:T(8,128)(2,1)S(1)} %bitcast.17, bf16[256,2432]{1,0:T(8,128)(2,1)S(1)} %collective-permute-done.3.theirs, ...), custom_call_target="tpu_custom_call" | custom-call | flops 4000000000 | bytes 1048576 | tf_op jit(solution)/shard_map/far_half/pallas_call | solution.py:256
  40.9 2.4 %collective-permute-start.11 = (s16[9,16,256]{2,1,0:T(8,128)(2,1)S(1)}, s16[9,16,256]{2,1,0:T(8,128)(2,1)S(1)}, u32[]{:S(2)}, u32[]{:S(2)}) collective-permute-start(s16[9,16,256]{2,1,0:T(8,128)(2,1)S(1)} %get-tuple-element.28), channel_id=1, source_target_pairs={{0,8},{1,9},{2,10},{3,11},{4,12},{5,13},{6,14},{7,15},{8,0},{9,1},... | collective-permute-start | bytes 221192 | tf_op jit(solution)/shard_map/ppermute | solution.py:343
  43.3 0.6 %collective-permute-start.12 = (s16[9,16,256]{2,1,0:T(8,128)(2,1)S(1)}, s16[9,16,256]{2,1,0:T(8,128)(2,1)S(1)}, u32[]{:S(2)}, u32[]{:S(2)}) collective-permute-start(s16[9,16,256]{2,1,0:T(8,128)(2,1)S(1)} %get-tuple-element.29), channel_id=1, source_target_pairs={{0,4},{1,5},{2,6},{3,7},{4,8},{5,9},{6,10},{7,11},{8,12},{9,13},{1... | collective-permute-start | bytes 221192 | tf_op jit(solution)/shard_map/ppermute | solution.py:343
  43.9 2.7 %collective-permute-start.13 = (s16[9,16,256]{2,1,0:T(8,128)(2,1)S(1)}, s16[9,16,256]{2,1,0:T(8,128)(2,1)S(1)}, u32[]{:S(2)}, u32[]{:S(2)}) collective-permute-start(s16[9,16,256]{2,1,0:T(8,128)(2,1)S(1)} %get-tuple-element.30), channel_id=1, source_target_pairs={{0,12},{1,13},{2,14},{3,15},{4,0},{5,1},{6,2},{7,3},{8,4},{9,5},{1... | collective-permute-start | bytes 221192 | tf_op jit(solution)/shard_map/ppermute | solution.py:343
  46.6 1.0 %collective-permute-done.11.refs_0_ = s16[9,16,256]{2,1,0:T(8,128)(2,1)S(1)} collective-permute-done((s16[9,16,256]{2,1,0:T(8,128)(2,1)S(1)}, s16[9,16,256]{2,1,0:T(8,128)(2,1)S(1)}, u32[]{:S(2)}, u32[]{:S(2)}) %collective-permute-start.11) | collective-permute-done | bytes 73760 | tf_op jit(solution)/shard_map/ppermute | solution.py:343
  47.6 1.3 %collective-permute-done.12.refs_1_ = s16[9,16,256]{2,1,0:T(8,128)(2,1)S(1)} collective-permute-done((s16[9,16,256]{2,1,0:T(8,128)(2,1)S(1)}, s16[9,16,256]{2,1,0:T(8,128)(2,1)S(1)}, u32[]{:S(2)}, u32[]{:S(2)}) %collective-permute-start.12) | collective-permute-done | bytes 73760 | tf_op jit(solution)/shard_map/ppermute | solution.py:343
  48.9 0.0 collective-permute-done.13.refs_2_
  48.9 0.7 %finish.1 = f32[8,16,256]{2,1,0:T(8,128)} custom-call(f32[8,16,256]{2,1,0:T(8,128)S(1)} %get-tuple-element.27.own, s16[9,16,256]{2,1,0:T(8,128)(2,1)S(1)} %collective-permute-done.11.refs_0_, s16[9,16,256]{2,1,0:T(8,128)(2,1)S(1)} %collective-permute-done.12.refs_1_, s16[9,16,256]{2,1,0:T(8,128)(2,1)S(1)} %collective-permute-done.13.refs_2_), custom_call_target="tpu_custom_call" | custom-call | tf_op jit(solution)/shard_map/finish/pallas_call | solution.py:286
  (3 shorter events, 0.0 us)
Async XLA Ops:
  0.0 8.7 %collective-permute-start = (bf16[8,16,256]{2,1,0:T(8,128)(2,1)}, bf16[8,16,256]{2,1,0:T(8,128)(2,1)S(1)}, u32[]{:S(2)}, u32[]{:S(2)}) collective-permute-start(bf16[8,16,256]{2,1,0:T(8,128)(2,1)} %param.10), channel_id=1, source_target_pairs={{0,1},{1,2},{2,3},{3,0},{4,5},{5,6},{6,7},{7,4},{8,9},{9,10},{10,1... | collective-permute-start | bytes 196616 | tf_op jit(solution)/shard_map/ppermute | solution.py:329
  1.6 7.2 %collective-permute-start.1 = (bf16[8,16,256]{2,1,0:T(8,128)(2,1)}, bf16[8,16,256]{2,1,0:T(8,128)(2,1)S(1)}, u32[]{:S(2)}, u32[]{:S(2)}) collective-permute-start(bf16[8,16,256]{2,1,0:T(8,128)(2,1)} %param.10), channel_id=1, source_target_pairs={{0,2},{1,3},{2,0},{3,1},{4,6},{5,7},{6,4},{7,5},{8,10},{9,11},{10,... | collective-permute-start | bytes 196616 | tf_op jit(solution)/shard_map/ppermute | solution.py:329
  4.3 4.5 %collective-permute-start.2 = (bf16[8,16,256]{2,1,0:T(8,128)(2,1)}, bf16[8,16,256]{2,1,0:T(8,128)(2,1)S(1)}, u32[]{:S(2)}, u32[]{:S(2)}) collective-permute-start(bf16[8,16,256]{2,1,0:T(8,128)(2,1)} %param.10), channel_id=1, source_target_pairs={{0,3},{1,0},{2,1},{3,2},{4,7},{5,4},{6,5},{7,6},{8,11},{9,8},{10,9... | collective-permute-start | bytes 196616 | tf_op jit(solution)/shard_map/ppermute | solution.py:329
  8.7 6.8 %copy-start.1 = (bf16[8,16,256]{2,1,0:T(8,128)(2,1)S(1)}, bf16[8,16,256]{2,1,0:T(8,128)(2,1)}, u32[]{:S(2)}) copy-start(bf16[8,16,256]{2,1,0:T(8,128)(2,1)} %param.10) | copy-start | bytes 196612
  8.7 12.2 %copy-start.3 = (s32[8,2]{0,1:T(2,128)S(1)}, s32[8,2]{0,1:T(2,128)}, u32[]{:S(2)}) copy-start(s32[8,2]{0,1:T(2,128)} %param.14) | copy-start | bytes 196
  8.7 12.3 %copy-start.2 = (s32[1,8,3]{1,0,2:T(1,128)S(1)}, s32[1,8,3]{1,0,2:T(1,128)}, u32[]{:S(2)}) copy-start(s32[1,8,3]{1,0,2:T(1,128)} %param.15) | copy-start | bytes 292
  8.7 12.5 %copy-start.4 = (s32[8]{0:T(128)S(1)}, s32[8]{0:T(128)}, u32[]{:S(2)}) copy-start(s32[8]{0:T(128)} %param.13) | copy-start | bytes 100
  8.8 25.0 %all-to-all-start = ((bf16[16,16,2432]{2,1,0:T(8,128)(2,1)}), bf16[16,16,2432]{2,1,0:T(8,128)(2,1)S(1)}, u32[]{:S(2)}, u32[]{:S(2)}) async-start(bf16[16,16,2432]{2,1,0:T(8,128)(2,1)} %bitcast.18), calls=%async_computation | async-start | bytes 2490368 | tf_op jit(solution)/shard_map/all_to_all | solution.py:333
  15.5 13.6 %collective-permute-start.6 = (bf16[4,8,16,256]{3,2,1,0:T(8,128)(2,1)S(1)}, bf16[4,8,16,256]{3,2,1,0:T(8,128)(2,1)S(1)}, u32[]{:S(2)}, u32[]{:S(2)}) collective-permute-start(bf16[4,8,16,256]{3,2,1,0:T(8,128)(2,1)S(1)} %pad_maximum_fusion.refs_0_), channel_id=1, source_target_pairs={{0,96},{16,112},{32,0},{48,16},{64,32},{80,48},{96,64},{112,80},{1... | collective-permute-start | bytes 786440 | tf_op jit(solution)/shard_map/ppermute | solution.py:338
  19.6 10.4 %collective-permute-start.4 = (bf16[4,8,16,256]{3,2,1,0:T(8,128)(2,1)S(1)}, bf16[4,8,16,256]{3,2,1,0:T(8,128)(2,1)S(1)}, u32[]{:S(2)}, u32[]{:S(2)}) collective-permute-start(bf16[4,8,16,256]{3,2,1,0:T(8,128)(2,1)S(1)} %pad_maximum_fusion.refs_0_), channel_id=1, source_target_pairs={{0,64},{16,80},{32,96},{48,112},{64,0},{80,16},{96,32},{112,48},{1... | collective-permute-start | bytes 786440 | tf_op jit(solution)/shard_map/ppermute | solution.py:338
  19.6 12.9 %collective-permute-start.5 = (bf16[4,8,16,256]{3,2,1,0:T(8,128)(2,1)S(1)}, bf16[4,8,16,256]{3,2,1,0:T(8,128)(2,1)S(1)}, u32[]{:S(2)}, u32[]{:S(2)}) collective-permute-start(bf16[4,8,16,256]{3,2,1,0:T(8,128)(2,1)S(1)} %pad_maximum_fusion.refs_0_), channel_id=1, source_target_pairs={{0,32},{16,48},{32,64},{48,80},{64,96},{80,112},{96,0},{112,16},{1... | collective-permute-start | bytes 786440 | tf_op jit(solution)/shard_map/ppermute | solution.py:338
  21.3 14.2 %collective-permute-start.7 = (bf16[4,8,16,256]{3,2,1,0:T(8,128)(2,1)S(1)}, bf16[4,8,16,256]{3,2,1,0:T(8,128)(2,1)S(1)}, u32[]{:S(2)}, u32[]{:S(2)}) collective-permute-start(bf16[4,8,16,256]{3,2,1,0:T(8,128)(2,1)S(1)} %pad_maximum_fusion.refs_0_), channel_id=1, source_target_pairs={{0,16},{16,0},{32,48},{48,32},{64,80},{80,64},{96,112},{112,96},{1... | collective-permute-start | bytes 786440 | tf_op jit(solution)/shard_map/ppermute | solution.py:340
  29.1 6.4 %collective-permute-start.10 = (bf16[4,8,16,256]{3,2,1,0:T(8,128)(2,1)S(1)}, bf16[4,8,16,256]{3,2,1,0:T(8,128)(2,1)S(1)}, u32[]{:S(2)}, u32[]{:S(2)}) collective-permute-start(bf16[4,8,16,256]{3,2,1,0:T(8,128)(2,1)S(1)} %collective-permute-done.6.refs_3_), channel_id=1, source_target_pairs={{0,16},{16,0},{32,48},{48,32},{64,80},{80,64},{96,112},{112,96},{1... | collective-permute-start | bytes 786440 | tf_op jit(solution)/shard_map/ppermute | solution.py:340
  30.1 5.5 %collective-permute-start.8 = (bf16[4,8,16,256]{3,2,1,0:T(8,128)(2,1)S(1)}, bf16[4,8,16,256]{3,2,1,0:T(8,128)(2,1)S(1)}, u32[]{:S(2)}, u32[]{:S(2)}) collective-permute-start(bf16[4,8,16,256]{3,2,1,0:T(8,128)(2,1)S(1)} %collective-permute-done.4.refs_1_), channel_id=1, source_target_pairs={{0,16},{16,0},{32,48},{48,32},{64,80},{80,64},{96,112},{112,96},{1... | collective-permute-start | bytes 786440 | tf_op jit(solution)/shard_map/ppermute | solution.py:340
  32.5 3.0 %collective-permute-start.9 = (bf16[4,8,16,256]{3,2,1,0:T(8,128)(2,1)S(1)}, bf16[4,8,16,256]{3,2,1,0:T(8,128)(2,1)S(1)}, u32[]{:S(2)}, u32[]{:S(2)}) collective-permute-start(bf16[4,8,16,256]{3,2,1,0:T(8,128)(2,1)S(1)} %collective-permute-done.5.refs_2_), channel_id=1, source_target_pairs={{0,16},{16,0},{32,48},{48,32},{64,80},{80,64},{96,112},{112,96},{1... | collective-permute-start | bytes 786440 | tf_op jit(solution)/shard_map/ppermute | solution.py:340
  33.8 3.4 %collective-permute-start.3 = (bf16[256,2432]{1,0:T(8,128)(2,1)S(1)}, bf16[256,2432]{1,0:T(8,128)(2,1)S(1)}, u32[]{:S(2)}, u32[]{:S(2)}) collective-permute-start(bf16[256,2432]{1,0:T(8,128)(2,1)S(1)} %bitcast.15), channel_id=1, source_target_pairs={{0,16},{16,0},{32,48},{48,32},{64,80},{80,64},{96,112},{112,96},{1... | collective-permute-start | bytes 3735560 | tf_op jit(solution)/shard_map/ppermute | solution.py:334
  35.5 1.6 %copy-start = (bf16[8,256,256]{2,1,0:T(8,128)(2,1)S(1)}, bf16[8,256,256]{2,1,0:T(8,128)(2,1)}, u32[]{:S(2)}) copy-start(bf16[8,256,256]{2,1,0:T(8,128)(2,1)} %right.1) | copy-start | bytes 3145732
  40.9 6.6 %collective-permute-start.11 = (s16[9,16,256]{2,1,0:T(8,128)(2,1)S(1)}, s16[9,16,256]{2,1,0:T(8,128)(2,1)S(1)}, u32[]{:S(2)}, u32[]{:S(2)}) collective-permute-start(s16[9,16,256]{2,1,0:T(8,128)(2,1)S(1)} %get-tuple-element.28), channel_id=1, source_target_pairs={{0,8},{1,9},{2,10},{3,11},{4,12},{5,13},{6,14},{7,15},{8,0},{9,1},... | collective-permute-start | bytes 221192 | tf_op jit(solution)/shard_map/ppermute | solution.py:343
  43.3 5.6 %collective-permute-start.12 = (s16[9,16,256]{2,1,0:T(8,128)(2,1)S(1)}, s16[9,16,256]{2,1,0:T(8,128)(2,1)S(1)}, u32[]{:S(2)}, u32[]{:S(2)}) collective-permute-start(s16[9,16,256]{2,1,0:T(8,128)(2,1)S(1)} %get-tuple-element.29), channel_id=1, source_target_pairs={{0,4},{1,5},{2,6},{3,7},{4,8},{5,9},{6,10},{7,11},{8,12},{9,13},{1... | collective-permute-start | bytes 221192 | tf_op jit(solution)/shard_map/ppermute | solution.py:343
  43.9 5.0 %collective-permute-start.13 = (s16[9,16,256]{2,1,0:T(8,128)(2,1)S(1)}, s16[9,16,256]{2,1,0:T(8,128)(2,1)S(1)}, u32[]{:S(2)}, u32[]{:S(2)}) collective-permute-start(s16[9,16,256]{2,1,0:T(8,128)(2,1)S(1)} %get-tuple-element.30), channel_id=1, source_target_pairs={{0,12},{1,13},{2,14},{3,15},{4,0},{5,1},{6,2},{7,3},{8,4},{9,5},{1... | collective-permute-start | bytes 221192 | tf_op jit(solution)/shard_map/ppermute | solution.py:343

commit v5 on v4

--- a/solution.py
+++ b/solution.py
@@ -28,6 +28,7 @@
 SIZE = ENV + SLOTS
 FETCH = SIZE + SLOTS // 2
 LISTED = 3
+CHUNK = 256
 LIMIT = 32700.0
 STEP = SLOTS * ROWS
 X_ORDER = (2, 1, 3)
@@ -57,29 +58,28 @@
     def hand(x):
         return pltpu.make_async_copy(ready.at[x], out_ref.at[:, x], out_sems.at[x])
 
+    for x in range(SIDE):
+        for u in range(2):
+            fetch(x, u).start()
     copies = []
     for n, ref in enumerate((pick_in, tab_in, slot_in, live_in)):
         copies.append(pltpu.make_async_copy(ref, lists.at[n], list_sems.at[n]))
         copies[n].start()
-    for x in range(SIDE):
-        for u in range(2):
-            fetch(x, u).start()
-    for copy in copies:
-        copy.wait()
-
-    terms = pick_in.shape[1]
-    tab_hot = (lax.broadcasted_iota(jnp.int32, (TABS, terms), 0) == lists[1]) & (lists[3] > 0)
-    pair = lists[2] * PICKS + lists[0]
-    pair_hot = lax.broadcasted_iota(jnp.int32, (PAIRS, terms), 0) == pair
-    counts = lax.dot_general(
-        tab_hot.astype(F32).astype(BF),
-        pair_hot.astype(F32).astype(BF),
-        (((1,), (1,)), ((), ())),
-        preferred_element_type=F32,
-    ).astype(BF)
-    for y in range(SIDE):
-        for x in range(SIDE):
-            ready[x, y, :, SHARE:SENT] = counts
+    def count():
+        for copy in copies:
+            copy.wait()
+
+        terms = pick_in.shape[1]
+        tab_hot = (lax.broadcasted_iota(jnp.int32, (TABS, terms), 0) == lists[1]) & (lists[3] > 0)
+        pair = lists[2] * PICKS + lists[0]
+        pair_hot = lax.broadcasted_iota(jnp.int32, (PAIRS, terms), 0) == pair
+        counts = lax.dot_general(
+            tab_hot.astype(F32).astype(BF),
+            pair_hot.astype(F32).astype(BF),
+            (((1,), (1,)), ((), ())),
+            preferred_element_type=F32,
+        ).astype(BF)
+        return counts
 
     low = lax.broadcasted_iota(jnp.int32, (TABS, 128), 1) < 64
     for x in range(SIDE):
@@ -89,6 +89,10 @@
                 block = held[x, u, t].astype(F32)
                 for k in range(2):
                     rows[k, u, t * ROW_PITCH : t * ROW_PITCH + ROWS, :] = block[:, k * 128 : k * 128 + 128]
+        if x == 0:
+            counts = count()
+        for y in range(SIDE):
+            ready[x, y, :, SHARE:SENT] = counts
         for q in range(ROWS):
             lanes = slice(q * 128, q * 128 + 128)
             for k in range(2):
@@ -139,7 +143,7 @@
             sums[start : start + PAIRS, :] = part[:, k * 128 : k * 128 + 128]
     low = lax.broadcasted_iota(jnp.int32, (ROWS, 128), 1) < 64
 
-    def one(s, carry):
+    for s in range(SLOTS):
         for k in range(PICKS // 2):
             row = s * PICKS + 2 * k
             a = sums[pl.ds(row, ROWS, stride=PITCH), :]
@@ -147,22 +151,15 @@
             mixed = swap_halves(jnp.where(low, b, a))
             for u, value in enumerate((jnp.where(low, a, mixed), jnp.where(low, mixed, b))):
                 hi = value.astype(BF)
-                place = pl.ds(pl.multiple_of(u * STEP + s * ROWS, ROWS), ROWS)
+                place = slice((2 * s + u) * ROWS, (2 * s + u + 1) * ROWS)
                 hi_ref[place, k * 128 : k * 128 + 128] = hi
                 lo_ref[place, k * 128 : k * 128 + 128] = (value - hi.astype(F32)).astype(BF)
-        return carry
-
-    lax.fori_loop(0, SLOTS, one, 0, unroll=4)
-
-
-def product(hi_ref, lo_ref, wave):
-    part = jnp.dot(hi_ref[...], wave[...], preferred_element_type=F32)
-    return part + jnp.dot(lo_ref[...], wave[...], preferred_element_type=F32)
-
-
-def multiply(hi_ref, lo_ref, weights):
-    part = jnp.dot(hi_ref[...], weights, preferred_element_type=F32)
-    return part + jnp.dot(lo_ref[...], weights, preferred_element_type=F32)
+
+
+def multiply(hi_ref, lo_ref, weights, n):
+    rows = slice(n * CHUNK, (n + 1) * CHUNK)
+    part = jnp.dot(hi_ref[rows, :], weights, preferred_element_type=F32)
+    return part + jnp.dot(lo_ref[rows, :], weights, preferred_element_type=F32)
 
 
 def own_kernel(mine, hi_ref, lo_ref, sums):
@@ -195,7 +192,9 @@
                 for d in range(SIDE):
                     rows = pl.ds(pl.multiple_of(lax.rem(x - d + SIDE, SIDE) * ROWS, ROWS), ROWS)
                     wave[pick, rows, :] = planes[c * SIDE + place][d, piece]
-    out_ref[...] = multiply(hi_ref, lo_ref, wave[...].reshape(DEPTH, WIDTH))
+    weights = wave[...].reshape(DEPTH, WIDTH)
+    for n in range(2 * STEP // CHUNK):
+        out_ref[n * CHUNK : (n + 1) * CHUNK, :] = multiply(hi_ref, lo_ref, weights, n)
 
 
 def choose(meta, own, planes):
@@ -216,25 +215,29 @@
     codes[...] = jnp.zeros_like(codes)
     spread(mine, theirs, sums, hi_ref, lo_ref)
     weights = wave[...].reshape(DEPTH, WIDTH)
-    for u in range(2):
-        rows = slice(u * STEP, (u + 1) * STEP)
-        channel[lax.rem(2 * u + core - y + SIDE, SIDE)] = own[rows, :]
-        part = jnp.dot(hi_ref[rows, :], weights, preferred_element_type=F32)
-        part = part + jnp.dot(lo_ref[rows, :], weights, preferred_element_type=F32)
-        channel[lax.rem(2 * u + 1 - core - y + SIDE, SIDE)] = part
+    for s in range(SLOTS):
+        for u in range(2):
+            step = lax.rem(2 * u + core - y + SIDE, SIDE)
+            channel[step, s * ROWS : (s + 1) * ROWS, :] = own[(2 * s + u) * ROWS : (2 * s + u + 1) * ROWS, :]
+    for n in range(2 * STEP // CHUNK):
+        part = multiply(hi_ref, lo_ref, weights, n)
+        for m in range(CHUNK // ROWS):
+            s, u = divmod(n * (CHUNK // ROWS) + m, 2)
+            step = lax.rem(2 * u + 1 - core - y + SIDE, SIDE)
+            channel[step, s * ROWS : (s + 1) * ROWS, :] = part[m * ROWS : (m + 1) * ROWS]
     columns = lax.broadcasted_iota(jnp.int32, (ROWS, WIDTH), 1)
     lines = lax.broadcasted_iota(jnp.int32, (ROWS, WIDTH), 0)
     reach = [jnp.maximum(lines + (lax.rem(y + d, SIDE) * SIDE + x) * ROWS, columns) for d in range(SIDE)]
     for o in range(SLOTS // 2):
-        result = None
+        hi, lo, env = [], [], []
         for s in (2 * o, 2 * o + 1):
-            env = right[meta[ENV + s]]
+            env.append(right[meta[ENV + s]])
             value = channel[:, s * ROWS : (s + 1) * ROWS, :].reshape(HALF, WIDTH)
-            hi = value.astype(BF)
-            lo = (value - hi.astype(F32)).astype(BF)
-            part = jnp.dot(jnp.concatenate([hi, lo], axis=0), env, preferred_element_type=F32)
-            part = part[:HALF] + part[HALF:]
-            result = part if result is None else result + part
+            hi.append(value.astype(BF))
+            lo.append((value - hi[-1].astype(F32)).astype(BF))
+        both = jnp.concatenate([jnp.concatenate(hi, axis=1), jnp.concatenate(lo, axis=1)], axis=0)
+        result = jnp.dot(both, jnp.concatenate(env, axis=0), preferred_element_type=F32)
+        result = result[:HALF] + result[HALF:]
         size = meta[SIZE + o]
         for d, ref in enumerate((s0, s1, s2, s3)):
             part = jnp.where(reach[d] < size, result[d * ROWS : (d + 1) * ROWS], 0.0)

time: 50 us -> 49.3 us (0.986)
  Pallas kernels: 10.7 us -> 9.86 us
  transfers between devices with their start and end apart: 15 -> 15, of which waited for: 6 -> 7; matrix products, arithmetic and copies ran while one was open for 1% -> 1% of each run, Pallas kernels for 13% -> 12%
where the time goes in v5:
time: 49.3 us; the launch traced here: 48.9 us
  starting transfers between devices  23.5 us (48%)
  waiting for transfers between devices  15 us (30%)
  Pallas kernels  9.86 us (20%)
    ppermute x3, waiting for transfers between devices, local(): planes[e] = lax.ppermute(planes[0], 'sector', along_sector(e, 0))  11.2 us
    all_to_all x1, starting transfers between devices, local(): mine = lax.all_to_all(sent, 'table', 0, 0).reshape(TABS * SIDE * SIDE, SENT)  6.66 us
    ppermute x3, starting transfers between devices, local(): lines[d] = lax.ppermute(wave_blocks, 'table', along_table(0, d))  5.74 us
    ppermute x3, starting transfers between devices, local(): lax.ppermute(parts[d], 'table', along_table(d, 0))  5.66 us
    ppermute x3, starting transfers between devices, local(): planes[e] = lax.ppermute(planes[0], 'sector', along_sector(e, 0))  5.37 us
    pallas_call x1, Pallas kernels, far_half(): pl.pallas_call(far_kernel, in_specs=[pl.BlockSpec(memory_space=pltpu.SMEM...  3.29 us
    pallas_call x1, Pallas kernels, pack(): pl.pallas_call(pack_kernel, in_specs=[pl.BlockSpec(memory_space=pltpu.SME...  2.82 us
    ppermute x3, waiting for transfers between devices, local(): lax.ppermute(parts[d], 'table', along_table(d, 0))  2.33 us
  transfers between devices with their start and end apart: 15, of which 7 were waited for; matrix products, arithmetic and copies ran while one was open for 1% of the time, Pallas kernels for 12%

profile of v5, /device:TPU:0, one launch (start us, length us, event | category | flops | bytes accessed | tf_op | source)
XLA Modules:
  0.0 48.9 jit_solution(9828374212418285903)
XLA Ops:
  0.0 1.6 %collective-permute-start = (bf16[8,16,256]{2,1,0:T(8,128)(2,1)}, bf16[8,16,256]{2,1,0:T(8,128)(2,1)S(1)}, u32[]{:S(2)}, u32[]{:S(2)}) collective-permute-start(bf16[8,16,256]{2,1,0:T(8,128)(2,1)} %param.10), channel_id=1, source_target_pairs={{0,1},{1,2},{2,3},{3,0},{4,5},{5,6},{6,7},{7,4},{8,9},{9,10},{10,1... | collective-permute-start | bytes 196616 | tf_op jit(solution)/shard_map/ppermute | solution.py:332
  1.6 2.7 %collective-permute-start.1 = (bf16[8,16,256]{2,1,0:T(8,128)(2,1)}, bf16[8,16,256]{2,1,0:T(8,128)(2,1)S(1)}, u32[]{:S(2)}, u32[]{:S(2)}) collective-permute-start(bf16[8,16,256]{2,1,0:T(8,128)(2,1)} %param.10), channel_id=1, source_target_pairs={{0,2},{1,3},{2,0},{3,1},{4,6},{5,7},{6,4},{7,5},{8,10},{9,11},{10,... | collective-permute-start | bytes 196616 | tf_op jit(solution)/shard_map/ppermute | solution.py:332
  4.3 1.4 %collective-permute-start.2 = (bf16[8,16,256]{2,1,0:T(8,128)(2,1)}, bf16[8,16,256]{2,1,0:T(8,128)(2,1)S(1)}, u32[]{:S(2)}, u32[]{:S(2)}) collective-permute-start(bf16[8,16,256]{2,1,0:T(8,128)(2,1)} %param.10), channel_id=1, source_target_pairs={{0,3},{1,0},{2,1},{3,2},{4,7},{5,4},{6,5},{7,6},{8,11},{9,8},{10,9... | collective-permute-start | bytes 196616 | tf_op jit(solution)/shard_map/ppermute | solution.py:332
  5.7 2.8 %pack.1 = bf16[4,4,16,2432]{3,2,1,0:T(8,128)(2,1)} custom-call(s32[1]{0:T(128)} %bitcast.meta, bf16[16,4,64,256]{3,2,1,0:T(8,128)(2,1)} %bitcast.19, s32[1,192]{1,0:T(1,128)} %bitcast.24, s32[1,192]{1,0:T(1,128)} %bitcast.25, s32[1,192]{1,0:T(1,128)} %bitcast.26, s32[1,192]{1,0:T(1,128)} %bitcast.27), custom_call_target="tpu_custom_call" | custom-call | tf_op jit(solution)/shard_map/pack/pallas_call | solution.py:111
  8.6 0.0 copy-start.1
  8.6 0.0 copy-start.3
  8.6 0.0 copy-start.2
  8.6 0.0 copy-start.4
  8.6 0.0 collective-permute-done
  8.6 0.0 collective-permute-done.1
  8.6 0.1 collective-permute-done.2
  8.8 6.7 %all-to-all-start = ((bf16[16,16,2432]{2,1,0:T(8,128)(2,1)}), bf16[16,16,2432]{2,1,0:T(8,128)(2,1)S(1)}, u32[]{:S(2)}, u32[]{:S(2)}) async-start(bf16[16,16,2432]{2,1,0:T(8,128)(2,1)} %bitcast.18), calls=%async_computation | async-start | bytes 2490368 | tf_op jit(solution)/shard_map/all_to_all | solution.py:336
  15.4 0.0 copy-done.1
  15.5 4.1 %collective-permute-start.6 = (bf16[4,8,16,256]{3,2,1,0:T(8,128)(2,1)S(1)}, bf16[4,8,16,256]{3,2,1,0:T(8,128)(2,1)S(1)}, u32[]{:S(2)}, u32[]{:S(2)}) collective-permute-start(bf16[4,8,16,256]{3,2,1,0:T(8,128)(2,1)S(1)} %pad_maximum_fusion.refs_0_), channel_id=1, source_target_pairs={{0,96},{16,112},{32,0},{48,16},{64,32},{80,48},{96,64},{112,80},{1... | collective-permute-start | bytes 786440 | tf_op jit(solution)/shard_map/ppermute | solution.py:341
  19.6 0.0 collective-permute-start.4
  19.6 1.3 %collective-permute-start.5 = (bf16[4,8,16,256]{3,2,1,0:T(8,128)(2,1)S(1)}, bf16[4,8,16,256]{3,2,1,0:T(8,128)(2,1)S(1)}, u32[]{:S(2)}, u32[]{:S(2)}) collective-permute-start(bf16[4,8,16,256]{3,2,1,0:T(8,128)(2,1)S(1)} %pad_maximum_fusion.refs_0_), channel_id=1, source_target_pairs={{0,32},{16,48},{32,64},{48,80},{64,96},{80,112},{96,0},{112,16},{1... | collective-permute-start | bytes 786440 | tf_op jit(solution)/shard_map/ppermute | solution.py:341
  20.9 0.0 copy-done.3
  20.9 0.1 copy.13
  21.0 0.1 reshape.28
  21.0 0.1 copy.14
  21.1 0.1 reshape.29
  21.2 0.1 concatenate.3.meta
  21.3 0.0 collective-permute-start.7
  21.3 7.7 %collective-permute-done.6.refs_3_ = bf16[4,8,16,256]{3,2,1,0:T(8,128)(2,1)S(1)} collective-permute-done((bf16[4,8,16,256]{3,2,1,0:T(8,128)(2,1)S(1)}, bf16[4,8,16,256]{3,2,1,0:T(8,128)(2,1)S(1)}, u32[]{:S(2)}, u32[]{:S(2)}) %collective-permute-start.6) | collective-permute-done | bytes 262176 | tf_op jit(solution)/shard_map/ppermute | solution.py:341
  29.1 0.0 collective-permute-start.10
  29.1 1.0 %collective-permute-done.4.refs_1_ = bf16[4,8,16,256]{3,2,1,0:T(8,128)(2,1)S(1)} collective-permute-done((bf16[4,8,16,256]{3,2,1,0:T(8,128)(2,1)S(1)}, bf16[4,8,16,256]{3,2,1,0:T(8,128)(2,1)S(1)}, u32[]{:S(2)}, u32[]{:S(2)}) %collective-permute-start.4) | collective-permute-done | bytes 262176 | tf_op jit(solution)/shard_map/ppermute | solution.py:341
  30.1 0.0 collective-permute-start.8
  30.1 2.4 %collective-permute-done.5.refs_2_ = bf16[4,8,16,256]{3,2,1,0:T(8,128)(2,1)S(1)} collective-permute-done((bf16[4,8,16,256]{3,2,1,0:T(8,128)(2,1)S(1)}, bf16[4,8,16,256]{3,2,1,0:T(8,128)(2,1)S(1)}, u32[]{:S(2)}, u32[]{:S(2)}) %collective-permute-start.5) | collective-permute-done | bytes 262176 | tf_op jit(solution)/shard_map/ppermute | solution.py:341
  32.5 0.0 collective-permute-start.9
  32.5 1.3 %all-to-all-done = bf16[16,16,2432]{2,1,0:T(8,128)(2,1)S(1)} async-done(((bf16[16,16,2432]{2,1,0:T(8,128)(2,1)}), bf16[16,16,2432]{2,1,0:T(8,128)(2,1)S(1)}, u32[]{:S(2)}, u32[]{:S(2)}) %all-to-all-start) | async-done | bytes 1245216 | tf_op jit(solution)/shard_map/all_to_all | solution.py:336
  33.8 0.0 collective-permute-start.3
  33.8 1.4 %own_half.1 = (bf16[512,1536]{1,0:T(8,128)(2,1)S(1)}, bf16[512,1536]{1,0:T(8,128)(2,1)S(1)}) custom-call(bf16[256,2432]{1,0:T(8,128)(2,1)S(1)} %bitcast.16), custom_call_target="tpu_custom_call" | custom-call | flops 99999997952 | bytes 1048576 | tf_op jit(solution)/shard_map/own_half/pallas_call | solution.py:171
  35.2 0.0 collective-permute-done.7.refs_4_
  35.2 0.0 collective-permute-done.10.refs_7_
  35.2 0.0 collective-permute-done.8.refs_5_
  35.3 0.0 collective-permute-done.9.refs_6_
  35.3 0.0 copy-start
  35.3 1.6 %choose.1 = (f32[512,256]{1,0:T(8,128)S(1)}, bf16[24,64,256]{2,1,0:T(8,128)(2,1)S(1)}) custom-call(s32[52]{0:T(128)S(1)} %concatenate.3.meta, bf16[512,1536]{1,0:T(8,128)(2,1)S(1)} %get-tuple-element.19.hi_ref, bf16[512,1536]{1,0:T(8,128)(2,1)S(1)} %get-tuple-element.20.lo_ref, bf16[4,8,16,256]{3,2,1,0:T(8,128)(2,1)S(1)} %pad_maximum_fusion.refs_0_, ...), custom_call_target="tpu_custom_call" | custom-call | flops 1000000000 | bytes 1048576 | tf_op jit(solution)/shard_map/choose/pallas_call | solution.py:202
  36.9 0.0 collective-permute-done.3.theirs
  36.9 0.0 copy-done
  36.9 3.3 %far_half.1 = (f32[8,16,256]{2,1,0:T(8,128)S(1)}, s16[9,16,256]{2,1,0:T(8,128)(2,1)S(1)}, s16[9,16,256]{2,1,0:T(8,128)(2,1)S(1)}, s16[9,16,256]{2,1,0:T(8,128)(2,1)S(1)}) custom-call(s32[52]{0:T(128)S(1)} %concatenate.3.meta, bf16[256,2432]{1,0:T(8,128)(2,1)S(1)} %bitcast.17, bf16[256,2432]{1,0:T(8,128)(2,1)S(1)} %collective-permute-done.3.theirs, ...), custom_call_target="tpu_custom_call" | custom-call | flops 4000000000 | bytes 1048576 | tf_op jit(solution)/shard_map/far_half/pallas_call | solution.py:259
  40.2 2.4 %collective-permute-start.11 = (s16[9,16,256]{2,1,0:T(8,128)(2,1)S(1)}, s16[9,16,256]{2,1,0:T(8,128)(2,1)S(1)}, u32[]{:S(2)}, u32[]{:S(2)}) collective-permute-start(s16[9,16,256]{2,1,0:T(8,128)(2,1)S(1)} %get-tuple-element.28), channel_id=1, source_target_pairs={{0,8},{1,9},{2,10},{3,11},{4,12},{5,13},{6,14},{7,15},{8,0},{9,1},... | collective-permute-start | bytes 221192 | tf_op jit(solution)/shard_map/ppermute | solution.py:346
  42.6 0.6 %collective-permute-start.12 = (s16[9,16,256]{2,1,0:T(8,128)(2,1)S(1)}, s16[9,16,256]{2,1,0:T(8,128)(2,1)S(1)}, u32[]{:S(2)}, u32[]{:S(2)}) collective-permute-start(s16[9,16,256]{2,1,0:T(8,128)(2,1)S(1)} %get-tuple-element.29), channel_id=1, source_target_pairs={{0,4},{1,5},{2,6},{3,7},{4,8},{5,9},{6,10},{7,11},{8,12},{9,13},{1... | collective-permute-start | bytes 221192 | tf_op jit(solution)/shard_map/ppermute | solution.py:346
  43.2 2.7 %collective-permute-start.13 = (s16[9,16,256]{2,1,0:T(8,128)(2,1)S(1)}, s16[9,16,256]{2,1,0:T(8,128)(2,1)S(1)}, u32[]{:S(2)}, u32[]{:S(2)}) collective-permute-start(s16[9,16,256]{2,1,0:T(8,128)(2,1)S(1)} %get-tuple-element.30), channel_id=1, source_target_pairs={{0,12},{1,13},{2,14},{3,15},{4,0},{5,1},{6,2},{7,3},{8,4},{9,5},{1... | collective-permute-start | bytes 221192 | tf_op jit(solution)/shard_map/ppermute | solution.py:346
  45.9 1.0 %collective-permute-done.11.refs_0_ = s16[9,16,256]{2,1,0:T(8,128)(2,1)S(1)} collective-permute-done((s16[9,16,256]{2,1,0:T(8,128)(2,1)S(1)}, s16[9,16,256]{2,1,0:T(8,128)(2,1)S(1)}, u32[]{:S(2)}, u32[]{:S(2)}) %collective-permute-start.11) | collective-permute-done | bytes 73760 | tf_op jit(solution)/shard_map/ppermute | solution.py:346
  46.9 1.3 %collective-permute-done.12.refs_1_ = s16[9,16,256]{2,1,0:T(8,128)(2,1)S(1)} collective-permute-done((s16[9,16,256]{2,1,0:T(8,128)(2,1)S(1)}, s16[9,16,256]{2,1,0:T(8,128)(2,1)S(1)}, u32[]{:S(2)}, u32[]{:S(2)}) %collective-permute-start.12) | collective-permute-done | bytes 73760 | tf_op jit(solution)/shard_map/ppermute | solution.py:346
  48.2 0.0 collective-permute-done.13.refs_2_
  48.2 0.7 %finish.1 = f32[8,16,256]{2,1,0:T(8,128)} custom-call(f32[8,16,256]{2,1,0:T(8,128)S(1)} %get-tuple-element.27.own, s16[9,16,256]{2,1,0:T(8,128)(2,1)S(1)} %collective-permute-done.11.refs_0_, s16[9,16,256]{2,1,0:T(8,128)(2,1)S(1)} %collective-permute-done.12.refs_1_, s16[9,16,256]{2,1,0:T(8,128)(2,1)S(1)} %collective-permute-done.13.refs_2_), custom_call_target="tpu_custom_call" | custom-call | tf_op jit(solution)/shard_map/finish/pallas_call | solution.py:289
  (3 shorter events, 0.0 us)
Async XLA Ops:
  0.0 8.6 %collective-permute-start = (bf16[8,16,256]{2,1,0:T(8,128)(2,1)}, bf16[8,16,256]{2,1,0:T(8,128)(2,1)S(1)}, u32[]{:S(2)}, u32[]{:S(2)}) collective-permute-start(bf16[8,16,256]{2,1,0:T(8,128)(2,1)} %param.10), channel_id=1, source_target_pairs={{0,1},{1,2},{2,3},{3,0},{4,5},{5,6},{6,7},{7,4},{8,9},{9,10},{10,1... | collective-permute-start | bytes 196616 | tf_op jit(solution)/shard_map/ppermute | solution.py:332
  1.6 7.1 %collective-permute-start.1 = (bf16[8,16,256]{2,1,0:T(8,128)(2,1)}, bf16[8,16,256]{2,1,0:T(8,128)(2,1)S(1)}, u32[]{:S(2)}, u32[]{:S(2)}) collective-permute-start(bf16[8,16,256]{2,1,0:T(8,128)(2,1)} %param.10), channel_id=1, source_target_pairs={{0,2},{1,3},{2,0},{3,1},{4,6},{5,7},{6,4},{7,5},{8,10},{9,11},{10,... | collective-permute-start | bytes 196616 | tf_op jit(solution)/shard_map/ppermute | solution.py:332
  4.3 4.5 %collective-permute-start.2 = (bf16[8,16,256]{2,1,0:T(8,128)(2,1)}, bf16[8,16,256]{2,1,0:T(8,128)(2,1)S(1)}, u32[]{:S(2)}, u32[]{:S(2)}) collective-permute-start(bf16[8,16,256]{2,1,0:T(8,128)(2,1)} %param.10), channel_id=1, source_target_pairs={{0,3},{1,0},{2,1},{3,2},{4,7},{5,4},{6,5},{7,6},{8,11},{9,8},{10,9... | collective-permute-start | bytes 196616 | tf_op jit(solution)/shard_map/ppermute | solution.py:332
  8.6 6.9 %copy-start.1 = (bf16[8,16,256]{2,1,0:T(8,128)(2,1)S(1)}, bf16[8,16,256]{2,1,0:T(8,128)(2,1)}, u32[]{:S(2)}) copy-start(bf16[8,16,256]{2,1,0:T(8,128)(2,1)} %param.10) | copy-start | bytes 196612
  8.6 12.3 %copy-start.3 = (s32[8,2]{0,1:T(2,128)S(1)}, s32[8,2]{0,1:T(2,128)}, u32[]{:S(2)}) copy-start(s32[8,2]{0,1:T(2,128)} %param.14) | copy-start | bytes 196
  8.6 12.4 %copy-start.2 = (s32[1,8,3]{1,0,2:T(1,128)S(1)}, s32[1,8,3]{1,0,2:T(1,128)}, u32[]{:S(2)}) copy-start(s32[1,8,3]{1,0,2:T(1,128)} %param.15) | copy-start | bytes 292
  8.6 12.6 %copy-start.4 = (s32[8]{0:T(128)S(1)}, s32[8]{0:T(128)}, u32[]{:S(2)}) copy-start(s32[8]{0:T(128)} %param.13) | copy-start | bytes 100
  8.8 25.0 %all-to-all-start = ((bf16[16,16,2432]{2,1,0:T(8,128)(2,1)}), bf16[16,16,2432]{2,1,0:T(8,128)(2,1)S(1)}, u32[]{:S(2)}, u32[]{:S(2)}) async-start(bf16[16,16,2432]{2,1,0:T(8,128)(2,1)} %bitcast.18), calls=%async_computation | async-start | bytes 2490368 | tf_op jit(solution)/shard_map/all_to_all | solution.py:336
  15.5 13.6 %collective-permute-start.6 = (bf16[4,8,16,256]{3,2,1,0:T(8,128)(2,1)S(1)}, bf16[4,8,16,256]{3,2,1,0:T(8,128)(2,1)S(1)}, u32[]{:S(2)}, u32[]{:S(2)}) collective-permute-start(bf16[4,8,16,256]{3,2,1,0:T(8,128)(2,1)S(1)} %pad_maximum_fusion.refs_0_), channel_id=1, source_target_pairs={{0,96},{16,112},{32,0},{48,16},{64,32},{80,48},{96,64},{112,80},{1... | collective-permute-start | bytes 786440 | tf_op jit(solution)/shard_map/ppermute | solution.py:341
  19.6 10.4 %collective-permute-start.4 = (bf16[4,8,16,256]{3,2,1,0:T(8,128)(2,1)S(1)}, bf16[4,8,16,256]{3,2,1,0:T(8,128)(2,1)S(1)}, u32[]{:S(2)}, u32[]{:S(2)}) collective-permute-start(bf16[4,8,16,256]{3,2,1,0:T(8,128)(2,1)S(1)} %pad_maximum_fusion.refs_0_), channel_id=1, source_target_pairs={{0,64},{16,80},{32,96},{48,112},{64,0},{80,16},{96,32},{112,48},{1... | collective-permute-start | bytes 786440 | tf_op jit(solution)/shard_map/ppermute | solution.py:341
  19.6 12.9 %collective-permute-start.5 = (bf16[4,8,16,256]{3,2,1,0:T(8,128)(2,1)S(1)}, bf16[4,8,16,256]{3,2,1,0:T(8,128)(2,1)S(1)}, u32[]{:S(2)}, u32[]{:S(2)}) collective-permute-start(bf16[4,8,16,256]{3,2,1,0:T(8,128)(2,1)S(1)} %pad_maximum_fusion.refs_0_), channel_id=1, source_target_pairs={{0,32},{16,48},{32,64},{48,80},{64,96},{80,112},{96,0},{112,16},{1... | collective-permute-start | bytes 786440 | tf_op jit(solution)/shard_map/ppermute | solution.py:341
  21.3 13.9 %collective-permute-start.7 = (bf16[4,8,16,256]{3,2,1,0:T(8,128)(2,1)S(1)}, bf16[4,8,16,256]{3,2,1,0:T(8,128)(2,1)S(1)}, u32[]{:S(2)}, u32[]{:S(2)}) collective-permute-start(bf16[4,8,16,256]{3,2,1,0:T(8,128)(2,1)S(1)} %pad_maximum_fusion.refs_0_), channel_id=1, source_target_pairs={{0,16},{16,0},{32,48},{48,32},{64,80},{80,64},{96,112},{112,96},{1... | collective-permute-start | bytes 786440 | tf_op jit(solution)/shard_map/ppermute | solution.py:343
  29.1 6.2 %collective-permute-start.10 = (bf16[4,8,16,256]{3,2,1,0:T(8,128)(2,1)S(1)}, bf16[4,8,16,256]{3,2,1,0:T(8,128)(2,1)S(1)}, u32[]{:S(2)}, u32[]{:S(2)}) collective-permute-start(bf16[4,8,16,256]{3,2,1,0:T(8,128)(2,1)S(1)} %collective-permute-done.6.refs_3_), channel_id=1, source_target_pairs={{0,16},{16,0},{32,48},{48,32},{64,80},{80,64},{96,112},{112,96},{1... | collective-permute-start | bytes 786440 | tf_op jit(solution)/shard_map/ppermute | solution.py:343
  30.1 5.2 %collective-permute-start.8 = (bf16[4,8,16,256]{3,2,1,0:T(8,128)(2,1)S(1)}, bf16[4,8,16,256]{3,2,1,0:T(8,128)(2,1)S(1)}, u32[]{:S(2)}, u32[]{:S(2)}) collective-permute-start(bf16[4,8,16,256]{3,2,1,0:T(8,128)(2,1)S(1)} %collective-permute-done.4.refs_1_), channel_id=1, source_target_pairs={{0,16},{16,0},{32,48},{48,32},{64,80},{80,64},{96,112},{112,96},{1... | collective-permute-start | bytes 786440 | tf_op jit(solution)/shard_map/ppermute | solution.py:343
  32.5 2.8 %collective-permute-start.9 = (bf16[4,8,16,256]{3,2,1,0:T(8,128)(2,1)S(1)}, bf16[4,8,16,256]{3,2,1,0:T(8,128)(2,1)S(1)}, u32[]{:S(2)}, u32[]{:S(2)}) collective-permute-start(bf16[4,8,16,256]{3,2,1,0:T(8,128)(2,1)S(1)} %collective-permute-done.5.refs_2_), channel_id=1, source_target_pairs={{0,16},{16,0},{32,48},{48,32},{64,80},{80,64},{96,112},{112,96},{1... | collective-permute-start | bytes 786440 | tf_op jit(solution)/shard_map/ppermute | solution.py:343
  33.8 3.1 %collective-permute-start.3 = (bf16[256,2432]{1,0:T(8,128)(2,1)S(1)}, bf16[256,2432]{1,0:T(8,128)(2,1)S(1)}, u32[]{:S(2)}, u32[]{:S(2)}) collective-permute-start(bf16[256,2432]{1,0:T(8,128)(2,1)S(1)} %bitcast.15), channel_id=1, source_target_pairs={{0,16},{16,0},{32,48},{48,32},{64,80},{80,64},{96,112},{112,96},{1... | collective-permute-start | bytes 3735560 | tf_op jit(solution)/shard_map/ppermute | solution.py:337
  35.3 1.6 %copy-start = (bf16[8,256,256]{2,1,0:T(8,128)(2,1)S(1)}, bf16[8,256,256]{2,1,0:T(8,128)(2,1)}, u32[]{:S(2)}) copy-start(bf16[8,256,256]{2,1,0:T(8,128)(2,1)} %right.1) | copy-start | bytes 3145732
  40.2 6.6 %collective-permute-start.11 = (s16[9,16,256]{2,1,0:T(8,128)(2,1)S(1)}, s16[9,16,256]{2,1,0:T(8,128)(2,1)S(1)}, u32[]{:S(2)}, u32[]{:S(2)}) collective-permute-start(s16[9,16,256]{2,1,0:T(8,128)(2,1)S(1)} %get-tuple-element.28), channel_id=1, source_target_pairs={{0,8},{1,9},{2,10},{3,11},{4,12},{5,13},{6,14},{7,15},{8,0},{9,1},... | collective-permute-start | bytes 221192 | tf_op jit(solution)/shard_map/ppermute | solution.py:346
  42.6 5.6 %collective-permute-start.12 = (s16[9,16,256]{2,1,0:T(8,128)(2,1)S(1)}, s16[9,16,256]{2,1,0:T(8,128)(2,1)S(1)}, u32[]{:S(2)}, u32[]{:S(2)}) collective-permute-start(s16[9,16,256]{2,1,0:T(8,128)(2,1)S(1)} %get-tuple-element.29), channel_id=1, source_target_pairs={{0,4},{1,5},{2,6},{3,7},{4,8},{5,9},{6,10},{7,11},{8,12},{9,13},{1... | collective-permute-start | bytes 221192 | tf_op jit(solution)/shard_map/ppermute | solution.py:346
  43.2 5.0 %collective-permute-start.13 = (s16[9,16,256]{2,1,0:T(8,128)(2,1)S(1)}, s16[9,16,256]{2,1,0:T(8,128)(2,1)S(1)}, u32[]{:S(2)}, u32[]{:S(2)}) collective-permute-start(s16[9,16,256]{2,1,0:T(8,128)(2,1)S(1)} %get-tuple-element.30), channel_id=1, source_target_pairs={{0,12},{1,13},{2,14},{3,15},{4,0},{5,1},{6,2},{7,3},{8,4},{9,5},{1... | collective-permute-start | bytes 221192 | tf_op jit(solution)/shard_map/ppermute | solution.py:346

commit v6 on v5

--- a/solution.py
+++ b/solution.py
@@ -28,7 +28,7 @@
 SIZE = ENV + SLOTS
 FETCH = SIZE + SLOTS // 2
 LISTED = 3
-CHUNK = 256
+CHUNK = 128
 LIMIT = 32700.0
 STEP = SLOTS * ROWS
 X_ORDER = (2, 1, 3)
@@ -210,10 +210,13 @@
     )(meta, *own, *planes)
 
 
-def far_kernel(meta, mine, theirs, own, wave, right, s0, s1, s2, s3, sums, hi_ref, lo_ref, channel, codes):
-    core, x, y = meta[0], meta[1], meta[2]
+def far_kernel(table, mine, theirs, own, wave, right, s0, s1, s2, s3, sums, hi_ref, lo_ref, channel, codes, meta, meta_sem):
+    fetch = pltpu.make_async_copy(table, meta, meta_sem)
+    fetch.start()
     codes[...] = jnp.zeros_like(codes)
     spread(mine, theirs, sums, hi_ref, lo_ref)
+    fetch.wait()
+    core, x, y = meta[0], meta[1], meta[2]
     weights = wave[...].reshape(DEPTH, WIDTH)
     for s in range(SLOTS):
         for u in range(2):
@@ -258,7 +261,7 @@
     here = pl.BlockSpec(memory_space=pltpu.VMEM)
     return pl.pallas_call(
         far_kernel,
-        in_specs=[pl.BlockSpec(memory_space=pltpu.SMEM)] + [here] * 5,
+        in_specs=[pl.BlockSpec(memory_space=pl.ANY)] + [here] * 5,
         out_specs=[here] * 4,
         out_shape=[pltpu.VMEM((sectors, ROWS, WIDTH), F32)] + [pltpu.VMEM((sectors + 1, ROWS, WIDTH), jnp.int16)] * 3,
         scratch_shapes=[
@@ -267,6 +270,8 @@
             pltpu.VMEM((2 * STEP, DEPTH), BF),
             pltpu.VMEM((SIDE, STEP, WIDTH), F32),
             pltpu.VMEM((3, ROWS, WIDTH), F32),
+            pltpu.SMEM(meta.shape, jnp.int32),
+            pltpu.SemaphoreType.DMA(()),
         ],
         compiler_params=pltpu.CompilerParams(vmem_limit_bytes=24 * MIB),
         cost_estimate=pl.CostEstimate(flops=FAR_COST, bytes_accessed=MIB, transcendentals=0),

time: 49.3 us -> 48.9 us (level)
  no operation moved by 1% of the time
where the time goes in v6:
time: 48.9 us; the launch traced here: 48.5 us
  starting transfers between devices  23.5 us (48%)
  waiting for transfers between devices  15 us (31%)
  Pallas kernels  9.42 us (19%)
    ppermute x3, waiting for transfers between devices, local(): planes[e] = lax.ppermute(planes[0], 'sector', along_sector(e, 0))  11.2 us
    all_to_all x1, starting transfers between devices, local(): mine = lax.all_to_all(sent, 'table', 0, 0).reshape(TABS * SIDE * SIDE, SENT)  6.66 us
    ppermute x3, starting transfers between devices, local(): lines[d] = lax.ppermute(wave_blocks, 'table', along_table(0, d))  5.74 us
    ppermute x3, starting transfers between devices, local(): lax.ppermute(parts[d], 'table', along_table(d, 0))  5.66 us
    ppermute x3, starting transfers between devices, local(): planes[e] = lax.ppermute(planes[0], 'sector', along_sector(e, 0))  5.37 us
    pallas_call x1, Pallas kernels, far_half(): pl.pallas_call(far_kernel, in_specs=[pl.BlockSpec(memory_space=pl.ANY)] +...  2.85 us
    pallas_call x1, Pallas kernels, pack(): pl.pallas_call(pack_kernel, in_specs=[pl.BlockSpec(memory_space=pltpu.SME...  2.82 us
    ppermute x3, waiting for transfers between devices, local(): lax.ppermute(parts[d], 'table', along_table(d, 0))  2.33 us
  transfers between devices with their start and end apart: 15, of which 7 were waited for; matrix products, arithmetic and copies ran while one was open for 1% of the time, Pallas kernels for 12%

profile of v6, /device:TPU:0, one launch (start us, length us, event | category | flops | bytes accessed | tf_op | source)
XLA Modules:
  0.0 48.5 jit_solution(6148305304470474267)
XLA Ops:
  0.0 1.6 %collective-permute-start = (bf16[8,16,256]{2,1,0:T(8,128)(2,1)}, bf16[8,16,256]{2,1,0:T(8,128)(2,1)S(1)}, u32[]{:S(2)}, u32[]{:S(2)}) collective-permute-start(bf16[8,16,256]{2,1,0:T(8,128)(2,1)} %param.10), channel_id=1, source_target_pairs={{0,1},{1,2},{2,3},{3,0},{4,5},{5,6},{6,7},{7,4},{8,9},{9,10},{10,1... | collective-permute-start | bytes 196616 | tf_op jit(solution)/shard_map/ppermute | solution.py:337
  1.6 2.7 %collective-permute-start.1 = (bf16[8,16,256]{2,1,0:T(8,128)(2,1)}, bf16[8,16,256]{2,1,0:T(8,128)(2,1)S(1)}, u32[]{:S(2)}, u32[]{:S(2)}) collective-permute-start(bf16[8,16,256]{2,1,0:T(8,128)(2,1)} %param.10), channel_id=1, source_target_pairs={{0,2},{1,3},{2,0},{3,1},{4,6},{5,7},{6,4},{7,5},{8,10},{9,11},{10,... | collective-permute-start | bytes 196616 | tf_op jit(solution)/shard_map/ppermute | solution.py:337
  4.3 1.4 %collective-permute-start.2 = (bf16[8,16,256]{2,1,0:T(8,128)(2,1)}, bf16[8,16,256]{2,1,0:T(8,128)(2,1)S(1)}, u32[]{:S(2)}, u32[]{:S(2)}) collective-permute-start(bf16[8,16,256]{2,1,0:T(8,128)(2,1)} %param.10), channel_id=1, source_target_pairs={{0,3},{1,0},{2,1},{3,2},{4,7},{5,4},{6,5},{7,6},{8,11},{9,8},{10,9... | collective-permute-start | bytes 196616 | tf_op jit(solution)/shard_map/ppermute | solution.py:337
  5.7 2.8 %pack.1 = bf16[4,4,16,2432]{3,2,1,0:T(8,128)(2,1)} custom-call(s32[1]{0:T(128)} %bitcast.meta, bf16[16,4,64,256]{3,2,1,0:T(8,128)(2,1)} %bitcast.19, s32[1,192]{1,0:T(1,128)} %bitcast.24, s32[1,192]{1,0:T(1,128)} %bitcast.25, s32[1,192]{1,0:T(1,128)} %bitcast.26, s32[1,192]{1,0:T(1,128)} %bitcast.27), custom_call_target="tpu_custom_call" | custom-call | tf_op jit(solution)/shard_map/pack/pallas_call | solution.py:111
  8.6 0.0 copy-start.1
  8.6 0.0 copy-start.3
  8.6 0.0 copy-start.2
  8.6 0.0 copy-start.4
  8.6 0.0 collective-permute-done
  8.6 0.0 collective-permute-done.1
  8.6 0.1 collective-permute-done.2
  8.8 6.7 %all-to-all-start = ((bf16[16,16,2432]{2,1,0:T(8,128)(2,1)}), bf16[16,16,2432]{2,1,0:T(8,128)(2,1)S(1)}, u32[]{:S(2)}, u32[]{:S(2)}) async-start(bf16[16,16,2432]{2,1,0:T(8,128)(2,1)} %bitcast.18), calls=%async_computation | async-start | bytes 2490368 | tf_op jit(solution)/shard_map/all_to_all | solution.py:341
  15.4 0.0 copy-done.1
  15.5 4.1 %collective-permute-start.6 = (bf16[4,8,16,256]{3,2,1,0:T(8,128)(2,1)S(1)}, bf16[4,8,16,256]{3,2,1,0:T(8,128)(2,1)S(1)}, u32[]{:S(2)}, u32[]{:S(2)}) collective-permute-start(bf16[4,8,16,256]{3,2,1,0:T(8,128)(2,1)S(1)} %pad_maximum_fusion.refs_0_), channel_id=1, source_target_pairs={{0,96},{16,112},{32,0},{48,16},{64,32},{80,48},{96,64},{112,80},{1... | collective-permute-start | bytes 786440 | tf_op jit(solution)/shard_map/ppermute | solution.py:346
  19.6 0.0 collective-permute-start.4
  19.6 1.3 %collective-permute-start.5 = (bf16[4,8,16,256]{3,2,1,0:T(8,128)(2,1)S(1)}, bf16[4,8,16,256]{3,2,1,0:T(8,128)(2,1)S(1)}, u32[]{:S(2)}, u32[]{:S(2)}) collective-permute-start(bf16[4,8,16,256]{3,2,1,0:T(8,128)(2,1)S(1)} %pad_maximum_fusion.refs_0_), channel_id=1, source_target_pairs={{0,32},{16,48},{32,64},{48,80},{64,96},{80,112},{96,0},{112,16},{1... | collective-permute-start | bytes 786440 | tf_op jit(solution)/shard_map/ppermute | solution.py:346
  20.9 0.1 copy.13
  21.0 0.1 reshape.28
  21.0 0.0 copy-done.2
  21.0 0.1 copy.14
  21.1 0.1 reshape.29
  21.2 0.1 concatenate.3.meta.table
  21.3 0.0 collective-permute-start.7
  21.3 7.7 %collective-permute-done.6.refs_3_ = bf16[4,8,16,256]{3,2,1,0:T(8,128)(2,1)S(1)} collective-permute-done((bf16[4,8,16,256]{3,2,1,0:T(8,128)(2,1)S(1)}, bf16[4,8,16,256]{3,2,1,0:T(8,128)(2,1)S(1)}, u32[]{:S(2)}, u32[]{:S(2)}) %collective-permute-start.6) | collective-permute-done | bytes 262176 | tf_op jit(solution)/shard_map/ppermute | solution.py:346
  29.1 0.0 collective-permute-start.10
  29.1 1.0 %collective-permute-done.4.refs_1_ = bf16[4,8,16,256]{3,2,1,0:T(8,128)(2,1)S(1)} collective-permute-done((bf16[4,8,16,256]{3,2,1,0:T(8,128)(2,1)S(1)}, bf16[4,8,16,256]{3,2,1,0:T(8,128)(2,1)S(1)}, u32[]{:S(2)}, u32[]{:S(2)}) %collective-permute-start.4) | collective-permute-done | bytes 262176 | tf_op jit(solution)/shard_map/ppermute | solution.py:346
  30.1 0.0 collective-permute-start.8
  30.1 2.4 %collective-permute-done.5.refs_2_ = bf16[4,8,16,256]{3,2,1,0:T(8,128)(2,1)S(1)} collective-permute-done((bf16[4,8,16,256]{3,2,1,0:T(8,128)(2,1)S(1)}, bf16[4,8,16,256]{3,2,1,0:T(8,128)(2,1)S(1)}, u32[]{:S(2)}, u32[]{:S(2)}) %collective-permute-start.5) | collective-permute-done | bytes 262176 | tf_op jit(solution)/shard_map/ppermute | solution.py:346
  32.5 0.0 collective-permute-start.9
  32.5 1.3 %all-to-all-done = bf16[16,16,2432]{2,1,0:T(8,128)(2,1)S(1)} async-done(((bf16[16,16,2432]{2,1,0:T(8,128)(2,1)}), bf16[16,16,2432]{2,1,0:T(8,128)(2,1)S(1)}, u32[]{:S(2)}, u32[]{:S(2)}) %all-to-all-start) | async-done | bytes 1245216 | tf_op jit(solution)/shard_map/all_to_all | solution.py:341
  33.8 0.0 collective-permute-start.3
  33.8 1.4 %own_half.1 = (bf16[512,1536]{1,0:T(8,128)(2,1)S(1)}, bf16[512,1536]{1,0:T(8,128)(2,1)S(1)}) custom-call(bf16[256,2432]{1,0:T(8,128)(2,1)S(1)} %bitcast.16), custom_call_target="tpu_custom_call" | custom-call | flops 99999997952 | bytes 1048576 | tf_op jit(solution)/shard_map/own_half/pallas_call | solution.py:171
  35.2 0.0 collective-permute-done.7.refs_4_
  35.2 0.0 collective-permute-done.10.refs_7_
  35.2 0.0 collective-permute-done.8.refs_5_
  35.3 0.0 collective-permute-done.9.refs_6_
  35.3 0.0 copy-start
  35.3 1.6 %choose.1 = (f32[512,256]{1,0:T(8,128)S(1)}, bf16[24,64,256]{2,1,0:T(8,128)(2,1)S(1)}) custom-call(s32[52]{0:T(128)S(1)} %concatenate.3.meta.table, bf16[512,1536]{1,0:T(8,128)(2,1)S(1)} %get-tuple-element.19.hi_ref, bf16[512,1536]{1,0:T(8,128)(2,1)S(1)} %get-tuple-element.20.lo_ref, bf16[4,8,16,256]{3,2,1,0:T(8,128)(2,1)S(1)} %pad_maximum_fusion.refs_0_, ...), custom_call_target="tpu_custom_call" | custom-call | flops 1000000000 | bytes 1048576 | tf_op jit(solution)/shard_map/choose/pallas_call | solution.py:202
  36.9 0.0 collective-permute-done.3.theirs
  36.9 0.0 copy-done
  36.9 2.8 %far_half.1 = (f32[8,16,256]{2,1,0:T(8,128)S(1)}, s16[9,16,256]{2,1,0:T(8,128)(2,1)S(1)}, s16[9,16,256]{2,1,0:T(8,128)(2,1)S(1)}, s16[9,16,256]{2,1,0:T(8,128)(2,1)S(1)}) custom-call(s32[52]{0:T(128)S(1)} %concatenate.3.meta.table, bf16[256,2432]{1,0:T(8,128)(2,1)S(1)} %bitcast.17, bf16[256,2432]{1,0:T(8,128)(2,1)S(1)} %collective-permute-done.3.theirs, ...), custom_call_target="tpu_custom_call" | custom-call | flops 4000000000 | bytes 1048576 | tf_op jit(solution)/shard_map/far_half/pallas_call | solution.py:262
  39.8 2.4 %collective-permute-start.11 = (s16[9,16,256]{2,1,0:T(8,128)(2,1)S(1)}, s16[9,16,256]{2,1,0:T(8,128)(2,1)S(1)}, u32[]{:S(2)}, u32[]{:S(2)}) collective-permute-start(s16[9,16,256]{2,1,0:T(8,128)(2,1)S(1)} %get-tuple-element.28), channel_id=1, source_target_pairs={{0,8},{1,9},{2,10},{3,11},{4,12},{5,13},{6,14},{7,15},{8,0},{9,1},... | collective-permute-start | bytes 221192 | tf_op jit(solution)/shard_map/ppermute | solution.py:351
  42.2 0.6 %collective-permute-start.12 = (s16[9,16,256]{2,1,0:T(8,128)(2,1)S(1)}, s16[9,16,256]{2,1,0:T(8,128)(2,1)S(1)}, u32[]{:S(2)}, u32[]{:S(2)}) collective-permute-start(s16[9,16,256]{2,1,0:T(8,128)(2,1)S(1)} %get-tuple-element.29), channel_id=1, source_target_pairs={{0,4},{1,5},{2,6},{3,7},{4,8},{5,9},{6,10},{7,11},{8,12},{9,13},{1... | collective-permute-start | bytes 221192 | tf_op jit(solution)/shard_map/ppermute | solution.py:351
  42.8 2.7 %collective-permute-start.13 = (s16[9,16,256]{2,1,0:T(8,128)(2,1)S(1)}, s16[9,16,256]{2,1,0:T(8,128)(2,1)S(1)}, u32[]{:S(2)}, u32[]{:S(2)}) collective-permute-start(s16[9,16,256]{2,1,0:T(8,128)(2,1)S(1)} %get-tuple-element.30), channel_id=1, source_target_pairs={{0,12},{1,13},{2,14},{3,15},{4,0},{5,1},{6,2},{7,3},{8,4},{9,5},{1... | collective-permute-start | bytes 221192 | tf_op jit(solution)/shard_map/ppermute | solution.py:351
  45.4 1.0 %collective-permute-done.11.refs_0_ = s16[9,16,256]{2,1,0:T(8,128)(2,1)S(1)} collective-permute-done((s16[9,16,256]{2,1,0:T(8,128)(2,1)S(1)}, s16[9,16,256]{2,1,0:T(8,128)(2,1)S(1)}, u32[]{:S(2)}, u32[]{:S(2)}) %collective-permute-start.11) | collective-permute-done | bytes 73760 | tf_op jit(solution)/shard_map/ppermute | solution.py:351
  46.4 1.3 %collective-permute-done.12.refs_1_ = s16[9,16,256]{2,1,0:T(8,128)(2,1)S(1)} collective-permute-done((s16[9,16,256]{2,1,0:T(8,128)(2,1)S(1)}, s16[9,16,256]{2,1,0:T(8,128)(2,1)S(1)}, u32[]{:S(2)}, u32[]{:S(2)}) %collective-permute-start.12) | collective-permute-done | bytes 73760 | tf_op jit(solution)/shard_map/ppermute | solution.py:351
  47.8 0.0 collective-permute-done.13.refs_2_
  47.8 0.7 %finish.1 = f32[8,16,256]{2,1,0:T(8,128)} custom-call(f32[8,16,256]{2,1,0:T(8,128)S(1)} %get-tuple-element.27.own, s16[9,16,256]{2,1,0:T(8,128)(2,1)S(1)} %collective-permute-done.11.refs_0_, s16[9,16,256]{2,1,0:T(8,128)(2,1)S(1)} %collective-permute-done.12.refs_1_, s16[9,16,256]{2,1,0:T(8,128)(2,1)S(1)} %collective-permute-done.13.refs_2_), custom_call_target="tpu_custom_call" | custom-call | tf_op jit(solution)/shard_map/finish/pallas_call | solution.py:294
  (3 shorter events, 0.0 us)
Async XLA Ops:
  0.0 8.6 %collective-permute-start = (bf16[8,16,256]{2,1,0:T(8,128)(2,1)}, bf16[8,16,256]{2,1,0:T(8,128)(2,1)S(1)}, u32[]{:S(2)}, u32[]{:S(2)}) collective-permute-start(bf16[8,16,256]{2,1,0:T(8,128)(2,1)} %param.10), channel_id=1, source_target_pairs={{0,1},{1,2},{2,3},{3,0},{4,5},{5,6},{6,7},{7,4},{8,9},{9,10},{10,1... | collective-permute-start | bytes 196616 | tf_op jit(solution)/shard_map/ppermute | solution.py:337
  1.6 7.1 %collective-permute-start.1 = (bf16[8,16,256]{2,1,0:T(8,128)(2,1)}, bf16[8,16,256]{2,1,0:T(8,128)(2,1)S(1)}, u32[]{:S(2)}, u32[]{:S(2)}) collective-permute-start(bf16[8,16,256]{2,1,0:T(8,128)(2,1)} %param.10), channel_id=1, source_target_pairs={{0,2},{1,3},{2,0},{3,1},{4,6},{5,7},{6,4},{7,5},{8,10},{9,11},{10,... | collective-permute-start | bytes 196616 | tf_op jit(solution)/shard_map/ppermute | solution.py:337
  4.3 4.5 %collective-permute-start.2 = (bf16[8,16,256]{2,1,0:T(8,128)(2,1)}, bf16[8,16,256]{2,1,0:T(8,128)(2,1)S(1)}, u32[]{:S(2)}, u32[]{:S(2)}) collective-permute-start(bf16[8,16,256]{2,1,0:T(8,128)(2,1)} %param.10), channel_id=1, source_target_pairs={{0,3},{1,0},{2,1},{3,2},{4,7},{5,4},{6,5},{7,6},{8,11},{9,8},{10,9... | collective-permute-start | bytes 196616 | tf_op jit(solution)/shard_map/ppermute | solution.py:337
  8.6 6.9 %copy-start.1 = (bf16[8,16,256]{2,1,0:T(8,128)(2,1)S(1)}, bf16[8,16,256]{2,1,0:T(8,128)(2,1)}, u32[]{:S(2)}) copy-start(bf16[8,16,256]{2,1,0:T(8,128)(2,1)} %param.10) | copy-start | bytes 196612
  8.6 12.3 %copy-start.3 = (s32[8,2]{0,1:T(2,128)S(1)}, s32[8,2]{0,1:T(2,128)}, u32[]{:S(2)}) copy-start(s32[8,2]{0,1:T(2,128)} %param.14) | copy-start | bytes 196
  8.6 12.4 %copy-start.2 = (s32[1,8,3]{1,0,2:T(1,128)S(1)}, s32[1,8,3]{1,0,2:T(1,128)}, u32[]{:S(2)}) copy-start(s32[1,8,3]{1,0,2:T(1,128)} %param.15) | copy-start | bytes 292
  8.6 12.6 %copy-start.4 = (s32[8]{0:T(128)S(1)}, s32[8]{0:T(128)}, u32[]{:S(2)}) copy-start(s32[8]{0:T(128)} %param.13) | copy-start | bytes 100
  8.8 25.0 %all-to-all-start = ((bf16[16,16,2432]{2,1,0:T(8,128)(2,1)}), bf16[16,16,2432]{2,1,0:T(8,128)(2,1)S(1)}, u32[]{:S(2)}, u32[]{:S(2)}) async-start(bf16[16,16,2432]{2,1,0:T(8,128)(2,1)} %bitcast.18), calls=%async_computation | async-start | bytes 2490368 | tf_op jit(solution)/shard_map/all_to_all | solution.py:341
  15.5 13.6 %collective-permute-start.6 = (bf16[4,8,16,256]{3,2,1,0:T(8,128)(2,1)S(1)}, bf16[4,8,16,256]{3,2,1,0:T(8,128)(2,1)S(1)}, u32[]{:S(2)}, u32[]{:S(2)}) collective-permute-start(bf16[4,8,16,256]{3,2,1,0:T(8,128)(2,1)S(1)} %pad_maximum_fusion.refs_0_), channel_id=1, source_target_pairs={{0,96},{16,112},{32,0},{48,16},{64,32},{80,48},{96,64},{112,80},{1... | collective-permute-start | bytes 786440 | tf_op jit(solution)/shard_map/ppermute | solution.py:346
  19.6 10.4 %collective-permute-start.4 = (bf16[4,8,16,256]{3,2,1,0:T(8,128)(2,1)S(1)}, bf16[4,8,16,256]{3,2,1,0:T(8,128)(2,1)S(1)}, u32[]{:S(2)}, u32[]{:S(2)}) collective-permute-start(bf16[4,8,16,256]{3,2,1,0:T(8,128)(2,1)S(1)} %pad_maximum_fusion.refs_0_), channel_id=1, source_target_pairs={{0,64},{16,80},{32,96},{48,112},{64,0},{80,16},{96,32},{112,48},{1... | collective-permute-start | bytes 786440 | tf_op jit(solution)/shard_map/ppermute | solution.py:346
  19.6 12.9 %collective-permute-start.5 = (bf16[4,8,16,256]{3,2,1,0:T(8,128)(2,1)S(1)}, bf16[4,8,16,256]{3,2,1,0:T(8,128)(2,1)S(1)}, u32[]{:S(2)}, u32[]{:S(2)}) collective-permute-start(bf16[4,8,16,256]{3,2,1,0:T(8,128)(2,1)S(1)} %pad_maximum_fusion.refs_0_), channel_id=1, source_target_pairs={{0,32},{16,48},{32,64},{48,80},{64,96},{80,112},{96,0},{112,16},{1... | collective-permute-start | bytes 786440 | tf_op jit(solution)/shard_map/ppermute | solution.py:346
  21.3 13.9 %collective-permute-start.7 = (bf16[4,8,16,256]{3,2,1,0:T(8,128)(2,1)S(1)}, bf16[4,8,16,256]{3,2,1,0:T(8,128)(2,1)S(1)}, u32[]{:S(2)}, u32[]{:S(2)}) collective-permute-start(bf16[4,8,16,256]{3,2,1,0:T(8,128)(2,1)S(1)} %pad_maximum_fusion.refs_0_), channel_id=1, source_target_pairs={{0,16},{16,0},{32,48},{48,32},{64,80},{80,64},{96,112},{112,96},{1... | collective-permute-start | bytes 786440 | tf_op jit(solution)/shard_map/ppermute | solution.py:348
  29.1 6.2 %collective-permute-start.10 = (bf16[4,8,16,256]{3,2,1,0:T(8,128)(2,1)S(1)}, bf16[4,8,16,256]{3,2,1,0:T(8,128)(2,1)S(1)}, u32[]{:S(2)}, u32[]{:S(2)}) collective-permute-start(bf16[4,8,16,256]{3,2,1,0:T(8,128)(2,1)S(1)} %collective-permute-done.6.refs_3_), channel_id=1, source_target_pairs={{0,16},{16,0},{32,48},{48,32},{64,80},{80,64},{96,112},{112,96},{1... | collective-permute-start | bytes 786440 | tf_op jit(solution)/shard_map/ppermute | solution.py:348
  30.1 5.2 %collective-permute-start.8 = (bf16[4,8,16,256]{3,2,1,0:T(8,128)(2,1)S(1)}, bf16[4,8,16,256]{3,2,1,0:T(8,128)(2,1)S(1)}, u32[]{:S(2)}, u32[]{:S(2)}) collective-permute-start(bf16[4,8,16,256]{3,2,1,0:T(8,128)(2,1)S(1)} %collective-permute-done.4.refs_1_), channel_id=1, source_target_pairs={{0,16},{16,0},{32,48},{48,32},{64,80},{80,64},{96,112},{112,96},{1... | collective-permute-start | bytes 786440 | tf_op jit(solution)/shard_map/ppermute | solution.py:348
  32.5 2.8 %collective-permute-start.9 = (bf16[4,8,16,256]{3,2,1,0:T(8,128)(2,1)S(1)}, bf16[4,8,16,256]{3,2,1,0:T(8,128)(2,1)S(1)}, u32[]{:S(2)}, u32[]{:S(2)}) collective-permute-start(bf16[4,8,16,256]{3,2,1,0:T(8,128)(2,1)S(1)} %collective-permute-done.5.refs_2_), channel_id=1, source_target_pairs={{0,16},{16,0},{32,48},{48,32},{64,80},{80,64},{96,112},{112,96},{1... | collective-permute-start | bytes 786440 | tf_op jit(solution)/shard_map/ppermute | solution.py:348
  33.8 3.1 %collective-permute-start.3 = (bf16[256,2432]{1,0:T(8,128)(2,1)S(1)}, bf16[256,2432]{1,0:T(8,128)(2,1)S(1)}, u32[]{:S(2)}, u32[]{:S(2)}) collective-permute-start(bf16[256,2432]{1,0:T(8,128)(2,1)S(1)} %bitcast.15), channel_id=1, source_target_pairs={{0,16},{16,0},{32,48},{48,32},{64,80},{80,64},{96,112},{112,96},{1... | collective-permute-start | bytes 3735560 | tf_op jit(solution)/shard_map/ppermute | solution.py:342
  35.3 1.7 %copy-start = (bf16[8,256,256]{2,1,0:T(8,128)(2,1)S(1)}, bf16[8,256,256]{2,1,0:T(8,128)(2,1)}, u32[]{:S(2)}) copy-start(bf16[8,256,256]{2,1,0:T(8,128)(2,1)} %right.1) | copy-start | bytes 3145732
  39.8 6.7 %collective-permute-start.11 = (s16[9,16,256]{2,1,0:T(8,128)(2,1)S(1)}, s16[9,16,256]{2,1,0:T(8,128)(2,1)S(1)}, u32[]{:S(2)}, u32[]{:S(2)}) collective-permute-start(s16[9,16,256]{2,1,0:T(8,128)(2,1)S(1)} %get-tuple-element.28), channel_id=1, source_target_pairs={{0,8},{1,9},{2,10},{3,11},{4,12},{5,13},{6,14},{7,15},{8,0},{9,1},... | collective-permute-start | bytes 221192 | tf_op jit(solution)/shard_map/ppermute | solution.py:351
  42.2 5.6 %collective-permute-start.12 = (s16[9,16,256]{2,1,0:T(8,128)(2,1)S(1)}, s16[9,16,256]{2,1,0:T(8,128)(2,1)S(1)}, u32[]{:S(2)}, u32[]{:S(2)}) collective-permute-start(s16[9,16,256]{2,1,0:T(8,128)(2,1)S(1)} %get-tuple-element.29), channel_id=1, source_target_pairs={{0,4},{1,5},{2,6},{3,7},{4,8},{5,9},{6,10},{7,11},{8,12},{9,13},{1... | collective-permute-start | bytes 221192 | tf_op jit(solution)/shard_map/ppermute | solution.py:351
  42.8 5.0 %collective-permute-start.13 = (s16[9,16,256]{2,1,0:T(8,128)(2,1)S(1)}, s16[9,16,256]{2,1,0:T(8,128)(2,1)S(1)}, u32[]{:S(2)}, u32[]{:S(2)}) collective-permute-start(s16[9,16,256]{2,1,0:T(8,128)(2,1)S(1)} %get-tuple-element.30), channel_id=1, source_target_pairs={{0,12},{1,13},{2,14},{3,15},{4,0},{5,1},{6,2},{7,3},{8,4},{9,5},{1... | collective-permute-start | bytes 221192 | tf_op jit(solution)/shard_map/ppermute | solution.py:351

commit v7 on v6

--- a/solution.py
+++ b/solution.py
@@ -132,7 +132,7 @@
     return out.reshape(SIDE * SIDE, TABS, SENT)
 
 
-def spread(counts_ref, share_ref, sums, hi_ref, lo_ref):
+def weigh(counts_ref, share_ref, sums):
     counts = counts_ref[:, SHARE:SENT]
     for n in range(ROWS // 2):
         part = lax.dot_general(
@@ -141,6 +141,9 @@
         for k in range(2):
             start = (2 * n + k) * PITCH
             sums[start : start + PAIRS, :] = part[:, k * 128 : k * 128 + 128]
+
+
+def relay(sums, hi_ref, lo_ref):
     low = lax.broadcasted_iota(jnp.int32, (ROWS, 128), 1) < 64
 
     for s in range(SLOTS):
@@ -162,8 +165,8 @@
     return part + jnp.dot(lo_ref[rows, :], weights, preferred_element_type=F32)
 
 
-def own_kernel(mine, hi_ref, lo_ref, sums):
-    spread(mine, mine, sums, hi_ref, lo_ref)
+def own_kernel(mine, sums):
+    weigh(mine, mine, sums)
 
 
 def own_half(mine):
@@ -171,17 +174,20 @@
     return pl.pallas_call(
         own_kernel,
         in_specs=[here],
-        out_specs=[here] * 2,
-        out_shape=[pltpu.VMEM((2 * STEP, DEPTH), BF)] * 2,
-        scratch_shapes=[pltpu.VMEM((ROWS * PITCH, 128), F32)],
+        out_specs=here,
+        out_shape=pltpu.VMEM((ROWS * PITCH, 128), F32),
         compiler_params=pltpu.CompilerParams(vmem_limit_bytes=16 * MIB),
         cost_estimate=pl.CostEstimate(flops=OWN_COST, bytes_accessed=MIB, transcendentals=0),
         name="own_half",
     )(mine)
 
 
-def choose_kernel(meta, hi_ref, lo_ref, *refs):
-    planes, (out_ref, wave) = refs[:8], refs[8:]
+def choose_kernel(table, sums, *refs):
+    planes, (out_ref, wave, hi_ref, lo_ref, meta, meta_sem) = refs[:8], refs[8:]
+    fetch = pltpu.make_async_copy(table, meta, meta_sem)
+    fetch.start()
+    relay(sums, hi_ref, lo_ref)
+    fetch.wait()
     core, x, z = meta[0], meta[1], meta[3]
     for c in range(2):
         for place, e in enumerate(PLANES):
@@ -201,20 +207,27 @@
     here = pl.BlockSpec(memory_space=pltpu.VMEM)
     return pl.pallas_call(
         choose_kernel,
-        in_specs=[pl.BlockSpec(memory_space=pltpu.SMEM)] + [here] * 10,
+        in_specs=[pl.BlockSpec(memory_space=pl.ANY)] + [here] * 9,
         out_specs=[here] * 2,
         out_shape=[pltpu.VMEM((2 * STEP, WIDTH), F32), pltpu.VMEM((PICKS, HALF, WIDTH), BF)],
+        scratch_shapes=[
+            pltpu.VMEM((2 * STEP, DEPTH), BF),
+            pltpu.VMEM((2 * STEP, DEPTH), BF),
+            pltpu.SMEM(meta.shape, jnp.int32),
+            pltpu.SemaphoreType.DMA(()),
+        ],
         compiler_params=pltpu.CompilerParams(vmem_limit_bytes=16 * MIB),
         cost_estimate=pl.CostEstimate(flops=CHOOSE_COST, bytes_accessed=MIB, transcendentals=0),
         name="choose",
-    )(meta, *own, *planes)
+    )(meta, own, *planes)
 
 
 def far_kernel(table, mine, theirs, own, wave, right, s0, s1, s2, s3, sums, hi_ref, lo_ref, channel, codes, meta, meta_sem):
     fetch = pltpu.make_async_copy(table, meta, meta_sem)
     fetch.start()
     codes[...] = jnp.zeros_like(codes)
-    spread(mine, theirs, sums, hi_ref, lo_ref)
+    weigh(mine, theirs, sums)
+    relay(sums, hi_ref, lo_ref)
     fetch.wait()
     core, x, y = meta[0], meta[1], meta[2]
     weights = wave[...].reshape(DEPTH, WIDTH)

time: 48.9 us -> 49 us (level)
  transfers between devices with their start and end apart: 15 -> 15, of which waited for: 7 -> 8; matrix products, arithmetic and copies ran while one was open for 1% -> 1% of each run, Pallas kernels for 12% -> 11%
where the time goes in v7:
time: 49 us; the launch traced here: 48.6 us
  starting transfers between devices  23.8 us (49%)
  waiting for transfers between devices  15.3 us (31%)
  Pallas kernels  9.01 us (18%)
    ppermute x3, waiting for transfers between devices, local(): planes[e] = lax.ppermute(planes[0], 'sector', along_sector(e, 0))  11.2 us
    all_to_all x1, starting transfers between devices, local(): mine = lax.all_to_all(sent, 'table', 0, 0).reshape(TABS * SIDE * SIDE, SENT)  6.8 us
    ppermute x3, starting transfers between devices, local(): lax.ppermute(parts[d], 'table', along_table(d, 0))  5.81 us
    ppermute x3, starting transfers between devices, local(): lines[d] = lax.ppermute(wave_blocks, 'table', along_table(0, d))  5.74 us
    ppermute x3, starting transfers between devices, local(): planes[e] = lax.ppermute(planes[0], 'sector', along_sector(e, 0))  5.37 us
    pallas_call x1, Pallas kernels, far_half(): pl.pallas_call(far_kernel, in_specs=[pl.BlockSpec(memory_space=pl.ANY)] +...  2.84 us
    pallas_call x1, Pallas kernels, pack(): pl.pallas_call(pack_kernel, in_specs=[pl.BlockSpec(memory_space=pltpu.SME...  2.82 us
    ppermute x3, waiting for transfers between devices, local(): lax.ppermute(parts[d], 'table', along_table(d, 0))  2.33 us
  transfers between devices with their start and end apart: 15, of which 8 were waited for; matrix products, arithmetic and copies ran while one was open for 1% of the time, Pallas kernels for 11%

profile of v7, /device:TPU:0, one launch (start us, length us, event | category | flops | bytes accessed | tf_op | source)
XLA Modules:
  0.0 48.6 jit_solution(14879605504148699497)
XLA Ops:
  0.0 1.6 %collective-permute-start = (bf16[8,16,256]{2,1,0:T(8,128)(2,1)}, bf16[8,16,256]{2,1,0:T(8,128)(2,1)S(1)}, u32[]{:S(2)}, u32[]{:S(2)}) collective-permute-start(bf16[8,16,256]{2,1,0:T(8,128)(2,1)} %param.10), channel_id=1, source_target_pairs={{0,1},{1,2},{2,3},{3,0},{4,5},{5,6},{6,7},{7,4},{8,9},{9,10},{10,1... | collective-permute-start | bytes 196616 | tf_op jit(solution)/shard_map/ppermute | solution.py:350
  1.6 2.7 %collective-permute-start.1 = (bf16[8,16,256]{2,1,0:T(8,128)(2,1)}, bf16[8,16,256]{2,1,0:T(8,128)(2,1)S(1)}, u32[]{:S(2)}, u32[]{:S(2)}) collective-permute-start(bf16[8,16,256]{2,1,0:T(8,128)(2,1)} %param.10), channel_id=1, source_target_pairs={{0,2},{1,3},{2,0},{3,1},{4,6},{5,7},{6,4},{7,5},{8,10},{9,11},{10,... | collective-permute-start | bytes 196616 | tf_op jit(solution)/shard_map/ppermute | solution.py:350
  4.3 1.4 %collective-permute-start.2 = (bf16[8,16,256]{2,1,0:T(8,128)(2,1)}, bf16[8,16,256]{2,1,0:T(8,128)(2,1)S(1)}, u32[]{:S(2)}, u32[]{:S(2)}) collective-permute-start(bf16[8,16,256]{2,1,0:T(8,128)(2,1)} %param.10), channel_id=1, source_target_pairs={{0,3},{1,0},{2,1},{3,2},{4,7},{5,4},{6,5},{7,6},{8,11},{9,8},{10,9... | collective-permute-start | bytes 196616 | tf_op jit(solution)/shard_map/ppermute | solution.py:350
  5.7 2.8 %pack.1 = bf16[4,4,16,2432]{3,2,1,0:T(8,128)(2,1)} custom-call(s32[1]{0:T(128)} %bitcast.meta, bf16[16,4,64,256]{3,2,1,0:T(8,128)(2,1)} %bitcast.19, s32[1,192]{1,0:T(1,128)} %bitcast.24, s32[1,192]{1,0:T(1,128)} %bitcast.25, s32[1,192]{1,0:T(1,128)} %bitcast.26, s32[1,192]{1,0:T(1,128)} %bitcast.27), custom_call_target="tpu_custom_call" | custom-call | tf_op jit(solution)/shard_map/pack/pallas_call | solution.py:111
  8.6 0.0 collective-permute-done
  8.6 0.0 collective-permute-done.1
  8.6 0.2 collective-permute-done.2
  8.8 0.0 copy-start.1
  8.8 0.0 copy-start.3
  8.8 6.8 %all-to-all-start = ((bf16[16,16,2432]{2,1,0:T(8,128)(2,1)}), bf16[16,16,2432]{2,1,0:T(8,128)(2,1)S(1)}, u32[]{:S(2)}, u32[]{:S(2)}) async-start(bf16[16,16,2432]{2,1,0:T(8,128)(2,1)} %bitcast.18), calls=%async_computation | async-start | bytes 2490368 | tf_op jit(solution)/shard_map/all_to_all | solution.py:354
  15.6 0.0 copy-done.1
  15.7 4.1 %collective-permute-start.6 = (bf16[4,8,16,256]{3,2,1,0:T(8,128)(2,1)S(1)}, bf16[4,8,16,256]{3,2,1,0:T(8,128)(2,1)S(1)}, u32[]{:S(2)}, u32[]{:S(2)}) collective-permute-start(bf16[4,8,16,256]{3,2,1,0:T(8,128)(2,1)S(1)} %pad_maximum_fusion.refs_0_), channel_id=1, source_target_pairs={{0,96},{16,112},{32,0},{48,16},{64,32},{80,48},{96,64},{112,80},{1... | collective-permute-start | bytes 786440 | tf_op jit(solution)/shard_map/ppermute | solution.py:359
  19.8 0.0 collective-permute-start.4
  19.8 1.3 %collective-permute-start.5 = (bf16[4,8,16,256]{3,2,1,0:T(8,128)(2,1)S(1)}, bf16[4,8,16,256]{3,2,1,0:T(8,128)(2,1)S(1)}, u32[]{:S(2)}, u32[]{:S(2)}) collective-permute-start(bf16[4,8,16,256]{3,2,1,0:T(8,128)(2,1)S(1)} %pad_maximum_fusion.refs_0_), channel_id=1, source_target_pairs={{0,32},{16,48},{32,64},{48,80},{64,96},{80,112},{96,0},{112,16},{1... | collective-permute-start | bytes 786440 | tf_op jit(solution)/shard_map/ppermute | solution.py:359
  21.0 0.0 copy-done.3
  21.0 0.1 copy.13
  21.1 0.1 reshape.28
  21.2 0.0 copy-done.2
  21.2 0.1 copy.14
  21.3 0.1 reshape.29
  21.4 0.0 copy-done.4
  21.4 0.1 concatenate.3.table
  21.4 0.0 collective-permute-start.7
  21.5 7.7 %collective-permute-done.6.refs_3_ = bf16[4,8,16,256]{3,2,1,0:T(8,128)(2,1)S(1)} collective-permute-done((bf16[4,8,16,256]{3,2,1,0:T(8,128)(2,1)S(1)}, bf16[4,8,16,256]{3,2,1,0:T(8,128)(2,1)S(1)}, u32[]{:S(2)}, u32[]{:S(2)}) %collective-permute-start.6) | collective-permute-done | bytes 262176 | tf_op jit(solution)/shard_map/ppermute | solution.py:359
  29.2 0.0 collective-permute-start.10
  29.2 1.0 %collective-permute-done.4.refs_1_ = bf16[4,8,16,256]{3,2,1,0:T(8,128)(2,1)S(1)} collective-permute-done((bf16[4,8,16,256]{3,2,1,0:T(8,128)(2,1)S(1)}, bf16[4,8,16,256]{3,2,1,0:T(8,128)(2,1)S(1)}, u32[]{:S(2)}, u32[]{:S(2)}) %collective-permute-start.4) | collective-permute-done | bytes 262176 | tf_op jit(solution)/shard_map/ppermute | solution.py:359
  30.2 0.0 collective-permute-start.8
  30.2 2.4 %collective-permute-done.5.refs_2_ = bf16[4,8,16,256]{3,2,1,0:T(8,128)(2,1)S(1)} collective-permute-done((bf16[4,8,16,256]{3,2,1,0:T(8,128)(2,1)S(1)}, bf16[4,8,16,256]{3,2,1,0:T(8,128)(2,1)S(1)}, u32[]{:S(2)}, u32[]{:S(2)}) %collective-permute-start.5) | collective-permute-done | bytes 262176 | tf_op jit(solution)/shard_map/ppermute | solution.py:359
  32.6 0.0 collective-permute-start.9
  32.6 1.3 %all-to-all-done = bf16[16,16,2432]{2,1,0:T(8,128)(2,1)S(1)} async-done(((bf16[16,16,2432]{2,1,0:T(8,128)(2,1)}), bf16[16,16,2432]{2,1,0:T(8,128)(2,1)S(1)}, u32[]{:S(2)}, u32[]{:S(2)}) %all-to-all-start) | async-done | bytes 1245216 | tf_op jit(solution)/shard_map/all_to_all | solution.py:354
  34.0 0.0 collective-permute-start.3
  34.0 0.6 %own_half.1.sums = f32[6272,128]{1,0:T(8,128)S(1)} custom-call(bf16[256,2432]{1,0:T(8,128)(2,1)S(1)} %bitcast.16), custom_call_target="tpu_custom_call" | custom-call | flops 99999997952 | bytes 1048576 | tf_op jit(solution)/shard_map/own_half/pallas_call | solution.py:174
  34.6 0.0 copy-start
  34.6 0.0 collective-permute-done.7.refs_4_
  34.6 0.0 collective-permute-done.10.refs_7_
  34.6 0.0 collective-permute-done.8.refs_5_
  34.6 0.0 collective-permute-done.9.refs_6_
  34.6 2.0 %choose.1 = (f32[512,256]{1,0:T(8,128)S(1)}, bf16[24,64,256]{2,1,0:T(8,128)(2,1)S(1)}) custom-call(s32[52]{0:T(128)S(1)} %concatenate.3.table, f32[6272,128]{1,0:T(8,128)S(1)} %own_half.1.sums, bf16[4,8,16,256]{3,2,1,0:T(8,128)(2,1)S(1)} %pad_maximum_fusion.refs_0_, bf16[4,8,16,256]{3,2,1,0:T(8,128)(2,1)S(1)} %collective-permute-done.4.refs_1_, ...), custom_call_target="tpu_custom_call" | custom-call | flops 1000000000 | bytes 1048576 | tf_op jit(solution)/shard_map/choose/pallas_call | solution.py:208
  36.6 0.3 collective-permute-done.3.theirs
  36.9 0.0 copy-done
  36.9 2.8 %far_half.1 = (f32[8,16,256]{2,1,0:T(8,128)S(1)}, s16[9,16,256]{2,1,0:T(8,128)(2,1)S(1)}, s16[9,16,256]{2,1,0:T(8,128)(2,1)S(1)}, s16[9,16,256]{2,1,0:T(8,128)(2,1)S(1)}) custom-call(s32[52]{0:T(128)S(1)} %concatenate.3.table, bf16[256,2432]{1,0:T(8,128)(2,1)S(1)} %bitcast.17, bf16[256,2432]{1,0:T(8,128)(2,1)S(1)} %collective-permute-done.3.theirs, ...), custom_call_target="tpu_custom_call" | custom-call | flops 4000000000 | bytes 1048576 | tf_op jit(solution)/shard_map/far_half/pallas_call | solution.py:275
  39.8 2.6 %collective-permute-start.11 = (s16[9,16,256]{2,1,0:T(8,128)(2,1)S(1)}, s16[9,16,256]{2,1,0:T(8,128)(2,1)S(1)}, u32[]{:S(2)}, u32[]{:S(2)}) collective-permute-start(s16[9,16,256]{2,1,0:T(8,128)(2,1)S(1)} %get-tuple-element.24), channel_id=1, source_target_pairs={{0,8},{1,9},{2,10},{3,11},{4,12},{5,13},{6,14},{7,15},{8,0},{9,1},... | collective-permute-start | bytes 221192 | tf_op jit(solution)/shard_map/ppermute | solution.py:364
  42.3 0.6 %collective-permute-start.12 = (s16[9,16,256]{2,1,0:T(8,128)(2,1)S(1)}, s16[9,16,256]{2,1,0:T(8,128)(2,1)S(1)}, u32[]{:S(2)}, u32[]{:S(2)}) collective-permute-start(s16[9,16,256]{2,1,0:T(8,128)(2,1)S(1)} %get-tuple-element.25), channel_id=1, source_target_pairs={{0,4},{1,5},{2,6},{3,7},{4,8},{5,9},{6,10},{7,11},{8,12},{9,13},{1... | collective-permute-start | bytes 221192 | tf_op jit(solution)/shard_map/ppermute | solution.py:364
  42.9 2.7 %collective-permute-start.13 = (s16[9,16,256]{2,1,0:T(8,128)(2,1)S(1)}, s16[9,16,256]{2,1,0:T(8,128)(2,1)S(1)}, u32[]{:S(2)}, u32[]{:S(2)}) collective-permute-start(s16[9,16,256]{2,1,0:T(8,128)(2,1)S(1)} %get-tuple-element.26), channel_id=1, source_target_pairs={{0,12},{1,13},{2,14},{3,15},{4,0},{5,1},{6,2},{7,3},{8,4},{9,5},{1... | collective-permute-start | bytes 221192 | tf_op jit(solution)/shard_map/ppermute | solution.py:364
  45.6 0.7 %collective-permute-done.11.refs_0_ = s16[9,16,256]{2,1,0:T(8,128)(2,1)S(1)} collective-permute-done((s16[9,16,256]{2,1,0:T(8,128)(2,1)S(1)}, s16[9,16,256]{2,1,0:T(8,128)(2,1)S(1)}, u32[]{:S(2)}, u32[]{:S(2)}) %collective-permute-start.11) | collective-permute-done | bytes 73760 | tf_op jit(solution)/shard_map/ppermute | solution.py:364
  46.3 1.6 %collective-permute-done.12.refs_1_ = s16[9,16,256]{2,1,0:T(8,128)(2,1)S(1)} collective-permute-done((s16[9,16,256]{2,1,0:T(8,128)(2,1)S(1)}, s16[9,16,256]{2,1,0:T(8,128)(2,1)S(1)}, u32[]{:S(2)}, u32[]{:S(2)}) %collective-permute-start.12) | collective-permute-done | bytes 73760 | tf_op jit(solution)/shard_map/ppermute | solution.py:364
  47.9 0.0 collective-permute-done.13.refs_2_
  47.9 0.7 %finish.1 = f32[8,16,256]{2,1,0:T(8,128)} custom-call(f32[8,16,256]{2,1,0:T(8,128)S(1)} %get-tuple-element.23.own, s16[9,16,256]{2,1,0:T(8,128)(2,1)S(1)} %collective-permute-done.11.refs_0_, s16[9,16,256]{2,1,0:T(8,128)(2,1)S(1)} %collective-permute-done.12.refs_1_, s16[9,16,256]{2,1,0:T(8,128)(2,1)S(1)} %collective-permute-done.13.refs_2_), custom_call_target="tpu_custom_call" | custom-call | tf_op jit(solution)/shard_map/finish/pallas_call | solution.py:307
  (3 shorter events, 0.0 us)
Async XLA Ops:
  0.0 8.6 %collective-permute-start = (bf16[8,16,256]{2,1,0:T(8,128)(2,1)}, bf16[8,16,256]{2,1,0:T(8,128)(2,1)S(1)}, u32[]{:S(2)}, u32[]{:S(2)}) collective-permute-start(bf16[8,16,256]{2,1,0:T(8,128)(2,1)} %param.10), channel_id=1, source_target_pairs={{0,1},{1,2},{2,3},{3,0},{4,5},{5,6},{6,7},{7,4},{8,9},{9,10},{10,1... | collective-permute-start | bytes 196616 | tf_op jit(solution)/shard_map/ppermute | solution.py:350
  1.6 7.0 %collective-permute-start.1 = (bf16[8,16,256]{2,1,0:T(8,128)(2,1)}, bf16[8,16,256]{2,1,0:T(8,128)(2,1)S(1)}, u32[]{:S(2)}, u32[]{:S(2)}) collective-permute-start(bf16[8,16,256]{2,1,0:T(8,128)(2,1)} %param.10), channel_id=1, source_target_pairs={{0,2},{1,3},{2,0},{3,1},{4,6},{5,7},{6,4},{7,5},{8,10},{9,11},{10,... | collective-permute-start | bytes 196616 | tf_op jit(solution)/shard_map/ppermute | solution.py:350
  4.3 4.5 %collective-permute-start.2 = (bf16[8,16,256]{2,1,0:T(8,128)(2,1)}, bf16[8,16,256]{2,1,0:T(8,128)(2,1)S(1)}, u32[]{:S(2)}, u32[]{:S(2)}) collective-permute-start(bf16[8,16,256]{2,1,0:T(8,128)(2,1)} %param.10), channel_id=1, source_target_pairs={{0,3},{1,0},{2,1},{3,2},{4,7},{5,4},{6,5},{7,6},{8,11},{9,8},{10,9... | collective-permute-start | bytes 196616 | tf_op jit(solution)/shard_map/ppermute | solution.py:350
  8.8 6.8 %copy-start.1 = (bf16[8,16,256]{2,1,0:T(8,128)(2,1)S(1)}, bf16[8,16,256]{2,1,0:T(8,128)(2,1)}, u32[]{:S(2)}) copy-start(bf16[8,16,256]{2,1,0:T(8,128)(2,1)} %param.10) | copy-start | bytes 196612
  8.8 12.2 %copy-start.3 = (s32[8,2]{0,1:T(2,128)S(1)}, s32[8,2]{0,1:T(2,128)}, u32[]{:S(2)}) copy-start(s32[8,2]{0,1:T(2,128)} %param.14) | copy-start | bytes 196
  8.8 12.4 %copy-start.2 = (s32[1,8,3]{1,0,2:T(1,128)S(1)}, s32[1,8,3]{1,0,2:T(1,128)}, u32[]{:S(2)}) copy-start(s32[1,8,3]{1,0,2:T(1,128)} %param.15) | copy-start | bytes 292
  8.8 12.6 %copy-start.4 = (s32[8]{0:T(128)S(1)}, s32[8]{0:T(128)}, u32[]{:S(2)}) copy-start(s32[8]{0:T(128)} %param.13) | copy-start | bytes 100
  8.8 25.2 %all-to-all-start = ((bf16[16,16,2432]{2,1,0:T(8,128)(2,1)}), bf16[16,16,2432]{2,1,0:T(8,128)(2,1)S(1)}, u32[]{:S(2)}, u32[]{:S(2)}) async-start(bf16[16,16,2432]{2,1,0:T(8,128)(2,1)} %bitcast.18), calls=%async_computation | async-start | bytes 2490368 | tf_op jit(solution)/shard_map/all_to_all | solution.py:354
  15.7 13.6 %collective-permute-start.6 = (bf16[4,8,16,256]{3,2,1,0:T(8,128)(2,1)S(1)}, bf16[4,8,16,256]{3,2,1,0:T(8,128)(2,1)S(1)}, u32[]{:S(2)}, u32[]{:S(2)}) collective-permute-start(bf16[4,8,16,256]{3,2,1,0:T(8,128)(2,1)S(1)} %pad_maximum_fusion.refs_0_), channel_id=1, source_target_pairs={{0,96},{16,112},{32,0},{48,16},{64,32},{80,48},{96,64},{112,80},{1... | collective-permute-start | bytes 786440 | tf_op jit(solution)/shard_map/ppermute | solution.py:359
  19.8 10.4 %collective-permute-start.4 = (bf16[4,8,16,256]{3,2,1,0:T(8,128)(2,1)S(1)}, bf16[4,8,16,256]{3,2,1,0:T(8,128)(2,1)S(1)}, u32[]{:S(2)}, u32[]{:S(2)}) collective-permute-start(bf16[4,8,16,256]{3,2,1,0:T(8,128)(2,1)S(1)} %pad_maximum_fusion.refs_0_), channel_id=1, source_target_pairs={{0,64},{16,80},{32,96},{48,112},{64,0},{80,16},{96,32},{112,48},{1... | collective-permute-start | bytes 786440 | tf_op jit(solution)/shard_map/ppermute | solution.py:359
  19.8 12.9 %collective-permute-start.5 = (bf16[4,8,16,256]{3,2,1,0:T(8,128)(2,1)S(1)}, bf16[4,8,16,256]{3,2,1,0:T(8,128)(2,1)S(1)}, u32[]{:S(2)}, u32[]{:S(2)}) collective-permute-start(bf16[4,8,16,256]{3,2,1,0:T(8,128)(2,1)S(1)} %pad_maximum_fusion.refs_0_), channel_id=1, source_target_pairs={{0,32},{16,48},{32,64},{48,80},{64,96},{80,112},{96,0},{112,16},{1... | collective-permute-start | bytes 786440 | tf_op jit(solution)/shard_map/ppermute | solution.py:359
  21.4 13.1 %collective-permute-start.7 = (bf16[4,8,16,256]{3,2,1,0:T(8,128)(2,1)S(1)}, bf16[4,8,16,256]{3,2,1,0:T(8,128)(2,1)S(1)}, u32[]{:S(2)}, u32[]{:S(2)}) collective-permute-start(bf16[4,8,16,256]{3,2,1,0:T(8,128)(2,1)S(1)} %pad_maximum_fusion.refs_0_), channel_id=1, source_target_pairs={{0,16},{16,0},{32,48},{48,32},{64,80},{80,64},{96,112},{112,96},{1... | collective-permute-start | bytes 786440 | tf_op jit(solution)/shard_map/ppermute | solution.py:361
  29.2 5.4 %collective-permute-start.10 = (bf16[4,8,16,256]{3,2,1,0:T(8,128)(2,1)S(1)}, bf16[4,8,16,256]{3,2,1,0:T(8,128)(2,1)S(1)}, u32[]{:S(2)}, u32[]{:S(2)}) collective-permute-start(bf16[4,8,16,256]{3,2,1,0:T(8,128)(2,1)S(1)} %collective-permute-done.6.refs_3_), channel_id=1, source_target_pairs={{0,16},{16,0},{32,48},{48,32},{64,80},{80,64},{96,112},{112,96},{1... | collective-permute-start | bytes 786440 | tf_op jit(solution)/shard_map/ppermute | solution.py:361
  30.2 4.4 %collective-permute-start.8 = (bf16[4,8,16,256]{3,2,1,0:T(8,128)(2,1)S(1)}, bf16[4,8,16,256]{3,2,1,0:T(8,128)(2,1)S(1)}, u32[]{:S(2)}, u32[]{:S(2)}) collective-permute-start(bf16[4,8,16,256]{3,2,1,0:T(8,128)(2,1)S(1)} %collective-permute-done.4.refs_1_), channel_id=1, source_target_pairs={{0,16},{16,0},{32,48},{48,32},{64,80},{80,64},{96,112},{112,96},{1... | collective-permute-start | bytes 786440 | tf_op jit(solution)/shard_map/ppermute | solution.py:361
  32.6 2.0 %collective-permute-start.9 = (bf16[4,8,16,256]{3,2,1,0:T(8,128)(2,1)S(1)}, bf16[4,8,16,256]{3,2,1,0:T(8,128)(2,1)S(1)}, u32[]{:S(2)}, u32[]{:S(2)}) collective-permute-start(bf16[4,8,16,256]{3,2,1,0:T(8,128)(2,1)S(1)} %collective-permute-done.5.refs_2_), channel_id=1, source_target_pairs={{0,16},{16,0},{32,48},{48,32},{64,80},{80,64},{96,112},{112,96},{1... | collective-permute-start | bytes 786440 | tf_op jit(solution)/shard_map/ppermute | solution.py:361
  34.0 2.9 %collective-permute-start.3 = (bf16[256,2432]{1,0:T(8,128)(2,1)S(1)}, bf16[256,2432]{1,0:T(8,128)(2,1)S(1)}, u32[]{:S(2)}, u32[]{:S(2)}) collective-permute-start(bf16[256,2432]{1,0:T(8,128)(2,1)S(1)} %bitcast.15), channel_id=1, source_target_pairs={{0,16},{16,0},{32,48},{48,32},{64,80},{80,64},{96,112},{112,96},{1... | collective-permute-start | bytes 3735560 | tf_op jit(solution)/shard_map/ppermute | solution.py:355
  34.6 2.3 %copy-start = (bf16[8,256,256]{2,1,0:T(8,128)(2,1)S(1)}, bf16[8,256,256]{2,1,0:T(8,128)(2,1)}, u32[]{:S(2)}) copy-start(bf16[8,256,256]{2,1,0:T(8,128)(2,1)} %right.1) | copy-start | bytes 3145732
  39.8 6.5 %collective-permute-start.11 = (s16[9,16,256]{2,1,0:T(8,128)(2,1)S(1)}, s16[9,16,256]{2,1,0:T(8,128)(2,1)S(1)}, u32[]{:S(2)}, u32[]{:S(2)}) collective-permute-start(s16[9,16,256]{2,1,0:T(8,128)(2,1)S(1)} %get-tuple-element.24), channel_id=1, source_target_pairs={{0,8},{1,9},{2,10},{3,11},{4,12},{5,13},{6,14},{7,15},{8,0},{9,1},... | collective-permute-start | bytes 221192 | tf_op jit(solution)/shard_map/ppermute | solution.py:364
  42.3 5.6 %collective-permute-start.12 = (s16[9,16,256]{2,1,0:T(8,128)(2,1)S(1)}, s16[9,16,256]{2,1,0:T(8,128)(2,1)S(1)}, u32[]{:S(2)}, u32[]{:S(2)}) collective-permute-start(s16[9,16,256]{2,1,0:T(8,128)(2,1)S(1)} %get-tuple-element.25), channel_id=1, source_target_pairs={{0,4},{1,5},{2,6},{3,7},{4,8},{5,9},{6,10},{7,11},{8,12},{9,13},{1... | collective-permute-start | bytes 221192 | tf_op jit(solution)/shard_map/ppermute | solution.py:364
  42.9 5.0 %collective-permute-start.13 = (s16[9,16,256]{2,1,0:T(8,128)(2,1)S(1)}, s16[9,16,256]{2,1,0:T(8,128)(2,1)S(1)}, u32[]{:S(2)}, u32[]{:S(2)}) collective-permute-start(s16[9,16,256]{2,1,0:T(8,128)(2,1)S(1)} %get-tuple-element.26), channel_id=1, source_target_pairs={{0,12},{1,13},{2,14},{3,15},{4,0},{5,1},{6,2},{7,3},{8,4},{9,5},{1... | collective-permute-start | bytes 221192 | tf_op jit(solution)/shard_map/ppermute | solution.py:364

commit v8 on v7

--- a/solution.py
+++ b/solution.py
@@ -28,7 +28,7 @@
 SIZE = ENV + SLOTS
 FETCH = SIZE + SLOTS // 2
 LISTED = 3
-CHUNK = 128
+CHUNK = 64
 LIMIT = 32700.0
 STEP = SLOTS * ROWS
 X_ORDER = (2, 1, 3)

time: 49 us -> 51.6 us (1.053)
  Pallas kernels: 9.01 us -> 11.6 us
    pallas_call x1, Pallas kernels: 2.84 us -> 4.14 us  [far_half(): pl.pallas_call(far_kernel, in_specs=[pl.BlockSpec(memory_space=pl.ANY)] +...]
    pallas_call x1, Pallas kernels: 2.03 us -> 3.31 us  [choose(): pl.pallas_call(choose_kernel, in_specs=[pl.BlockSpec(memory_space=pl.ANY)...]
  transfers between devices with their start and end apart: 15 -> 15, of which waited for: 8 -> 7; matrix products, arithmetic and copies ran while one was open for 1% -> 1% of each run, Pallas kernels for 11% -> 13%
where the time goes in v8:
time: 51.6 us; the launch traced here: 51.2 us
  starting transfers between devices  24 us (47%)
  waiting for transfers between devices  15 us (29%)
  Pallas kernels  11.6 us (22%)
    ppermute x3, waiting for transfers between devices, local(): planes[e] = lax.ppermute(planes[0], 'sector', along_sector(e, 0))  11.2 us
    all_to_all x1, starting transfers between devices, local(): mine = lax.all_to_all(sent, 'table', 0, 0).reshape(TABS * SIDE * SIDE, SENT)  6.8 us
    ppermute x3, starting transfers between devices, local(): lax.ppermute(parts[d], 'table', along_table(d, 0))  6.03 us
    ppermute x3, starting transfers between devices, local(): lines[d] = lax.ppermute(wave_blocks, 'table', along_table(0, d))  5.74 us
    ppermute x3, starting transfers between devices, local(): planes[e] = lax.ppermute(planes[0], 'sector', along_sector(e, 0))  5.37 us
    pallas_call x1, Pallas kernels, far_half(): pl.pallas_call(far_kernel, in_specs=[pl.BlockSpec(memory_space=pl.ANY)] +...  4.14 us
    pallas_call x1, Pallas kernels, choose(): pl.pallas_call(choose_kernel, in_specs=[pl.BlockSpec(memory_space=pl.ANY)...  3.31 us
    pallas_call x1, Pallas kernels, pack(): pl.pallas_call(pack_kernel, in_specs=[pl.BlockSpec(memory_space=pltpu.SME...  2.82 us
  transfers between devices with their start and end apart: 15, of which 7 were waited for; matrix products, arithmetic and copies ran while one was open for 1% of the time, Pallas kernels for 13%

profile of v8, /device:TPU:0, one launch (start us, length us, event | category | flops | bytes accessed | tf_op | source)
XLA Modules:
  0.0 51.2 jit_solution(1310389253480032559)
XLA Ops:
  0.0 1.6 %collective-permute-start = (bf16[8,16,256]{2,1,0:T(8,128)(2,1)}, bf16[8,16,256]{2,1,0:T(8,128)(2,1)S(1)}, u32[]{:S(2)}, u32[]{:S(2)}) collective-permute-start(bf16[8,16,256]{2,1,0:T(8,128)(2,1)} %param.10), channel_id=1, source_target_pairs={{0,1},{1,2},{2,3},{3,0},{4,5},{5,6},{6,7},{7,4},{8,9},{9,10},{10,1... | collective-permute-start | bytes 196616 | tf_op jit(solution)/shard_map/ppermute | solution.py:350
  1.6 2.7 %collective-permute-start.1 = (bf16[8,16,256]{2,1,0:T(8,128)(2,1)}, bf16[8,16,256]{2,1,0:T(8,128)(2,1)S(1)}, u32[]{:S(2)}, u32[]{:S(2)}) collective-permute-start(bf16[8,16,256]{2,1,0:T(8,128)(2,1)} %param.10), channel_id=1, source_target_pairs={{0,2},{1,3},{2,0},{3,1},{4,6},{5,7},{6,4},{7,5},{8,10},{9,11},{10,... | collective-permute-start | bytes 196616 | tf_op jit(solution)/shard_map/ppermute | solution.py:350
  4.3 1.4 %collective-permute-start.2 = (bf16[8,16,256]{2,1,0:T(8,128)(2,1)}, bf16[8,16,256]{2,1,0:T(8,128)(2,1)S(1)}, u32[]{:S(2)}, u32[]{:S(2)}) collective-permute-start(bf16[8,16,256]{2,1,0:T(8,128)(2,1)} %param.10), channel_id=1, source_target_pairs={{0,3},{1,0},{2,1},{3,2},{4,7},{5,4},{6,5},{7,6},{8,11},{9,8},{10,9... | collective-permute-start | bytes 196616 | tf_op jit(solution)/shard_map/ppermute | solution.py:350
  5.7 2.8 %pack.1 = bf16[4,4,16,2432]{3,2,1,0:T(8,128)(2,1)} custom-call(s32[1]{0:T(128)} %bitcast.meta, bf16[16,4,64,256]{3,2,1,0:T(8,128)(2,1)} %bitcast.19, s32[1,192]{1,0:T(1,128)} %bitcast.24, s32[1,192]{1,0:T(1,128)} %bitcast.25, s32[1,192]{1,0:T(1,128)} %bitcast.26, s32[1,192]{1,0:T(1,128)} %bitcast.27), custom_call_target="tpu_custom_call" | custom-call | tf_op jit(solution)/shard_map/pack/pallas_call | solution.py:111
  8.6 0.0 collective-permute-done
  8.6 0.0 collective-permute-done.1
  8.6 0.2 collective-permute-done.2
  8.8 0.0 copy-start.1
  8.8 0.0 copy-start.3
  8.8 6.8 %all-to-all-start = ((bf16[16,16,2432]{2,1,0:T(8,128)(2,1)}), bf16[16,16,2432]{2,1,0:T(8,128)(2,1)S(1)}, u32[]{:S(2)}, u32[]{:S(2)}) async-start(bf16[16,16,2432]{2,1,0:T(8,128)(2,1)} %bitcast.18), calls=%async_computation | async-start | bytes 2490368 | tf_op jit(solution)/shard_map/all_to_all | solution.py:354
  15.6 0.0 copy-done.1
  15.7 4.1 %collective-permute-start.6 = (bf16[4,8,16,256]{3,2,1,0:T(8,128)(2,1)S(1)}, bf16[4,8,16,256]{3,2,1,0:T(8,128)(2,1)S(1)}, u32[]{:S(2)}, u32[]{:S(2)}) collective-permute-start(bf16[4,8,16,256]{3,2,1,0:T(8,128)(2,1)S(1)} %pad_maximum_fusion.refs_0_), channel_id=1, source_target_pairs={{0,96},{16,112},{32,0},{48,16},{64,32},{80,48},{96,64},{112,80},{1... | collective-permute-start | bytes 786440 | tf_op jit(solution)/shard_map/ppermute | solution.py:359
  19.8 0.0 collective-permute-start.4
  19.8 1.3 %collective-permute-start.5 = (bf16[4,8,16,256]{3,2,1,0:T(8,128)(2,1)S(1)}, bf16[4,8,16,256]{3,2,1,0:T(8,128)(2,1)S(1)}, u32[]{:S(2)}, u32[]{:S(2)}) collective-permute-start(bf16[4,8,16,256]{3,2,1,0:T(8,128)(2,1)S(1)} %pad_maximum_fusion.refs_0_), channel_id=1, source_target_pairs={{0,32},{16,48},{32,64},{48,80},{64,96},{80,112},{96,0},{112,16},{1... | collective-permute-start | bytes 786440 | tf_op jit(solution)/shard_map/ppermute | solution.py:359
  21.0 0.0 copy-done.3
  21.0 0.1 copy.13
  21.1 0.1 reshape.28
  21.2 0.0 copy-done.2
  21.2 0.1 copy.14
  21.3 0.1 reshape.29
  21.4 0.0 copy-done.4
  21.4 0.1 concatenate.3.table
  21.4 0.0 collective-permute-start.7
  21.5 7.7 %collective-permute-done.6.refs_3_ = bf16[4,8,16,256]{3,2,1,0:T(8,128)(2,1)S(1)} collective-permute-done((bf16[4,8,16,256]{3,2,1,0:T(8,128)(2,1)S(1)}, bf16[4,8,16,256]{3,2,1,0:T(8,128)(2,1)S(1)}, u32[]{:S(2)}, u32[]{:S(2)}) %collective-permute-start.6) | collective-permute-done | bytes 262176 | tf_op jit(solution)/shard_map/ppermute | solution.py:359
  29.2 0.0 collective-permute-start.10
  29.2 1.0 %collective-permute-done.4.refs_1_ = bf16[4,8,16,256]{3,2,1,0:T(8,128)(2,1)S(1)} collective-permute-done((bf16[4,8,16,256]{3,2,1,0:T(8,128)(2,1)S(1)}, bf16[4,8,16,256]{3,2,1,0:T(8,128)(2,1)S(1)}, u32[]{:S(2)}, u32[]{:S(2)}) %collective-permute-start.4) | collective-permute-done | bytes 262176 | tf_op jit(solution)/shard_map/ppermute | solution.py:359
  30.2 0.0 collective-permute-start.8
  30.2 2.4 %collective-permute-done.5.refs_2_ = bf16[4,8,16,256]{3,2,1,0:T(8,128)(2,1)S(1)} collective-permute-done((bf16[4,8,16,256]{3,2,1,0:T(8,128)(2,1)S(1)}, bf16[4,8,16,256]{3,2,1,0:T(8,128)(2,1)S(1)}, u32[]{:S(2)}, u32[]{:S(2)}) %collective-permute-start.5) | collective-permute-done | bytes 262176 | tf_op jit(solution)/shard_map/ppermute | solution.py:359
  32.6 0.0 collective-permute-start.9
  32.6 1.3 %all-to-all-done = bf16[16,16,2432]{2,1,0:T(8,128)(2,1)S(1)} async-done(((bf16[16,16,2432]{2,1,0:T(8,128)(2,1)}), bf16[16,16,2432]{2,1,0:T(8,128)(2,1)S(1)}, u32[]{:S(2)}, u32[]{:S(2)}) %all-to-all-start) | async-done | bytes 1245216 | tf_op jit(solution)/shard_map/all_to_all | solution.py:354
  34.0 0.0 collective-permute-start.3
  34.0 0.6 %own_half.1.sums = f32[6272,128]{1,0:T(8,128)S(1)} custom-call(bf16[256,2432]{1,0:T(8,128)(2,1)S(1)} %bitcast.16), custom_call_target="tpu_custom_call" | custom-call | flops 99999997952 | bytes 1048576 | tf_op jit(solution)/shard_map/own_half/pallas_call | solution.py:174
  34.6 0.0 copy-start
  34.6 0.0 collective-permute-done.7.refs_4_
  34.6 0.0 collective-permute-done.10.refs_7_
  34.6 0.0 collective-permute-done.8.refs_5_
  34.6 0.0 collective-permute-done.9.refs_6_
  34.6 3.3 %choose.1 = (f32[512,256]{1,0:T(8,128)S(1)}, bf16[24,64,256]{2,1,0:T(8,128)(2,1)S(1)}) custom-call(s32[52]{0:T(128)S(1)} %concatenate.3.table, f32[6272,128]{1,0:T(8,128)S(1)} %own_half.1.sums, bf16[4,8,16,256]{3,2,1,0:T(8,128)(2,1)S(1)} %pad_maximum_fusion.refs_0_, bf16[4,8,16,256]{3,2,1,0:T(8,128)(2,1)S(1)} %collective-permute-done.4.refs_1_, ...), custom_call_target="tpu_custom_call" | custom-call | flops 1000000000 | bytes 1048576 | tf_op jit(solution)/shard_map/choose/pallas_call | solution.py:208
  37.9 0.0 collective-permute-done.3.theirs
  37.9 0.0 copy-done
  38.0 4.1 %far_half.1 = (f32[8,16,256]{2,1,0:T(8,128)S(1)}, s16[9,16,256]{2,1,0:T(8,128)(2,1)S(1)}, s16[9,16,256]{2,1,0:T(8,128)(2,1)S(1)}, s16[9,16,256]{2,1,0:T(8,128)(2,1)S(1)}) custom-call(s32[52]{0:T(128)S(1)} %concatenate.3.table, bf16[256,2432]{1,0:T(8,128)(2,1)S(1)} %bitcast.17, bf16[256,2432]{1,0:T(8,128)(2,1)S(1)} %collective-permute-done.3.theirs, ...), custom_call_target="tpu_custom_call" | custom-call | flops 4000000000 | bytes 1048576 | tf_op jit(solution)/shard_map/far_half/pallas_call | solution.py:275
  42.1 2.8 %collective-permute-start.11 = (s16[9,16,256]{2,1,0:T(8,128)(2,1)S(1)}, s16[9,16,256]{2,1,0:T(8,128)(2,1)S(1)}, u32[]{:S(2)}, u32[]{:S(2)}) collective-permute-start(s16[9,16,256]{2,1,0:T(8,128)(2,1)S(1)} %get-tuple-element.24), channel_id=1, source_target_pairs={{0,8},{1,9},{2,10},{3,11},{4,12},{5,13},{6,14},{7,15},{8,0},{9,1},... | collective-permute-start | bytes 221192 | tf_op jit(solution)/shard_map/ppermute | solution.py:364
  44.9 0.6 %collective-permute-start.12 = (s16[9,16,256]{2,1,0:T(8,128)(2,1)S(1)}, s16[9,16,256]{2,1,0:T(8,128)(2,1)S(1)}, u32[]{:S(2)}, u32[]{:S(2)}) collective-permute-start(s16[9,16,256]{2,1,0:T(8,128)(2,1)S(1)} %get-tuple-element.25), channel_id=1, source_target_pairs={{0,4},{1,5},{2,6},{3,7},{4,8},{5,9},{6,10},{7,11},{8,12},{9,13},{1... | collective-permute-start | bytes 221192 | tf_op jit(solution)/shard_map/ppermute | solution.py:364
  45.5 2.7 %collective-permute-start.13 = (s16[9,16,256]{2,1,0:T(8,128)(2,1)S(1)}, s16[9,16,256]{2,1,0:T(8,128)(2,1)S(1)}, u32[]{:S(2)}, u32[]{:S(2)}) collective-permute-start(s16[9,16,256]{2,1,0:T(8,128)(2,1)S(1)} %get-tuple-element.26), channel_id=1, source_target_pairs={{0,12},{1,13},{2,14},{3,15},{4,0},{5,1},{6,2},{7,3},{8,4},{9,5},{1... | collective-permute-start | bytes 221192 | tf_op jit(solution)/shard_map/ppermute | solution.py:364
  48.1 0.6 %collective-permute-done.11.refs_0_ = s16[9,16,256]{2,1,0:T(8,128)(2,1)S(1)} collective-permute-done((s16[9,16,256]{2,1,0:T(8,128)(2,1)S(1)}, s16[9,16,256]{2,1,0:T(8,128)(2,1)S(1)}, u32[]{:S(2)}, u32[]{:S(2)}) %collective-permute-start.11) | collective-permute-done | bytes 73760 | tf_op jit(solution)/shard_map/ppermute | solution.py:364
  48.7 1.7 %collective-permute-done.12.refs_1_ = s16[9,16,256]{2,1,0:T(8,128)(2,1)S(1)} collective-permute-done((s16[9,16,256]{2,1,0:T(8,128)(2,1)S(1)}, s16[9,16,256]{2,1,0:T(8,128)(2,1)S(1)}, u32[]{:S(2)}, u32[]{:S(2)}) %collective-permute-start.12) | collective-permute-done | bytes 73760 | tf_op jit(solution)/shard_map/ppermute | solution.py:364
  50.5 0.0 collective-permute-done.13.refs_2_
  50.5 0.7 %finish.1 = f32[8,16,256]{2,1,0:T(8,128)} custom-call(f32[8,16,256]{2,1,0:T(8,128)S(1)} %get-tuple-element.23.own, s16[9,16,256]{2,1,0:T(8,128)(2,1)S(1)} %collective-permute-done.11.refs_0_, s16[9,16,256]{2,1,0:T(8,128)(2,1)S(1)} %collective-permute-done.12.refs_1_, s16[9,16,256]{2,1,0:T(8,128)(2,1)S(1)} %collective-permute-done.13.refs_2_), custom_call_target="tpu_custom_call" | custom-call | tf_op jit(solution)/shard_map/finish/pallas_call | solution.py:307
  (3 shorter events, 0.0 us)
Async XLA Ops:
  0.0 8.6 %collective-permute-start = (bf16[8,16,256]{2,1,0:T(8,128)(2,1)}, bf16[8,16,256]{2,1,0:T(8,128)(2,1)S(1)}, u32[]{:S(2)}, u32[]{:S(2)}) collective-permute-start(bf16[8,16,256]{2,1,0:T(8,128)(2,1)} %param.10), channel_id=1, source_target_pairs={{0,1},{1,2},{2,3},{3,0},{4,5},{5,6},{6,7},{7,4},{8,9},{9,10},{10,1... | collective-permute-start | bytes 196616 | tf_op jit(solution)/shard_map/ppermute | solution.py:350
  1.6 7.0 %collective-permute-start.1 = (bf16[8,16,256]{2,1,0:T(8,128)(2,1)}, bf16[8,16,256]{2,1,0:T(8,128)(2,1)S(1)}, u32[]{:S(2)}, u32[]{:S(2)}) collective-permute-start(bf16[8,16,256]{2,1,0:T(8,128)(2,1)} %param.10), channel_id=1, source_target_pairs={{0,2},{1,3},{2,0},{3,1},{4,6},{5,7},{6,4},{7,5},{8,10},{9,11},{10,... | collective-permute-start | bytes 196616 | tf_op jit(solution)/shard_map/ppermute | solution.py:350
  4.3 4.5 %collective-permute-start.2 = (bf16[8,16,256]{2,1,0:T(8,128)(2,1)}, bf16[8,16,256]{2,1,0:T(8,128)(2,1)S(1)}, u32[]{:S(2)}, u32[]{:S(2)}) collective-permute-start(bf16[8,16,256]{2,1,0:T(8,128)(2,1)} %param.10), channel_id=1, source_target_pairs={{0,3},{1,0},{2,1},{3,2},{4,7},{5,4},{6,5},{7,6},{8,11},{9,8},{10,9... | collective-permute-start | bytes 196616 | tf_op jit(solution)/shard_map/ppermute | solution.py:350
  8.8 6.8 %copy-start.1 = (bf16[8,16,256]{2,1,0:T(8,128)(2,1)S(1)}, bf16[8,16,256]{2,1,0:T(8,128)(2,1)}, u32[]{:S(2)}) copy-start(bf16[8,16,256]{2,1,0:T(8,128)(2,1)} %param.10) | copy-start | bytes 196612
  8.8 12.2 %copy-start.3 = (s32[8,2]{0,1:T(2,128)S(1)}, s32[8,2]{0,1:T(2,128)}, u32[]{:S(2)}) copy-start(s32[8,2]{0,1:T(2,128)} %param.14) | copy-start | bytes 196
  8.8 12.4 %copy-start.2 = (s32[1,8,3]{1,0,2:T(1,128)S(1)}, s32[1,8,3]{1,0,2:T(1,128)}, u32[]{:S(2)}) copy-start(s32[1,8,3]{1,0,2:T(1,128)} %param.15) | copy-start | bytes 292
  8.8 12.6 %copy-start.4 = (s32[8]{0:T(128)S(1)}, s32[8]{0:T(128)}, u32[]{:S(2)}) copy-start(s32[8]{0:T(128)} %param.13) | copy-start | bytes 100
  8.8 25.2 %all-to-all-start = ((bf16[16,16,2432]{2,1,0:T(8,128)(2,1)}), bf16[16,16,2432]{2,1,0:T(8,128)(2,1)S(1)}, u32[]{:S(2)}, u32[]{:S(2)}) async-start(bf16[16,16,2432]{2,1,0:T(8,128)(2,1)} %bitcast.18), calls=%async_computation | async-start | bytes 2490368 | tf_op jit(solution)/shard_map/all_to_all | solution.py:354
  15.7 13.6 %collective-permute-start.6 = (bf16[4,8,16,256]{3,2,1,0:T(8,128)(2,1)S(1)}, bf16[4,8,16,256]{3,2,1,0:T(8,128)(2,1)S(1)}, u32[]{:S(2)}, u32[]{:S(2)}) collective-permute-start(bf16[4,8,16,256]{3,2,1,0:T(8,128)(2,1)S(1)} %pad_maximum_fusion.refs_0_), channel_id=1, source_target_pairs={{0,96},{16,112},{32,0},{48,16},{64,32},{80,48},{96,64},{112,80},{1... | collective-permute-start | bytes 786440 | tf_op jit(solution)/shard_map/ppermute | solution.py:359
  19.8 10.4 %collective-permute-start.4 = (bf16[4,8,16,256]{3,2,1,0:T(8,128)(2,1)S(1)}, bf16[4,8,16,256]{3,2,1,0:T(8,128)(2,1)S(1)}, u32[]{:S(2)}, u32[]{:S(2)}) collective-permute-start(bf16[4,8,16,256]{3,2,1,0:T(8,128)(2,1)S(1)} %pad_maximum_fusion.refs_0_), channel_id=1, source_target_pairs={{0,64},{16,80},{32,96},{48,112},{64,0},{80,16},{96,32},{112,48},{1... | collective-permute-start | bytes 786440 | tf_op jit(solution)/shard_map/ppermute | solution.py:359
  19.8 12.9 %collective-permute-start.5 = (bf16[4,8,16,256]{3,2,1,0:T(8,128)(2,1)S(1)}, bf16[4,8,16,256]{3,2,1,0:T(8,128)(2,1)S(1)}, u32[]{:S(2)}, u32[]{:S(2)}) collective-permute-start(bf16[4,8,16,256]{3,2,1,0:T(8,128)(2,1)S(1)} %pad_maximum_fusion.refs_0_), channel_id=1, source_target_pairs={{0,32},{16,48},{32,64},{48,80},{64,96},{80,112},{96,0},{112,16},{1... | collective-permute-start | bytes 786440 | tf_op jit(solution)/shard_map/ppermute | solution.py:359
  21.4 13.1 %collective-permute-start.7 = (bf16[4,8,16,256]{3,2,1,0:T(8,128)(2,1)S(1)}, bf16[4,8,16,256]{3,2,1,0:T(8,128)(2,1)S(1)}, u32[]{:S(2)}, u32[]{:S(2)}) collective-permute-start(bf16[4,8,16,256]{3,2,1,0:T(8,128)(2,1)S(1)} %pad_maximum_fusion.refs_0_), channel_id=1, source_target_pairs={{0,16},{16,0},{32,48},{48,32},{64,80},{80,64},{96,112},{112,96},{1... | collective-permute-start | bytes 786440 | tf_op jit(solution)/shard_map/ppermute | solution.py:361
  29.2 5.4 %collective-permute-start.10 = (bf16[4,8,16,256]{3,2,1,0:T(8,128)(2,1)S(1)}, bf16[4,8,16,256]{3,2,1,0:T(8,128)(2,1)S(1)}, u32[]{:S(2)}, u32[]{:S(2)}) collective-permute-start(bf16[4,8,16,256]{3,2,1,0:T(8,128)(2,1)S(1)} %collective-permute-done.6.refs_3_), channel_id=1, source_target_pairs={{0,16},{16,0},{32,48},{48,32},{64,80},{80,64},{96,112},{112,96},{1... | collective-permute-start | bytes 786440 | tf_op jit(solution)/shard_map/ppermute | solution.py:361
  30.2 4.4 %collective-permute-start.8 = (bf16[4,8,16,256]{3,2,1,0:T(8,128)(2,1)S(1)}, bf16[4,8,16,256]{3,2,1,0:T(8,128)(2,1)S(1)}, u32[]{:S(2)}, u32[]{:S(2)}) collective-permute-start(bf16[4,8,16,256]{3,2,1,0:T(8,128)(2,1)S(1)} %collective-permute-done.4.refs_1_), channel_id=1, source_target_pairs={{0,16},{16,0},{32,48},{48,32},{64,80},{80,64},{96,112},{112,96},{1... | collective-permute-start | bytes 786440 | tf_op jit(solution)/shard_map/ppermute | solution.py:361
  32.6 2.0 %collective-permute-start.9 = (bf16[4,8,16,256]{3,2,1,0:T(8,128)(2,1)S(1)}, bf16[4,8,16,256]{3,2,1,0:T(8,128)(2,1)S(1)}, u32[]{:S(2)}, u32[]{:S(2)}) collective-permute-start(bf16[4,8,16,256]{3,2,1,0:T(8,128)(2,1)S(1)} %collective-permute-done.5.refs_2_), channel_id=1, source_target_pairs={{0,16},{16,0},{32,48},{48,32},{64,80},{80,64},{96,112},{112,96},{1... | collective-permute-start | bytes 786440 | tf_op jit(solution)/shard_map/ppermute | solution.py:361
  34.0 4.0 %collective-permute-start.3 = (bf16[256,2432]{1,0:T(8,128)(2,1)S(1)}, bf16[256,2432]{1,0:T(8,128)(2,1)S(1)}, u32[]{:S(2)}, u32[]{:S(2)}) collective-permute-start(bf16[256,2432]{1,0:T(8,128)(2,1)S(1)} %bitcast.15), channel_id=1, source_target_pairs={{0,16},{16,0},{32,48},{48,32},{64,80},{80,64},{96,112},{112,96},{1... | collective-permute-start | bytes 3735560 | tf_op jit(solution)/shard_map/ppermute | solution.py:355
  34.6 3.4 %copy-start = (bf16[8,256,256]{2,1,0:T(8,128)(2,1)S(1)}, bf16[8,256,256]{2,1,0:T(8,128)(2,1)}, u32[]{:S(2)}) copy-start(bf16[8,256,256]{2,1,0:T(8,128)(2,1)} %right.1) | copy-start | bytes 3145732
  42.1 6.6 %collective-permute-start.11 = (s16[9,16,256]{2,1,0:T(8,128)(2,1)S(1)}, s16[9,16,256]{2,1,0:T(8,128)(2,1)S(1)}, u32[]{:S(2)}, u32[]{:S(2)}) collective-permute-start(s16[9,16,256]{2,1,0:T(8,128)(2,1)S(1)} %get-tuple-element.24), channel_id=1, source_target_pairs={{0,8},{1,9},{2,10},{3,11},{4,12},{5,13},{6,14},{7,15},{8,0},{9,1},... | collective-permute-start | bytes 221192 | tf_op jit(solution)/shard_map/ppermute | solution.py:364
  44.9 5.6 %collective-permute-start.12 = (s16[9,16,256]{2,1,0:T(8,128)(2,1)S(1)}, s16[9,16,256]{2,1,0:T(8,128)(2,1)S(1)}, u32[]{:S(2)}, u32[]{:S(2)}) collective-permute-start(s16[9,16,256]{2,1,0:T(8,128)(2,1)S(1)} %get-tuple-element.25), channel_id=1, source_target_pairs={{0,4},{1,5},{2,6},{3,7},{4,8},{5,9},{6,10},{7,11},{8,12},{9,13},{1... | collective-permute-start | bytes 221192 | tf_op jit(solution)/shard_map/ppermute | solution.py:364
  45.5 5.0 %collective-permute-start.13 = (s16[9,16,256]{2,1,0:T(8,128)(2,1)S(1)}, s16[9,16,256]{2,1,0:T(8,128)(2,1)S(1)}, u32[]{:S(2)}, u32[]{:S(2)}) collective-permute-start(s16[9,16,256]{2,1,0:T(8,128)(2,1)S(1)} %get-tuple-element.26), channel_id=1, source_target_pairs={{0,12},{1,13},{2,14},{3,15},{4,0},{5,1},{6,2},{7,3},{8,4},{9,5},{1... | collective-permute-start | bytes 221192 | tf_op jit(solution)/shard_map/ppermute | solution.py:364
